TPU v7x, 128 devices: a whole 4x4x4 slice. The times are simulated.
128 devices in a mesh: row: 8 (over y, z_hi), col: 16 (over z_lo, x, core).
Axes of the slice: x: 4, y: 4, z: 4 (z_hi: 2, z_lo: 2; z = z_hi * 2 + z_lo), core: 2. Of those that a mesh axis runs over, the one named last changes fastest.
Arguments:
- features: bfloat16 [65536, 128], P(('row', 'col')), may hold values from -6 to 6
- cotangent: bfloat16 [65536, 256], P(('row', 'col')), may hold values from -6 to 6
- w_self1: bfloat16 [128, 256], replicated, may hold values from -0.5 to 0.5
- w_neigh1: bfloat16 [128, 256], replicated, may hold values from -0.5 to 0.5
- w_self2: bfloat16 [256, 256], replicated, may hold values from -0.375 to 0.375
- w_neigh2: bfloat16 [256, 256], replicated, may hold values from -0.375 to 0.375
- tile_rows: int32 [8, 16, 448], P('row', 'col'), may hold values from 0 to 63, as said below
- tile_cols: int32 [8, 16, 448], P('row', 'col'), may hold values from 0 to 31, as said below
- tile_values: bfloat16 [8, 16, 448, 128, 128], P('row', 'col'), may hold values from -0.046875 to 0.046875
- tile_live: int32 [8, 16], P('row', 'col'), may hold values from 112 to 448, as said below
Outputs:
- output: bfloat16 [65536, 256], P(('row', 'col'))
- grad_self1: float32 [128, 256], replicated
- grad_neigh1: float32 [128, 256], replicated
- grad_self2: float32 [256, 256], replicated
- grad_neigh2: float32 [256, 256], replicated
Inputs may be any that keep to these rules, and one draw needn't show every extreme that they name: `tile_rows`: on each device the 448 slots name distinct tiles; block rows lie in the device's row group of 16 * 4 blocks. `tile_cols`: block columns lie in the device's column group of 8 * 4 blocks. Slots from tile_live on are not part of the adjacency; some device has all 448 slots live.
All inputs are finite; a program needn't handle non-finite values.
Results may differ from a plain program's by a relative error of at most 0.0049.
Values may be sent and summed in bfloat16 or wider, within the bound.
No kernel may reach another device: no remote copies, remote signals or barrier semaphores. Data moves between devices by JAX's collectives and lax.ppermute only.
A program may use at most 128 MiB of HBM per device.

v0:
```python
import math

import jax
import jax.numpy as jnp
from jax import lax
from jax.sharding import PartitionSpec as P


def fdot(left, right):
    return jnp.dot(
        left,
        right.astype(jnp.float32),
        precision=lax.Precision.HIGHEST,
        preferred_element_type=jnp.float32,
    )


def apply_tiles(source, src_index, dst_index, values, live_count, dst_blocks, transpose):
    block_size = values.shape[-1]
    width = source.shape[-1]
    blocks = source.reshape(-1, block_size, width)
    src_blocks = blocks.shape[0]
    group = math.gcd(values.shape[0], 64)
    turns = (live_count + group - 1) // group
    offsets = jnp.arange(group, dtype=jnp.int32)
    src_ids = jnp.arange(src_blocks, dtype=jnp.int32)
    dst_ids = jnp.arange(dst_blocks, dtype=jnp.int32)
    form = "tji,tjw->tiw" if transpose else "tij,tjw->tiw"

    def one_turn(turn, total):
        start = turn * group
        tile_group = lax.dynamic_slice_in_dim(values, start, group, 0)
        src_group = lax.dynamic_slice_in_dim(src_index, start, group, 0)
        dst_group = lax.dynamic_slice_in_dim(dst_index, start, group, 0)
        pick_table = (src_group[:, None] == src_ids[None, :]).astype(blocks.dtype)
        picked = jnp.einsum(
            "gs,sbw->gbw", pick_table, blocks, preferred_element_type=jnp.float32
        ).astype(blocks.dtype)
        product = jnp.einsum(form, tile_group, picked, preferred_element_type=jnp.float32)
        valid = (start + offsets < live_count).astype(jnp.float32)
        place_table = (dst_group[:, None] == dst_ids[None, :]).astype(jnp.float32) * valid[:, None]
        placed = jnp.einsum(
            "gd,gbw->dbw",
            place_table,
            product,
            precision=lax.Precision.HIGHEST,
            preferred_element_type=jnp.float32,
        )
        return total + placed

    empty = jnp.zeros((dst_blocks, block_size, width), jnp.float32)
    total = lax.fori_loop(0, turns, one_turn, empty)
    return total.reshape(dst_blocks * block_size, width)


def local(
    features,
    cotangent,
    w_self1,
    w_neigh1,
    w_self2,
    w_neigh2,
    tile_rows,
    tile_cols,
    tile_values,
    tile_live,
):
    rows_here = tile_rows[0, 0]
    cols_here = tile_cols[0, 0]
    values = tile_values[0, 0]
    live_count = tile_live[0, 0]
    block_size = values.shape[-1]
    seg_count = features.shape[0] // block_size
    row_blocks = lax.axis_size("col") * seg_count
    col_blocks = lax.axis_size("row") * seg_count
    gathered_x = lax.all_gather(features, "row", axis=0, tiled=True)
    partial_one = apply_tiles(
        gathered_x, cols_here, rows_here, values, live_count, row_blocks, False
    )
    agg1 = lax.psum_scatter(partial_one, "col", scatter_dimension=0, tiled=True)
    z1 = jnp.dot(features, w_self1, preferred_element_type=jnp.float32) + fdot(agg1, w_neigh1)
    h1 = jax.nn.silu(z1).astype(jnp.bfloat16)
    gathered_h = lax.all_gather(h1, "row", axis=0, tiled=True)
    partial_two = apply_tiles(
        gathered_h, cols_here, rows_here, values, live_count, row_blocks, False
    )
    agg2 = lax.psum_scatter(partial_two, "col", scatter_dimension=0, tiled=True)
    output = (
        jnp.dot(h1, w_self2, preferred_element_type=jnp.float32) + fdot(agg2, w_neigh2)
    ).astype(jnp.bfloat16)
    local_self2 = jnp.dot(h1.T, cotangent, preferred_element_type=jnp.float32)
    local_neigh2 = fdot(agg2.T, cotangent)
    gathered_c = lax.all_gather(cotangent, "col", axis=0, tiled=True)
    partial_back = apply_tiles(
        gathered_c, rows_here, cols_here, values, live_count, col_blocks, True
    )
    back = lax.psum_scatter(partial_back, "row", scatter_dimension=0, tiled=True)
    dh1 = jnp.dot(cotangent, w_self2.T, preferred_element_type=jnp.float32) + fdot(back, w_neigh2.T)
    sigma = jax.nn.sigmoid(z1)
    dz1 = (dh1 * (sigma + z1 * sigma * (1.0 - sigma))).astype(jnp.bfloat16)
    local_self1 = jnp.dot(features.T, dz1, preferred_element_type=jnp.float32)
    local_neigh1 = fdot(agg1.T, dz1)
    grad_self1, grad_neigh1, grad_self2, grad_neigh2 = lax.psum(
        (local_self1, local_neigh1, local_self2, local_neigh2), ("row", "col")
    )
    return (output, grad_self1, grad_neigh1, grad_self2, grad_neigh2)


def solution(mesh):
    return jax.shard_map(
        local,
        mesh=mesh,
        in_specs=(
            P(("row", "col"), None),
            P(("row", "col"), None),
            P(),
            P(),
            P(),
            P(),
            P("row", "col", None),
            P("row", "col", None),
            P("row", "col", None, None, None),
            P("row", "col"),
        ),
        out_specs=(P(("row", "col"), None), P(), P(), P(), P()),
        check_vma=False,
    )
```

profile of v0, /device:TPU:0, one launch (start us, length us, event | category | flops | bytes accessed | tf_op | source)
XLA Modules:
  0.0 863.4 jit_solution(17272978004550511467)
XLA Ops:
  8.6 51.7 %all-gather.4.cloned.1.call-done = bf16[4096,128]{1,0:T(8,128)(2,1)} async-done(((bf16[512,128]{1,0:T(8,128)(2,1)}), bf16[4096,128]{1,0:T(8,128)(2,1)}) %all-gather.4.cloned.1.call-update) | async-done | bytes 1048592 | tf_op jit(solution)/shard_map/all_gather | solution.py:76
  62.8 97.2 %while.39 = (s32[]{:T(128)}, f32[64,128,128]{2,0,1:T(8,128)}, s32[]{:T(128)}, s32[448]{0:T(512)S(1)}, s32[]{:T(128)}, /*index=5*/bf16[448,128,128]{2,1,0:T(8,128...) while((s32[]{:T(128)}, f32[64,128,128]{2,0,1:T(8,128)}, ...), condition=%wide.region_1.2_spmd.clone.clone, body=%wide.region_0.1_spmd.clone.clone.sunk | while | flops 1141909760 | bytes 24119480 | solution.py:52
  68.5 10.5 %fusion.131 = f32[64,128,128]{2,0,1:T(8,128)} fusion(f32[64,128,128]{2,0,1:T(8,128)} %get-tuple-element.619, f32[64,128,128]{2,1,0:T(8,128)S(1)} %fusion.130, f32[64]{0:T(128)S(1)} %compare_convert_fusion.6, s32[64]{0:T(128)S(1)} %dynamic_slice.71), kind=kOutput, calls=%fused_computation.9.clone.1 | convolution fusion | flops 806363136 | bytes 12583424 | tf_op jit(solution)/shard_map/while/body/gd,gbw->dbw/dot_general | solution.py:42
  84.7 10.5 %fusion.131 = f32[64,128,128]{2,0,1:T(8,128)} fusion(f32[64,128,128]{2,0,1:T(8,128)} %get-tuple-element.619, f32[64,128,128]{2,1,0:T(8,128)S(1)} %fusion.130, f32[64]{0:T(128)S(1)} %compare_convert_fusion.6, s32[64]{0:T(128)S(1)} %dynamic_slice.71), kind=kOutput, calls=%fused_computation.9.clone.1 | convolution fusion | flops 806363136 | bytes 12583424 | tf_op jit(solution)/shard_map/while/body/gd,gbw->dbw/dot_general | solution.py:42
  100.9 10.5 %fusion.131 = f32[64,128,128]{2,0,1:T(8,128)} fusion(f32[64,128,128]{2,0,1:T(8,128)} %get-tuple-element.619, f32[64,128,128]{2,1,0:T(8,128)S(1)} %fusion.130, f32[64]{0:T(128)S(1)} %compare_convert_fusion.6, s32[64]{0:T(128)S(1)} %dynamic_slice.71), kind=kOutput, calls=%fused_computation.9.clone.1 | convolution fusion | flops 806363136 | bytes 12583424 | tf_op jit(solution)/shard_map/while/body/gd,gbw->dbw/dot_general | solution.py:42
  117.1 10.5 %fusion.131 = f32[64,128,128]{2,0,1:T(8,128)} fusion(f32[64,128,128]{2,0,1:T(8,128)} %get-tuple-element.619, f32[64,128,128]{2,1,0:T(8,128)S(1)} %fusion.130, f32[64]{0:T(128)S(1)} %compare_convert_fusion.6, s32[64]{0:T(128)S(1)} %dynamic_slice.71), kind=kOutput, calls=%fused_computation.9.clone.1 | convolution fusion | flops 806363136 | bytes 12583424 | tf_op jit(solution)/shard_map/while/body/gd,gbw->dbw/dot_general | solution.py:42
  133.3 10.5 %fusion.131 = f32[64,128,128]{2,0,1:T(8,128)} fusion(f32[64,128,128]{2,0,1:T(8,128)} %get-tuple-element.619, f32[64,128,128]{2,1,0:T(8,128)S(1)} %fusion.130, f32[64]{0:T(128)S(1)} %compare_convert_fusion.6, s32[64]{0:T(128)S(1)} %dynamic_slice.71), kind=kOutput, calls=%fused_computation.9.clone.1 | convolution fusion | flops 806363136 | bytes 12583424 | tf_op jit(solution)/shard_map/while/body/gd,gbw->dbw/dot_general | solution.py:42
  149.5 10.5 %fusion.131 = f32[64,128,128]{2,0,1:T(8,128)} fusion(f32[64,128,128]{2,0,1:T(8,128)} %get-tuple-element.619, f32[64,128,128]{2,1,0:T(8,128)S(1)} %fusion.130, f32[64]{0:T(128)S(1)} %compare_convert_fusion.6, s32[64]{0:T(128)S(1)} %dynamic_slice.71), kind=kOutput, calls=%fused_computation.9.clone.1 | convolution fusion | flops 806363136 | bytes 12583424 | tf_op jit(solution)/shard_map/while/body/gd,gbw->dbw/dot_general | solution.py:42
  160.0 6.6 copy.16
  167.5 80.4 %reduce-scatter.4.cloned.1.call-done = f32[512,128]{1,0:T(8,128)} async-done(((f32[8192,128]{1,0:T(8,128)}), f32[512,128]{1,0:T(8,128)}) %reduce-scatter.4.cloned.1.call-update) | async-done | bytes 262160 | tf_op jit(solution)/shard_map/reduce_scatter | solution.py:80
  250.3 35.1 %all-gather.8.cloned.1.call-done = bf16[8192,256]{1,0:T(8,128)(2,1)} async-done(((bf16[512,256]{1,0:T(8,128)(2,1)}), bf16[8192,256]{1,0:T(8,128)(2,1)}) %all-gather.8.cloned.1.call-update) | async-done | bytes 4194320 | tf_op jit(solution)/shard_map/all_gather | solution.py:93
  288.0 134.3 %while.41 = (s32[]{:T(128)}, f32[32,128,256]{2,0,1:T(8,128)}, s32[]{:T(128)}, s32[448]{0:T(512)S(1)}, s32[]{:T(128)}, /*index=5*/bf16[448,128,128]{2,1,0:T(8,128...) while((s32[]{:T(128)}, f32[32,128,256]{2,0,1:T(8,128)}, ...), condition=%wide.region_7.8_spmd.clone.clone, body=%wide.region_6.7_spmd.clone.clone.sunk | while | flops 1611669760 | bytes 39848120 | solution.py:52
  288.5 5.5 fusion.145
  294.0 4.9 fusion.146
  299.7 11.1 %fusion.147 = f32[32,128,256]{2,0,1:T(8,128)} fusion(f32[32,128,256]{2,0,1:T(8,128)} %get-tuple-element.691, f32[64,128,256]{2,1,0:T(8,128)S(1)} %fusion.146, f32[64]{0:T(128)S(1)} %compare_convert_fusion.8, s32[64]{0:T(128)S(1)} %dynamic_slice.77), kind=kOutput, calls=%fused_computation.54.clone.1 | convolution fusion | flops 806359040 | bytes 16777728 | tf_op jit(solution)/shard_map/while/body/gd,gbw->dbw/dot_general | solution.py:42
  310.8 5.5 fusion.145
  316.3 4.9 fusion.146
  322.0 11.1 %fusion.147 = f32[32,128,256]{2,0,1:T(8,128)} fusion(f32[32,128,256]{2,0,1:T(8,128)} %get-tuple-element.691, f32[64,128,256]{2,1,0:T(8,128)S(1)} %fusion.146, f32[64]{0:T(128)S(1)} %compare_convert_fusion.8, s32[64]{0:T(128)S(1)} %dynamic_slice.77), kind=kOutput, calls=%fused_computation.54.clone.1 | convolution fusion | flops 806359040 | bytes 16777728 | tf_op jit(solution)/shard_map/while/body/gd,gbw->dbw/dot_general | solution.py:42
  333.1 5.5 fusion.145
  338.6 4.9 fusion.146
  344.2 11.1 %fusion.147 = f32[32,128,256]{2,0,1:T(8,128)} fusion(f32[32,128,256]{2,0,1:T(8,128)} %get-tuple-element.691, f32[64,128,256]{2,1,0:T(8,128)S(1)} %fusion.146, f32[64]{0:T(128)S(1)} %compare_convert_fusion.8, s32[64]{0:T(128)S(1)} %dynamic_slice.77), kind=kOutput, calls=%fused_computation.54.clone.1 | convolution fusion | flops 806359040 | bytes 16777728 | tf_op jit(solution)/shard_map/while/body/gd,gbw->dbw/dot_general | solution.py:42
  355.4 5.5 fusion.145
  360.9 4.9 fusion.146
  366.5 11.1 %fusion.147 = f32[32,128,256]{2,0,1:T(8,128)} fusion(f32[32,128,256]{2,0,1:T(8,128)} %get-tuple-element.691, f32[64,128,256]{2,1,0:T(8,128)S(1)} %fusion.146, f32[64]{0:T(128)S(1)} %compare_convert_fusion.8, s32[64]{0:T(128)S(1)} %dynamic_slice.77), kind=kOutput, calls=%fused_computation.54.clone.1 | convolution fusion | flops 806359040 | bytes 16777728 | tf_op jit(solution)/shard_map/while/body/gd,gbw->dbw/dot_general | solution.py:42
  377.7 5.5 fusion.145
  383.1 4.9 fusion.146
  388.8 11.1 %fusion.147 = f32[32,128,256]{2,0,1:T(8,128)} fusion(f32[32,128,256]{2,0,1:T(8,128)} %get-tuple-element.691, f32[64,128,256]{2,1,0:T(8,128)S(1)} %fusion.146, f32[64]{0:T(128)S(1)} %compare_convert_fusion.8, s32[64]{0:T(128)S(1)} %dynamic_slice.77), kind=kOutput, calls=%fused_computation.54.clone.1 | convolution fusion | flops 806359040 | bytes 16777728 | tf_op jit(solution)/shard_map/while/body/gd,gbw->dbw/dot_general | solution.py:42
  399.9 5.5 fusion.145
  405.4 4.9 fusion.146
  411.1 11.1 %fusion.147 = f32[32,128,256]{2,0,1:T(8,128)} fusion(f32[32,128,256]{2,0,1:T(8,128)} %get-tuple-element.691, f32[64,128,256]{2,1,0:T(8,128)S(1)} %fusion.146, f32[64]{0:T(128)S(1)} %compare_convert_fusion.8, s32[64]{0:T(128)S(1)} %dynamic_slice.77), kind=kOutput, calls=%fused_computation.54.clone.1 | convolution fusion | flops 806359040 | bytes 16777728 | tf_op jit(solution)/shard_map/while/body/gd,gbw->dbw/dot_general | solution.py:42
  422.3 6.6 copy.18
  429.0 4.3 broadcast_in_dim.40
  433.3 134.1 %while.40 = (s32[]{:T(128)}, f32[64,128,256]{2,0,1:T(8,128)}, s32[]{:T(128)}, s32[448]{0:T(512)S(1)}, s32[]{:T(128)}, /*index=5*/bf16[448,128,128]{2,1,0:T(8,128...) while((s32[]{:T(128)}, f32[64,128,256]{2,0,1:T(8,128)}, ...), condition=%wide.region_4.5_spmd.clone.clone, body=%wide.region_3.4_spmd.clone.clone.sunk | while | flops 2283809024 | bytes 46139576 | solution.py:52
  434.9 4.6 fusion.138
  440.2 15.4 %fusion.139 = f32[64,128,256]{2,0,1:T(8,128)} fusion(f32[64,128,256]{2,0,1:T(8,128)} %get-tuple-element.655, f32[64,128,256]{2,1,0:T(8,128)S(1)} %fusion.138, f32[64]{0:T(128)S(1)} %compare_convert_fusion.7, s32[64]{0:T(128)S(1)} %dynamic_slice.74), kind=kOutput, calls=%fused_computation.31.clone.1 | convolution fusion | flops 1612718080 | bytes 25166336 | tf_op jit(solution)/shard_map/while/body/gd,gbw->dbw/dot_general | solution.py:42
  457.1 4.6 fusion.138
  462.4 15.4 %fusion.139 = f32[64,128,256]{2,0,1:T(8,128)} fusion(f32[64,128,256]{2,0,1:T(8,128)} %get-tuple-element.655, f32[64,128,256]{2,1,0:T(8,128)S(1)} %fusion.138, f32[64]{0:T(128)S(1)} %compare_convert_fusion.7, s32[64]{0:T(128)S(1)} %dynamic_slice.74), kind=kOutput, calls=%fused_computation.31.clone.1 | convolution fusion | flops 1612718080 | bytes 25166336 | tf_op jit(solution)/shard_map/while/body/gd,gbw->dbw/dot_general | solution.py:42
  479.4 4.6 fusion.138
  484.7 15.4 %fusion.139 = f32[64,128,256]{2,0,1:T(8,128)} fusion(f32[64,128,256]{2,0,1:T(8,128)} %get-tuple-element.655, f32[64,128,256]{2,1,0:T(8,128)S(1)} %fusion.138, f32[64]{0:T(128)S(1)} %compare_convert_fusion.7, s32[64]{0:T(128)S(1)} %dynamic_slice.74), kind=kOutput, calls=%fused_computation.31.clone.1 | convolution fusion | flops 1612718080 | bytes 25166336 | tf_op jit(solution)/shard_map/while/body/gd,gbw->dbw/dot_general | solution.py:42
  501.8 4.6 fusion.138
  507.1 15.4 %fusion.139 = f32[64,128,256]{2,0,1:T(8,128)} fusion(f32[64,128,256]{2,0,1:T(8,128)} %get-tuple-element.655, f32[64,128,256]{2,1,0:T(8,128)S(1)} %fusion.138, f32[64]{0:T(128)S(1)} %compare_convert_fusion.7, s32[64]{0:T(128)S(1)} %dynamic_slice.74), kind=kOutput, calls=%fused_computation.31.clone.1 | convolution fusion | flops 1612718080 | bytes 25166336 | tf_op jit(solution)/shard_map/while/body/gd,gbw->dbw/dot_general | solution.py:42
  524.1 4.6 fusion.138
  529.5 15.4 %fusion.139 = f32[64,128,256]{2,0,1:T(8,128)} fusion(f32[64,128,256]{2,0,1:T(8,128)} %get-tuple-element.655, f32[64,128,256]{2,1,0:T(8,128)S(1)} %fusion.138, f32[64]{0:T(128)S(1)} %compare_convert_fusion.7, s32[64]{0:T(128)S(1)} %dynamic_slice.74), kind=kOutput, calls=%fused_computation.31.clone.1 | convolution fusion | flops 1612718080 | bytes 25166336 | tf_op jit(solution)/shard_map/while/body/gd,gbw->dbw/dot_general | solution.py:42
  546.5 4.6 fusion.138
  551.8 15.4 %fusion.139 = f32[64,128,256]{2,0,1:T(8,128)} fusion(f32[64,128,256]{2,0,1:T(8,128)} %get-tuple-element.655, f32[64,128,256]{2,1,0:T(8,128)S(1)} %fusion.138, f32[64]{0:T(128)S(1)} %compare_convert_fusion.7, s32[64]{0:T(128)S(1)} %dynamic_slice.74), kind=kOutput, calls=%fused_computation.31.clone.1 | convolution fusion | flops 1612718080 | bytes 25166336 | tf_op jit(solution)/shard_map/while/body/gd,gbw->dbw/dot_general | solution.py:42
  567.3 11.5 %copy.17 = f32[64,128,256]{2,1,0:T(8,128)} copy(f32[64,128,256]{2,0,1:T(8,128)} %get-tuple-element.255) | data formatting | bytes 16777216 | tf_op jit(solution)/shard_map/while | solution.py:52
  584.6 113.5 %reduce-scatter.6.cloned.1.call-done = f32[512,256]{1,0:T(8,128)} async-done(((f32[8192,256]{1,0:T(8,128)}), f32[512,256]{1,0:T(8,128)}) %reduce-scatter.6.cloned.1.call-update) | async-done | bytes 524304 | tf_op jit(solution)/shard_map/reduce_scatter | solution.py:87
  702.9 146.9 %all-reduce.3.cloned.1.call-done = (f32[128,256]{0,1:T(8,128)}, f32[128,256]{1,0:T(8,128)}, f32[256,256]{1,0:T(8,128)}, f32[256,256]{1,0:T(8,128)}) async-done(((f32[128,256]{0,1:T(8,128)}, f32[128,256]{1,0:T(8,128)}, f32[256,256]{1,0:T(8,128)}, f32[256,256]{1,0:T(8,128)}), (f32[128,256]{0,1:T(8,128)}, f32[128,256]{1,0:T(8,128)}, f32[256,256]{1,0:T(8,128)}, ...) | async-done | bytes 786448 | tf_op jit(solution)/shard_map/psum | solution.py:103
  (128 shorter events, 78.8 us)
Async XLA Ops:
  7.2 573.7 %copy-start = (bf16[256,256]{1,0:T(8,128)(2,1)S(1)}, bf16[256,256]{1,0:T(8,128)(2,1)}, u32[]{:S(2)}) copy-start(bf16[256,256]{1,0:T(8,128)(2,1)} %param.21) | copy-start | bytes 393220
  7.2 55.6 %copy-start.10 = (s32[1,1,448]{2,1,0:T(1,128)S(1)}, s32[1,1,448]{2,1,0:T(1,128)}, u32[]{:S(2)}) copy-start(s32[1,1,448]{2,1,0:T(1,128)} %param.22) | copy-start | bytes 5380
  7.2 55.6 %copy-start.11 = (s32[1,1,448]{2,1,0:T(1,128)S(1)}, s32[1,1,448]{2,1,0:T(1,128)}, u32[]{:S(2)}) copy-start(s32[1,1,448]{2,1,0:T(1,128)} %param.23) | copy-start | bytes 5380
  7.2 53.1 %all-gather.4.cloned.1.call-start = ((), (), s32[]{:S(2)}) async-start(), calls=%async_computation.3 | async-start | bytes 1179648 | tf_op jit(solution)/shard_map/all_gather | solution.py:76
  7.9 240.0 %reduce-scatter.4.cloned.1.call-start = ((), (), s32[]{:S(2)}) async-start(), calls=%async_computation.4 | async-start | bytes 4456448 | tf_op jit(solution)/shard_map/reduce_scatter | solution.py:80
  60.3 2.5 copy-start.2
  166.7 81.2 %copy-start.8 = (bf16[128,256]{1,0:T(8,128)(2,1)S(1)}, bf16[128,256]{1,0:T(8,128)(2,1)}, u32[]{:S(2)}) copy-start(bf16[128,256]{1,0:T(8,128)(2,1)} %param.19) | copy-start | bytes 196612
  166.7 82.6 %copy-start.6 = (bf16[512,128]{1,0:T(8,128)(2,1)S(1)}, bf16[512,128]{1,0:T(8,128)(2,1)}, u32[]{:S(2)}) copy-start(bf16[512,128]{1,0:T(8,128)(2,1)} %param.16) | copy-start | bytes 393220
  166.7 82.6 %copy-start.9 = (bf16[128,256]{1,0:T(8,128)(2,1)S(1)}, bf16[128,256]{1,0:T(8,128)(2,1)}, u32[]{:S(2)}) copy-start(bf16[128,256]{1,0:T(8,128)(2,1)} %param.18) | copy-start | bytes 196612
  166.7 118.8 %all-gather.8.cloned.1.call-start = ((), (), s32[]{:S(2)}) async-start(), calls=%async_computation.7 | async-start | bytes 4456448 | tf_op jit(solution)/shard_map/all_gather | solution.py:93
  167.4 261.5 %all-gather.6.cloned.1.call-start = ((), (), s32[]{:S(2)}) async-start(), calls=%async_computation.5 | async-start | bytes 2359296 | tf_op jit(solution)/shard_map/all_gather | solution.py:83
  250.3 330.6 %reduce-scatter.8.cloned.1.call-start = ((), (), s32[]{:S(2)}) async-start(), calls=%async_computation.8 | async-start | bytes 4718592 | tf_op jit(solution)/shard_map/reduce_scatter | solution.py:97
  428.9 269.2 %reduce-scatter.6.cloned.1.call-start = ((), (), s32[]{:S(2)}) async-start(), calls=%async_computation.6 | async-start | bytes 8912896 | tf_op jit(solution)/shard_map/reduce_scatter | solution.py:87
  429.0 4.3 copy-start.1
  578.9 0.9 copy-start.3
  578.9 1.0 copy-start.4
  578.9 3.5 copy-start.7
  578.9 4.7 copy-start.5
  578.9 270.9 %all-reduce.3.cloned.1.call-start = ((), (), s32[]{:S(2)}) async-start(), calls=%async_computation.9 | async-start | bytes 1572864 | tf_op jit(solution)/shard_map/psum | solution.py:103
Sparse Core Ops, SparseCore 0:
  10.4 49.8 all-gather.3
  166.8 81.0 reduce-scatter.3
  249.6 35.7 all-gather.7
  288.2 55.0 all-gather.5
  429.0 107.2 reduce-scatter.7
  579.0 119.0 reduce-scatter.5
  703.8 145.9 all-reduce.2
where the time goes:
time: 873 us; the launch traced here: 863 us
  waiting for transfers between devices  429 us (49%)
  matrix products  362 us (41%)
  local copies, waits for them, and re-layouts  44.3 us (5%)
  between operations  15.2 us (2%)
  other arithmetic  11.7 us (1%)
    dot_general x18, matrix products, one_turn(): jnp.einsum('gd,gbw->dbw', place_table, product, precision=lax.Precision.H...  222 us
    psum x1, waiting for transfers between devices, local(): lax.psum((local_self1, local_neigh1, local_self2, local_neigh2), ('row',...  147 us
    reduce_scatter x1, waiting for transfers between devices, local(): agg2 = lax.psum_scatter(partial_two, 'col', scatter_dimension=0, tiled=True)  113 us
    dot_general x18, matrix products, one_turn(): jnp.einsum(form, tile_group, picked, preferred_element_type=jnp.float32)  80.7 us
    reduce_scatter x1, waiting for transfers between devices, local(): agg1 = lax.psum_scatter(partial_one, 'col', scatter_dimension=0, tiled=True)  80.4 us
    all_gather x1, waiting for transfers between devices, local(): gathered_x = lax.all_gather(features, 'row', axis=0, tiled=True)  51.7 us
    dot_general x18, matrix products, one_turn(): jnp.einsum('gs,sbw->gbw', pick_table, blocks, preferred_element_type=jnp....  47.5 us
    all_gather x1, waiting for transfers between devices, local(): gathered_c = lax.all_gather(cotangent, 'col', axis=0, tiled=True)  35.1 us
  transfers between devices with their start and end apart: 7, of which 5 were waited for; matrix products, arithmetic and copies ran while one was open for 35% of the time, Pallas kernels for 0%

commit v1 on v0

v1 whole, which is shorter than its diff:
```python
import functools

import jax
import jax.numpy as jnp
from jax import lax
from jax.experimental import pallas as pl
from jax.experimental.pallas import tpu as pltpu
from jax.sharding import PartitionSpec as P

BF = jnp.bfloat16
F32 = jnp.float32
UNROLL = 16
GROUP = 64
ROW_ORDER = ((0, 0), (0, 1), (3, 0), (1, 0), (3, 1), (1, 1), (2, 0), (2, 1))
COL_ORDER = tuple((dx, dz) for dx in range(4) for dz in range(2))


def row_perm(dy, dz):
    return [(y * 2 + h, ((y + dy) % 4) * 2 + (h ^ dz)) for y in range(4) for h in range(2)]


def col_perm(dx, dz, dc):
    return [
        ((z * 4 + x) * 2 + c, ((z ^ dz) * 4 + (x + dx) % 4) * 2 + (c ^ dc))
        for z in range(2)
        for x in range(4)
        for c in range(2)
    ]


def send_row(value, dy, dz):
    return lax.ppermute(value, "row", row_perm(dy, dz))


def send_col(value, dx, dz, dc=0):
    return lax.ppermute(value, "col", col_perm(dx, dz, dc))


def gather_row(value):
    half = value.shape[0] // 2
    flip = send_row(value, 0, 1)
    below = send_row(value, 1, 0)
    above = send_row(value, 3, 0)
    flip_below = send_row(flip, 1, 0)
    flip_above = send_row(flip, 3, 0)
    far_a = send_row(below[:half], 1, 0)
    far_b = send_row(above[half:], 3, 0)
    flip_far_a = send_row(flip_below[:half], 1, 0)
    flip_far_b = send_row(flip_above[half:], 3, 0)
    return [value, flip, below, above, flip_below, flip_above, far_a, far_b, flip_far_a, flip_far_b]


def tile_kernel(groups, transpose, n_pieces, splits, *refs):
    src, dst, turns = refs[:3]
    pieces = refs[3 : 3 + n_pieces]
    values = refs[3 + n_pieces]
    outs = refs[4 + n_pieces : 4 + n_pieces + len(splits)]
    held, total, sems = refs[4 + n_pieces + len(splits) :]
    g = pl.program_id(0)

    @pl.when(g == 0)
    def _():
        copies = []
        at = 0
        for k, piece in enumerate(pieces):
            rows = piece.shape[0]
            copy = pltpu.make_async_copy(piece, held.at[pl.ds(at, rows)], sems.at[k])
            copy.start()
            copies.append(copy)
            at += rows
        total[...] = jnp.zeros_like(total)
        for copy in copies:
            copy.wait()

    per_group = GROUP // UNROLL
    steps = jnp.clip(turns[0] - g * per_group, 0, per_group)

    def body(i, carry):
        for u in range(UNROLL):
            t = i * UNROLL + u
            s = src[g * GROUP + t]
            d = dst[g * GROUP + t]
            dims = (((0,), (0,)), ((), ())) if transpose else (((1,), (0,)), ((), ()))
            total[d] += lax.dot_general(values[t], held[s], dims, preferred_element_type=F32)
        return carry

    lax.fori_loop(0, steps, body, 0)

    @pl.when(g == groups - 1)
    def _():
        at = 0
        for out, (count, _) in zip(outs, splits):
            out[...] = total[at : at + count].astype(out.dtype)
            at += count


def tile_product(src, dst, turns, pieces, values, splits, transpose, name):
    slots, block, _ = values.shape
    width = pieces[0].shape[-1]
    pieces = [piece.reshape(-1, block, width) for piece in pieces]
    n_src = sum(piece.shape[0] for piece in pieces)
    n_dst = sum(count for count, _ in splits)
    groups = slots // GROUP
    per_group = GROUP // UNROLL

    def value_map(g, src, dst, turns):
        last = jnp.maximum((turns[0] + per_group - 1) // per_group - 1, 0)
        return (jnp.minimum(g, last), 0, 0)

    whole = lambda g, src, dst, turns: (0, 0, 0)
    return pl.pallas_call(
        functools.partial(tile_kernel, groups, transpose, len(pieces), splits),
        grid_spec=pltpu.PrefetchScalarGridSpec(
            num_scalar_prefetch=3,
            grid=(groups,),
            in_specs=[pl.BlockSpec(memory_space=pl.ANY)] * len(pieces)
            + [pl.BlockSpec((GROUP, block, block), value_map)],
            out_specs=[pl.BlockSpec((count, block, width), whole) for count, _ in splits],
            scratch_shapes=[
                pltpu.VMEM((n_src, block, width), BF),
                pltpu.VMEM((n_dst + 1, block, width), F32),
                pltpu.SemaphoreType.DMA((len(pieces),)),
            ],
        ),
        out_shape=[jax.ShapeDtypeStruct((count, block, width), kind) for count, kind in splits],
        compiler_params=pltpu.CompilerParams(vmem_limit_bytes=56 << 20),
        cost_estimate=pl.CostEstimate(flops=18_000_000_000, bytes_accessed=20 << 20, transcendentals=0),
        name=name,
    )(src, dst, turns, *pieces, values)


def scatter_col(own, other):
    width = own.shape[-1]
    got = send_col(other, 0, 0, 1)
    sums = {}
    for k in (4, 5, 2, 3, 6, 7, 1, 0):
        part = own[4 * k : 4 * k + 4] + got[4 * k : 4 * k + 4].astype(F32)
        sums[k] = part if k == 0 else send_col(part.astype(BF), *COL_ORDER[k])
    total = sums[0]
    for k in range(1, 8):
        total = total + sums[k].astype(F32)
    return total.reshape(-1, width)


def scatter_row(parts):
    width = parts[0].shape[-1]
    total = parts[0]
    got = {k: send_row(parts[k], *ROW_ORDER[k]) for k in (6, 7, 4, 5, 2, 3, 1)}
    for k in range(1, 8):
        total = total + got[k].astype(F32)
    return total.reshape(-1, width)


def sum_all(value, y, x, core):
    rows, width = value.shape

    def pick(parts, i):
        return lax.dynamic_index_in_dim(parts, i, 0, False)

    def scatter(part, send, i):
        parts = part.reshape(4, -1, width)
        total = pick(parts, i)
        for d in (1, 2, 3):
            total = total + send(pick(parts, (i + d) % 4), d, 0)
        return total

    def gather(part, send, i):
        parts = jnp.stack([part] + [send(part, d, 0) for d in (1, 2, 3)])
        out = jnp.concatenate([pick(parts, (i - j) % 4) for j in range(4)])
        return out

    halves = value.reshape(2, rows // 2, width)
    part = pick(halves, core) + send_col(pick(halves, 1 - core), 0, 0, 1)
    part = scatter(part, send_col, x)
    part = scatter(part, send_row, y)
    part = part + send_row(part, 0, 1)
    part = part + send_col(part, 0, 1)
    part = gather(part, send_row, y)
    part = gather(part, send_col, x)
    other = send_col(part, 0, 0, 1)
    first = jnp.where(core == 0, part, other)
    second = jnp.where(core == 0, other, part)
    return jnp.concatenate([first, second])


def fdot(left, right):
    return jnp.dot(left, right.astype(F32), precision=lax.Precision.HIGHEST, preferred_element_type=F32)


def local(
    features,
    cotangent,
    w_self1,
    w_neigh1,
    w_self2,
    w_neigh2,
    tile_rows,
    tile_cols,
    tile_values,
    tile_live,
):
    values = tile_values[0, 0]
    slots = values.shape[0]
    live = tile_live[0, 0]
    rows_here = tile_rows[0, 0]
    cols_here = tile_cols[0, 0]
    row_at = lax.axis_index("row")
    col_at = lax.axis_index("col")
    y, z_hi = row_at // 2, row_at % 2
    z_lo, x, core = col_at // 8, (col_at // 2) % 4, col_at % 2

    owner = cols_here // 4
    dy = (owner // 2 - y) % 4
    dz = (owner % 2) ^ z_hi
    place = jnp.where(dy == 0, dz, jnp.where(dy == 3, 2 + 2 * dz, jnp.where(dy == 1, 3 + 2 * dz, 6 + dz)))
    col_place = place * 4 + cols_here % 4
    owner = rows_here // 4
    dx = ((owner // 2) % 4 - x) % 4
    dz = (owner // 8) ^ z_lo
    row_place = ((owner % 2) ^ core) * 32 + (dx * 2 + dz) * 4 + rows_here % 4
    alive = jnp.arange(slots, dtype=jnp.int32) < live
    row_target = jnp.where(alive, row_place, 64)
    col_target = jnp.where(alive, col_place, 32)
    turns = ((live + UNROLL - 1) // UNROLL).reshape(1)

    forward_splits = ((32, F32), (32, BF))
    back_splits = ((4, F32),) + ((4, BF),) * 7

    gathered_c = lax.all_gather(cotangent, "col", axis=0, tiled=True)
    gathered_x = gather_row(features)
    own, other = tile_product(
        col_place, row_target, turns, gathered_x, values, forward_splits, False, "neighbour_sum_one"
    )
    back_parts = tile_product(
        rows_here, col_target, turns, [gathered_c], values, back_splits, True, "neighbour_sum_back"
    )
    agg1 = scatter_col(own, other)
    z1 = jnp.dot(features, w_self1, preferred_element_type=F32) + fdot(agg1, w_neigh1)
    h1 = jax.nn.silu(z1).astype(BF)
    gathered_h = gather_row(h1)
    own, other = tile_product(
        col_place, row_target, turns, gathered_h, values, forward_splits, False, "neighbour_sum_two"
    )
    back = scatter_row(back_parts)
    dh1 = jnp.dot(cotangent, w_self2.T, preferred_element_type=F32) + fdot(back, w_neigh2.T)
    sigma = jax.nn.sigmoid(z1)
    dz1 = (dh1 * (sigma + z1 * sigma * (1.0 - sigma))).astype(BF)
    local_self2 = jnp.dot(h1.T, cotangent, preferred_element_type=F32)
    local_neigh2 = jnp.dot(
        h1.T.astype(F32), back, precision=lax.Precision.HIGHEST, preferred_element_type=F32
    )
    local_self1 = jnp.dot(features.T, dz1, preferred_element_type=F32)
    local_neigh1 = fdot(agg1.T, dz1)
    grads = sum_all(jnp.concatenate([local_self1, local_neigh1, local_self2, local_neigh2]), y, x, core)
    agg2 = scatter_col(own, other)
    output = (jnp.dot(h1, w_self2, preferred_element_type=F32) + fdot(agg2, w_neigh2)).astype(BF)
    return (output, grads[:128], grads[128:256], grads[256:512], grads[512:])


def solution(mesh):
    return jax.shard_map(
        local,
        mesh=mesh,
        in_specs=(
            P(("row", "col"), None),
            P(("row", "col"), None),
            P(),
            P(),
            P(),
            P(),
            P("row", "col", None),
            P("row", "col", None),
            P("row", "col", None, None, None),
            P("row", "col"),
        ),
        out_specs=(P(("row", "col"), None), P(), P(), P(), P()),
        check_vma=False,
    )
```

time: 873 us -> 232 us (0.27); the launches traced: 863 us -> 232 us
  waiting for transfers between devices: 429 us -> 50.7 us
  matrix products: 362 us -> 4.82 us
  starting transfers between devices: 0.28 us -> 97.7 us
  Pallas kernels: 0 us -> 45.4 us
  local copies, waits for them, and re-layouts: 44.3 us -> 4.03 us
    dot_general x64 -> x10, matrix products: 362 us -> 4.82 us  [the longest x4 3.18 us: fdot(): jnp.dot(left, right.astype(F32), precision=lax.Precision.HIGHEST, preferr...]
    reduce_scatter x3 -> x0, waiting for transfers between devices: 194 us -> none  [the longest x1 113 us: local(): agg2 = lax.psum_scatter(partial_two, 'col', scatter_dimension=0, tiled=True)]
    psum x1 -> x0, waiting for transfers between devices: 147 us -> none  [local(): lax.psum((local_self1, local_neigh1, local_self2, local_neigh2), ('row',...]
    ppermute x0 -> x57, starting transfers between devices: none -> 97.7 us  [the longest x32 60.4 us: send_row(): return lax.ppermute(value, 'row', row_perm(dy, dz))]
    all_gather x2 -> x0, waiting for transfers between devices: 51.7 us -> none  [the longest x1 51.7 us: local(): gathered_x = lax.all_gather(features, 'row', axis=0, tiled=True)]
    ppermute x0 -> x57, waiting for transfers between devices: none -> 50 us  [the longest x25 34 us: send_col(): return lax.ppermute(value, 'col', col_perm(dx, dz, dc))]
    pallas_call x0 -> x3, Pallas kernels: none -> 45.4 us  [tile_product(): pl.pallas_call(functools.partial(tile_kernel, groups, transpose, len(piec...]
    all_gather x1, waiting for transfers between devices: 35.1 us -> 0.01 us  [local(): gathered_c = lax.all_gather(cotangent, 'col', axis=0, tiled=True)]
  transfers between devices with their start and end apart: 7 -> 58, of which waited for: 5 -> 20; matrix products, arithmetic and copies ran while one was open for 35% -> 8% of each run, Pallas kernels for 0% -> 20%
where the time goes in v1:
time: 232 us
  starting transfers between devices  97.7 us (42%)
  waiting for transfers between devices  50.7 us (22%)
  Pallas kernels  45.4 us (20%)
  between operations  15.6 us (7%)
  other arithmetic  13.6 us (6%)
  matrix products  4.82 us (2%)
  local copies, waits for them, and re-layouts  4.03 us (2%)
    ppermute x32, starting transfers between devices, send_row(): return lax.ppermute(value, 'row', row_perm(dy, dz))  60.4 us
    pallas_call x3, Pallas kernels, tile_product(): pl.pallas_call(functools.partial(tile_kernel, groups, transpose, len(piec...  45.4 us
    ppermute x25, starting transfers between devices, send_col(): return lax.ppermute(value, 'col', col_perm(dx, dz, dc))  37.3 us
    ppermute x25, waiting for transfers between devices, send_col(): return lax.ppermute(value, 'col', col_perm(dx, dz, dc))  34 us
    ppermute x32, waiting for transfers between devices, send_row(): return lax.ppermute(value, 'row', row_perm(dy, dz))  16 us
  transfers between devices with their start and end apart: 58, of which 20 were waited for; matrix products, arithmetic and copies ran while one was open for 8% of the time, Pallas kernels for 20%

profile of v1, /device:TPU:0, one launch (start us, length us, event | category | flops | bytes accessed | tf_op | source)
XLA Modules:
  0.0 231.8 jit_solution(6035869177176606798)
XLA Ops:
  7.9 4.0 %collective-permute-start = (bf16[512,128]{1,0:T(8,128)(2,1)}, bf16[512,128]{1,0:T(8,128)(2,1)S(1)}, u32[]{:S(2)}, u32[]{:S(2)}) collective-permute-start(bf16[512,128]{1,0:T(8,128)(2,1)} %param.10), channel_id=1, source_target_pairs={{0,16},{16,0},{32,48},{48,32},{64,80},{80,64},{96,112},{112,96},{1... | collective-permute-start | bytes 393224 | tf_op jit(solution)/shard_map/ppermute | solution.py:32
  12.0 1.6 collective-permute-start.1
  13.5 1.7 collective-permute-start.2
  17.2 1.9 collective-permute-start.4
  20.7 3.2 %collective-permute-start.6 = (bf16[256,128]{1,0:T(8,128)(2,1)S(1)}, bf16[256,128]{1,0:T(8,128)(2,1)S(1)}, u32[]{:S(2)}, u32[]{:S(2)}) collective-permute-start(bf16[256,128]{1,0:T(8,128)(2,1)S(1)} %slice.177), channel_id=1, source_target_pairs={{0,96},{16,112},{32,0},{48,16},{64,32},{80,48},{96,64},{112,80},{1... | collective-permute-start | bytes 196616 | tf_op jit(solution)/shard_map/ppermute | solution.py:32
  24.0 3.3 %collective-permute-start.8 = (bf16[256,128]{1,0:T(8,128)(2,1)S(1)}, bf16[256,128]{1,0:T(8,128)(2,1)S(1)}, u32[]{:S(2)}, u32[]{:S(2)}) collective-permute-start(bf16[256,128]{1,0:T(8,128)(2,1)S(1)} %slice.179), channel_id=1, source_target_pairs={{0,96},{16,112},{32,0},{48,16},{64,32},{80,48},{96,64},{112,80},{1... | collective-permute-start | bytes 196616 | tf_op jit(solution)/shard_map/ppermute | solution.py:32
  30.1 12.8 %neighbour_sum_one.1 = (f32[32,128,128]{2,1,0:T(8,128)}, bf16[32,128,128]{2,1,0:T(8,128)(2,1)}) custom-call(s32[448]{0:T(512)} %get-tuple-element.30.refs_0_, s32[448]{0:T(512)} %fusion.17.refs_1_, s32[1]{0:T(128)} %bitcast.3.refs_2_, bf16[4,128,128]{2,1,0:T(8,128)(2,1)} %bitcast.120, bf16[4,128,128]{2,1,0:T(8,128)(2,1)} %bitcast.144, ...), custom_call_target="tpu_custom_call" | custom-call | flops 17999998976 | bytes 20971520 | tf_op jit(solution)/shard_map/neighbour_sum_one/pallas_call | solution.py:111
  43.0 2.9 %collective-permute-done.9 = bf16[32,128,128]{2,1,0:T(8,128)(2,1)S(1)} collective-permute-done((bf16[32,128,128]{2,1,0:T(8,128)(2,1)}, bf16[32,128,128]{2,1,0:T(8,128)(2,1)S(1)}, u32[]{:S(2)}, u32[]{:S(2)}) %collective-permute-start.9) | collective-permute-done | bytes 1048608 | tf_op jit(solution)/shard_map/ppermute | solution.py:36
  46.0 1.7 add_convert_fusion.13
  47.7 3.9 %collective-permute-start.10 = (bf16[4,128,128]{2,1,0:T(8,128)(2,1)S(1)}, bf16[4,128,128]{2,1,0:T(8,128)(2,1)S(1)}, u32[]{:S(2)}, u32[]{:S(2)}) collective-permute-start(bf16[4,128,128]{2,1,0:T(8,128)(2,1)S(1)} %get-tuple-element.38), channel_id=1, source_target_pairs={{0,8},{1,9},{2,10},{3,11},{4,12},{5,13},{6,14},{7,15},{8,0},{9,1},... | collective-permute-start | bytes 393224 | tf_op jit(solution)/shard_map/ppermute | solution.py:36
  51.6 2.8 %collective-permute-start.12 = (bf16[4,128,128]{2,1,0:T(8,128)(2,1)S(1)}, bf16[4,128,128]{2,1,0:T(8,128)(2,1)S(1)}, u32[]{:S(2)}, u32[]{:S(2)}) collective-permute-start(bf16[4,128,128]{2,1,0:T(8,128)(2,1)S(1)} %get-tuple-element.43), channel_id=1, source_target_pairs={{0,10},{1,11},{2,12},{3,13},{4,14},{5,15},{6,8},{7,9},{8,2},{9,3},... | collective-permute-start | bytes 393224 | tf_op jit(solution)/shard_map/ppermute | solution.py:36
  55.8 1.6 collective-permute-start.14
  57.4 1.8 collective-permute-start.15
  59.2 1.5 collective-permute-start.16
  61.0 3.2 %collective-permute-done.13 = bf16[4,128,128]{2,1,0:T(8,128)(2,1)S(1)} collective-permute-done((bf16[4,128,128]{2,1,0:T(8,128)(2,1)S(1)}, bf16[4,128,128]{2,1,0:T(8,128)(2,1)S(1)}, u32[]{:S(2)}, u32[]{:S(2)}) %collective-permute-start.13) | collective-permute-done | bytes 131104 | tf_op jit(solution)/shard_map/ppermute | solution.py:36
  64.2 3.9 %collective-permute-done.14 = bf16[4,128,128]{2,1,0:T(8,128)(2,1)S(1)} collective-permute-done((bf16[4,128,128]{2,1,0:T(8,128)(2,1)S(1)}, bf16[4,128,128]{2,1,0:T(8,128)(2,1)S(1)}, u32[]{:S(2)}, u32[]{:S(2)}) %collective-permute-start.14) | collective-permute-done | bytes 131104 | tf_op jit(solution)/shard_map/ppermute | solution.py:36
  71.2 3.1 %collective-permute-start.17 = (bf16[512,256]{1,0:T(8,128)(2,1)S(1)}, bf16[512,256]{1,0:T(8,128)(2,1)}, u32[]{:S(2)}, u32[]{:S(2)}) collective-permute-start(bf16[512,256]{1,0:T(8,128)(2,1)S(1)} %get-tuple-element.67), channel_id=1, source_target_pairs={{0,16},{16,0},{32,48},{48,32},{64,80},{80,64},{96,112},{112,96},{1... | collective-permute-start | bytes 786440 | tf_op jit(solution)/shard_map/ppermute | solution.py:32
  74.3 3.2 %collective-permute-start.19 = (bf16[512,256]{1,0:T(8,128)(2,1)S(1)}, bf16[512,256]{1,0:T(8,128)(2,1)S(1)}, u32[]{:S(2)}, u32[]{:S(2)}) collective-permute-start(bf16[512,256]{1,0:T(8,128)(2,1)S(1)} %get-tuple-element.67), channel_id=1, source_target_pairs={{0,96},{16,112},{32,0},{48,16},{64,32},{80,48},{96,64},{112,80},{1... | collective-permute-start | bytes 786440 | tf_op jit(solution)/shard_map/ppermute | solution.py:32
  77.5 2.6 %collective-permute-done.18 = bf16[512,256]{1,0:T(8,128)(2,1)S(1)} collective-permute-done((bf16[512,256]{1,0:T(8,128)(2,1)S(1)}, bf16[512,256]{1,0:T(8,128)(2,1)S(1)}, u32[]{:S(2)}, u32[]{:S(2)}) %collective-permute-start.18) | collective-permute-done | bytes 262176 | tf_op jit(solution)/shard_map/ppermute | solution.py:32
  80.9 2.6 %collective-permute-start.21 = (bf16[512,256]{1,0:T(8,128)(2,1)}, bf16[512,256]{1,0:T(8,128)(2,1)}, u32[]{:S(2)}, u32[]{:S(2)}) collective-permute-start(bf16[512,256]{1,0:T(8,128)(2,1)} %collective-permute-done.17), channel_id=1, source_target_pairs={{0,96},{16,112},{32,0},{48,16},{64,32},{80,48},{96,64},{112,80},{1... | collective-permute-start | bytes 786440 | tf_op jit(solution)/shard_map/ppermute | solution.py:32
  83.5 16.3 %neighbour_sum_back.1 = (f32[4,128,256]{2,1,0:T(8,128)}, bf16[4,128,256]{2,1,0:T(8,128)(2,1)}, bf16[4,128,256]{2,1,0:T(8,128)(2,1)}, bf16[4,128,256]{2,1,0:T(8,1...) custom-call(s32[448]{0:T(512)} %bitcast.138, ...), custom_call_target="tpu_custom_call" | custom-call | flops 17999998976 | bytes 20971520 | tf_op jit(solution)/shard_map/neighbour_sum_back/pallas_call | solution.py:111
  99.9 5.1 %collective-permute-start.34 = (bf16[4,128,256]{2,1,0:T(8,128)(2,1)}, bf16[4,128,256]{2,1,0:T(8,128)(2,1)S(1)}, u32[]{:S(2)}, u32[]{:S(2)}) collective-permute-start(bf16[4,128,256]{2,1,0:T(8,128)(2,1)} %get-tuple-element.22), channel_id=1, source_target_pairs={{0,16},{16,0},{32,48},{48,32},{64,80},{80,64},{96,112},{112,96},{1... | collective-permute-start | bytes 786440 | tf_op jit(solution)/shard_map/ppermute | solution.py:32
  106.4 2.1 collective-permute-start.24
  111.0 3.3 %collective-permute-done.23 = bf16[256,256]{1,0:T(8,128)(2,1)S(1)} collective-permute-done((bf16[256,256]{1,0:T(8,128)(2,1)S(1)}, bf16[256,256]{1,0:T(8,128)(2,1)S(1)}, u32[]{:S(2)}, u32[]{:S(2)}) %collective-permute-start.23) | collective-permute-done | bytes 131104 | tf_op jit(solution)/shard_map/ppermute | solution.py:32
  114.9 5.9 %collective-permute-start.37 = (bf16[4,128,256]{2,1,0:T(8,128)(2,1)}, bf16[4,128,256]{2,1,0:T(8,128)(2,1)S(1)}, u32[]{:S(2)}, u32[]{:S(2)}) collective-permute-start(bf16[4,128,256]{2,1,0:T(8,128)(2,1)} %get-tuple-element.25), channel_id=1, source_target_pairs={{0,112},{16,96},{32,16},{48,0},{64,48},{80,32},{96,80},{112,64},{1... | collective-permute-start | bytes 786440 | tf_op jit(solution)/shard_map/ppermute | solution.py:32
  120.9 2.8 %collective-permute-start.39 = (bf16[4,128,256]{2,1,0:T(8,128)(2,1)}, bf16[4,128,256]{2,1,0:T(8,128)(2,1)S(1)}, u32[]{:S(2)}, u32[]{:S(2)}) collective-permute-start(bf16[4,128,256]{2,1,0:T(8,128)(2,1)} %get-tuple-element.27), channel_id=1, source_target_pairs={{0,64},{16,80},{32,96},{48,112},{64,0},{80,16},{96,32},{112,48},{1... | collective-permute-start | bytes 786440 | tf_op jit(solution)/shard_map/ppermute | solution.py:32
  123.6 2.0 collective-permute-start.40
  125.7 16.3 %neighbour_sum_two.1 = (f32[32,128,256]{2,1,0:T(8,128)}, bf16[32,128,256]{2,1,0:T(8,128)(2,1)}) custom-call(s32[448]{0:T(512)} %get-tuple-element.30.refs_0_, s32[448]{0:T(512)} %fusion.17.refs_1_, s32[1]{0:T(128)} %bitcast.3.refs_2_, bf16[4,128,256]{2,1,0:T(8,128)(2,1)} %bitcast.112, bf16[4,128,256]{2,1,0:T(8,128)(2,1)} %bitcast.17.refs_4_, ...), custom_call_target="tpu_custom_call" | custom-call | flops 17999998976 | bytes 20971520 | tf_op jit(solution)/shard_map/neighbour_sum_two/pallas_call | solution.py:111
  146.4 1.7 collective-permute-done.41
  149.9 3.1 %collective-permute-start.42 = (f32[96,256]{1,0:T(8,128)S(1)}, f32[96,256]{1,0:T(8,128)S(1)}, u32[]{:S(2)}, u32[]{:S(2)}) collective-permute-start(f32[96,256]{1,0:T(8,128)S(1)} %get-tuple-element.55), channel_id=1, source_target_pairs={{0,2},{1,3},{2,4},{3,5},{4,6},{5,7},{6,0},{7,1},{8,10},{9,11},{10,... | collective-permute-start | bytes 294920 | tf_op jit(solution)/shard_map/ppermute | solution.py:36
  153.0 1.9 collective-permute-start.43
  154.9 1.5 collective-permute-start.44
  156.8 3.3 %collective-permute-done.43 = f32[96,256]{1,0:T(8,128)S(1)} collective-permute-done((f32[96,256]{1,0:T(8,128)S(1)}, f32[96,256]{1,0:T(8,128)S(1)}, u32[]{:S(2)}, u32[]{:S(2)}) %collective-permute-start.43) | collective-permute-done | bytes 98336 | tf_op jit(solution)/shard_map/ppermute | solution.py:36
  161.0 3.8 %collective-permute-start.45 = (f32[24,256]{1,0:T(8,128)S(1)}, f32[24,256]{1,0:T(8,128)S(1)}, u32[]{:S(2)}, u32[]{:S(2)}) collective-permute-start(f32[24,256]{1,0:T(8,128)S(1)} %get-tuple-element.64), channel_id=1, source_target_pairs={{0,32},{16,48},{32,64},{48,80},{64,96},{80,112},{96,0},{112,16},{1... | collective-permute-start | bytes 73736 | tf_op jit(solution)/shard_map/ppermute | solution.py:32
  164.8 4.5 %collective-permute-start.46 = (f32[24,256]{1,0:T(8,128)S(1)}, f32[24,256]{1,0:T(8,128)S(1)}, u32[]{:S(2)}, u32[]{:S(2)}) collective-permute-start(f32[24,256]{1,0:T(8,128)S(1)} %get-tuple-element.66), channel_id=1, source_target_pairs={{0,64},{16,80},{32,96},{48,112},{64,0},{80,16},{96,32},{112,48},{1... | collective-permute-start | bytes 73736 | tf_op jit(solution)/shard_map/ppermute | solution.py:32
  171.4 1.8 collective-permute-done.47
  173.2 5.3 %collective-permute-done.48 = f32[24,256]{1,0:T(8,128)S(1)} collective-permute-done((f32[24,256]{1,0:T(8,128)S(1)}, f32[24,256]{1,0:T(8,128)S(1)}, u32[]{:S(2)}, u32[]{:S(2)}) %collective-permute-start.48) | collective-permute-done | bytes 24608 | tf_op jit(solution)/shard_map/ppermute | solution.py:32
  178.7 3.6 %collective-permute-done.49 = f32[24,256]{1,0:T(8,128)S(1)} collective-permute-done((f32[24,256]{1,0:T(8,128)S(1)}, f32[24,256]{1,0:T(8,128)S(1)}, u32[]{:S(2)}, u32[]{:S(2)}) %collective-permute-start.49) | collective-permute-done | bytes 24608 | tf_op jit(solution)/shard_map/ppermute | solution.py:36
  182.4 2.7 %collective-permute-start.51 = (f32[24,256]{1,0:T(8,128)S(1)}, f32[24,256]{1,0:T(8,128)S(1)}, u32[]{:S(2)}, u32[]{:S(2)}) collective-permute-start(f32[24,256]{1,0:T(8,128)S(1)} %add.446), channel_id=1, source_target_pairs={{0,64},{16,80},{32,96},{48,112},{64,0},{80,16},{96,32},{112,48},{1... | collective-permute-start | bytes 73736 | tf_op jit(solution)/shard_map/ppermute | solution.py:32
  186.5 2.6 %add_convert_fusion.6 = (bf16[4,128,256]{2,1,0:T(8,128)(2,1)S(1)}, bf16[4,128,256]{2,1,0:T(8,128)(2,1)S(1)}, bf16[4,128,256]{2,1,0:T(8,128)(2,1)S(1)}, bf16[4,12...) fusion(f32[32,128,256]{2,1,0:T(8,128)} %get-tuple-element.19, ...), kind=kLoop, calls=%fused_computation.16 | loop fusion | flops 2752512 | bytes 7340032 | tf_op jit(solution)/shard_map/convert_element_type | solution.py:138
  190.5 3.9 %collective-permute-start.54 = (f32[96,256]{1,0:T(8,128)S(1)}, f32[96,256]{1,0:T(8,128)S(1)}, u32[]{:S(2)}, u32[]{:S(2)}) collective-permute-start(f32[96,256]{1,0:T(8,128)S(1)} %get-tuple-element.59), channel_id=1, source_target_pairs={{0,4},{1,5},{2,6},{3,7},{4,0},{5,1},{6,2},{7,3},{8,12},{9,13},{10,... | collective-permute-start | bytes 294920 | tf_op jit(solution)/shard_map/ppermute | solution.py:36
  194.4 1.7 collective-permute-start.55
  196.4 1.7 collective-permute-start.29
  198.6 3.1 %collective-permute-start.30 = (bf16[4,128,256]{2,1,0:T(8,128)(2,1)S(1)}, bf16[4,128,256]{2,1,0:T(8,128)(2,1)S(1)}, u32[]{:S(2)}, u32[]{:S(2)}) collective-permute-start(bf16[4,128,256]{2,1,0:T(8,128)(2,1)S(1)} %get-tuple-element.35), channel_id=1, source_target_pairs={{0,4},{1,5},{2,6},{3,7},{4,0},{5,1},{6,2},{7,3},{8,12},{9,13},{10,... | collective-permute-start | bytes 786440 | tf_op jit(solution)/shard_map/ppermute | solution.py:36
  202.1 3.4 %collective-permute-start.31 = (bf16[4,128,256]{2,1,0:T(8,128)(2,1)S(1)}, bf16[4,128,256]{2,1,0:T(8,128)(2,1)S(1)}, u32[]{:S(2)}, u32[]{:S(2)}) collective-permute-start(bf16[4,128,256]{2,1,0:T(8,128)(2,1)S(1)} %get-tuple-element.34), channel_id=1, source_target_pairs={{0,12},{1,13},{2,14},{3,15},{4,8},{5,9},{6,10},{7,11},{8,4},{9,5},... | collective-permute-start | bytes 786440 | tf_op jit(solution)/shard_map/ppermute | solution.py:36
  206.0 1.5 collective-permute-start.33
  207.6 9.9 %collective-permute-done.29 = bf16[4,128,256]{2,1,0:T(8,128)(2,1)S(1)} collective-permute-done((bf16[4,128,256]{2,1,0:T(8,128)(2,1)S(1)}, bf16[4,128,256]{2,1,0:T(8,128)(2,1)S(1)}, u32[]{:S(2)}, u32[]{:S(2)}) %collective-permute-start.29) | collective-permute-done | bytes 262176 | tf_op jit(solution)/shard_map/ppermute | solution.py:36
  217.6 3.4 %collective-permute-done.33 = bf16[4,128,256]{2,1,0:T(8,128)(2,1)S(1)} collective-permute-done((bf16[4,128,256]{2,1,0:T(8,128)(2,1)S(1)}, bf16[4,128,256]{2,1,0:T(8,128)(2,1)S(1)}, u32[]{:S(2)}, u32[]{:S(2)}) %collective-permute-start.33) | collective-permute-done | bytes 262176 | tf_op jit(solution)/shard_map/ppermute | solution.py:36
  (173 shorter events, 34.5 us)
Async XLA Ops:
  7.2 76.3 %all-gather.2.cloned.1.call-start = ((), (), s32[]{:S(2)}) async-start(), calls=%async_computation | async-start | bytes 4456448 | tf_op jit(solution)/shard_map/all_gather | solution.py:229
  7.9 8.0 %collective-permute-start = (bf16[512,128]{1,0:T(8,128)(2,1)}, bf16[512,128]{1,0:T(8,128)(2,1)S(1)}, u32[]{:S(2)}, u32[]{:S(2)}) collective-permute-start(bf16[512,128]{1,0:T(8,128)(2,1)} %param.10), channel_id=1, source_target_pairs={{0,16},{16,0},{32,48},{48,32},{64,80},{80,64},{96,112},{112,96},{1... | collective-permute-start | bytes 393224 | tf_op jit(solution)/shard_map/ppermute | solution.py:32
  12.0 8.5 %collective-permute-start.1 = (bf16[512,128]{1,0:T(8,128)(2,1)}, bf16[512,128]{1,0:T(8,128)(2,1)S(1)}, u32[]{:S(2)}, u32[]{:S(2)}) collective-permute-start(bf16[512,128]{1,0:T(8,128)(2,1)} %param.10), channel_id=1, source_target_pairs={{0,32},{16,48},{32,64},{48,80},{64,96},{80,112},{96,0},{112,16},{1... | collective-permute-start | bytes 393224 | tf_op jit(solution)/shard_map/ppermute | solution.py:32
  13.5 7.1 %collective-permute-start.2 = (bf16[512,128]{1,0:T(8,128)(2,1)}, bf16[512,128]{1,0:T(8,128)(2,1)S(1)}, u32[]{:S(2)}, u32[]{:S(2)}) collective-permute-start(bf16[512,128]{1,0:T(8,128)(2,1)} %param.10), channel_id=1, source_target_pairs={{0,96},{16,112},{32,0},{48,16},{64,32},{80,48},{96,64},{112,80},{1... | collective-permute-start | bytes 393224 | tf_op jit(solution)/shard_map/ppermute | solution.py:32
  15.9 8.0 %collective-permute-start.3 = (bf16[512,128]{1,0:T(8,128)(2,1)S(1)}, bf16[512,128]{1,0:T(8,128)(2,1)S(1)}, u32[]{:S(2)}, u32[]{:S(2)}) collective-permute-start(bf16[512,128]{1,0:T(8,128)(2,1)S(1)} %collective-permute-done), channel_id=1, source_target_pairs={{0,32},{16,48},{32,64},{48,80},{64,96},{80,112},{96,0},{112,16},{1... | collective-permute-start | bytes 393224 | tf_op jit(solution)/shard_map/ppermute | solution.py:32
  17.2 6.8 %collective-permute-start.4 = (bf16[512,128]{1,0:T(8,128)(2,1)S(1)}, bf16[512,128]{1,0:T(8,128)(2,1)S(1)}, u32[]{:S(2)}, u32[]{:S(2)}) collective-permute-start(bf16[512,128]{1,0:T(8,128)(2,1)S(1)} %collective-permute-done), channel_id=1, source_target_pairs={{0,96},{16,112},{32,0},{48,16},{64,32},{80,48},{96,64},{112,80},{1... | collective-permute-start | bytes 393224 | tf_op jit(solution)/shard_map/ppermute | solution.py:32
  20.5 8.1 %collective-permute-start.5 = (bf16[256,128]{1,0:T(8,128)(2,1)S(1)}, bf16[256,128]{1,0:T(8,128)(2,1)S(1)}, u32[]{:S(2)}, u32[]{:S(2)}) collective-permute-start(bf16[256,128]{1,0:T(8,128)(2,1)S(1)} %slice.176), channel_id=1, source_target_pairs={{0,32},{16,48},{32,64},{48,80},{64,96},{80,112},{96,0},{112,16},{1... | collective-permute-start | bytes 196616 | tf_op jit(solution)/shard_map/ppermute | solution.py:32
  20.7 7.9 %collective-permute-start.6 = (bf16[256,128]{1,0:T(8,128)(2,1)S(1)}, bf16[256,128]{1,0:T(8,128)(2,1)S(1)}, u32[]{:S(2)}, u32[]{:S(2)}) collective-permute-start(bf16[256,128]{1,0:T(8,128)(2,1)S(1)} %slice.177), channel_id=1, source_target_pairs={{0,96},{16,112},{32,0},{48,16},{64,32},{80,48},{96,64},{112,80},{1... | collective-permute-start | bytes 196616 | tf_op jit(solution)/shard_map/ppermute | solution.py:32
  47.7 9.7 %collective-permute-start.10 = (bf16[4,128,128]{2,1,0:T(8,128)(2,1)S(1)}, bf16[4,128,128]{2,1,0:T(8,128)(2,1)S(1)}, u32[]{:S(2)}, u32[]{:S(2)}) collective-permute-start(bf16[4,128,128]{2,1,0:T(8,128)(2,1)S(1)} %get-tuple-element.38), channel_id=1, source_target_pairs={{0,8},{1,9},{2,10},{3,11},{4,12},{5,13},{6,14},{7,15},{8,0},{9,1},... | collective-permute-start | bytes 393224 | tf_op jit(solution)/shard_map/ppermute | solution.py:36
  51.6 7.7 %collective-permute-start.11 = (bf16[4,128,128]{2,1,0:T(8,128)(2,1)S(1)}, bf16[4,128,128]{2,1,0:T(8,128)(2,1)S(1)}, u32[]{:S(2)}, u32[]{:S(2)}) collective-permute-start(bf16[4,128,128]{2,1,0:T(8,128)(2,1)S(1)} %get-tuple-element.44), channel_id=1, source_target_pairs={{0,2},{1,3},{2,4},{3,5},{4,6},{5,7},{6,0},{7,1},{8,10},{9,11},{10,... | collective-permute-start | bytes 393224 | tf_op jit(solution)/shard_map/ppermute | solution.py:36
  51.6 9.4 %collective-permute-start.12 = (bf16[4,128,128]{2,1,0:T(8,128)(2,1)S(1)}, bf16[4,128,128]{2,1,0:T(8,128)(2,1)S(1)}, u32[]{:S(2)}, u32[]{:S(2)}) collective-permute-start(bf16[4,128,128]{2,1,0:T(8,128)(2,1)S(1)} %get-tuple-element.43), channel_id=1, source_target_pairs={{0,10},{1,11},{2,12},{3,13},{4,14},{5,15},{6,8},{7,9},{8,2},{9,3},... | collective-permute-start | bytes 393224 | tf_op jit(solution)/shard_map/ppermute | solution.py:36
  54.4 9.8 %collective-permute-start.13 = (bf16[4,128,128]{2,1,0:T(8,128)(2,1)S(1)}, bf16[4,128,128]{2,1,0:T(8,128)(2,1)S(1)}, u32[]{:S(2)}, u32[]{:S(2)}) collective-permute-start(bf16[4,128,128]{2,1,0:T(8,128)(2,1)S(1)} %get-tuple-element.42), channel_id=1, source_target_pairs={{0,4},{1,5},{2,6},{3,7},{4,0},{5,1},{6,2},{7,3},{8,12},{9,13},{10,... | collective-permute-start | bytes 393224 | tf_op jit(solution)/shard_map/ppermute | solution.py:36
  55.8 12.3 %collective-permute-start.14 = (bf16[4,128,128]{2,1,0:T(8,128)(2,1)S(1)}, bf16[4,128,128]{2,1,0:T(8,128)(2,1)S(1)}, u32[]{:S(2)}, u32[]{:S(2)}) collective-permute-start(bf16[4,128,128]{2,1,0:T(8,128)(2,1)S(1)} %get-tuple-element.41), channel_id=1, source_target_pairs={{0,12},{1,13},{2,14},{3,15},{4,8},{5,9},{6,10},{7,11},{8,4},{9,5},... | collective-permute-start | bytes 393224 | tf_op jit(solution)/shard_map/ppermute | solution.py:36
  57.4 10.6 %collective-permute-start.15 = (bf16[4,128,128]{2,1,0:T(8,128)(2,1)S(1)}, bf16[4,128,128]{2,1,0:T(8,128)(2,1)S(1)}, u32[]{:S(2)}, u32[]{:S(2)}) collective-permute-start(bf16[4,128,128]{2,1,0:T(8,128)(2,1)S(1)} %get-tuple-element.40), channel_id=1, source_target_pairs={{0,6},{1,7},{2,0},{3,1},{4,2},{5,3},{6,4},{7,5},{8,14},{9,15},{10,... | collective-permute-start | bytes 393224 | tf_op jit(solution)/shard_map/ppermute | solution.py:36
  59.2 9.6 %collective-permute-start.16 = (bf16[4,128,128]{2,1,0:T(8,128)(2,1)S(1)}, bf16[4,128,128]{2,1,0:T(8,128)(2,1)S(1)}, u32[]{:S(2)}, u32[]{:S(2)}) collective-permute-start(bf16[4,128,128]{2,1,0:T(8,128)(2,1)S(1)} %get-tuple-element.39), channel_id=1, source_target_pairs={{0,14},{1,15},{2,8},{3,9},{4,10},{5,11},{6,12},{7,13},{8,6},{9,7},... | collective-permute-start | bytes 393224 | tf_op jit(solution)/shard_map/ppermute | solution.py:36
  71.2 8.9 %collective-permute-start.18 = (bf16[512,256]{1,0:T(8,128)(2,1)S(1)}, bf16[512,256]{1,0:T(8,128)(2,1)S(1)}, u32[]{:S(2)}, u32[]{:S(2)}) collective-permute-start(bf16[512,256]{1,0:T(8,128)(2,1)S(1)} %get-tuple-element.67), channel_id=1, source_target_pairs={{0,32},{16,48},{32,64},{48,80},{64,96},{80,112},{96,0},{112,16},{1... | collective-permute-start | bytes 786440 | tf_op jit(solution)/shard_map/ppermute | solution.py:32
  71.2 9.0 %collective-permute-start.17 = (bf16[512,256]{1,0:T(8,128)(2,1)S(1)}, bf16[512,256]{1,0:T(8,128)(2,1)}, u32[]{:S(2)}, u32[]{:S(2)}) collective-permute-start(bf16[512,256]{1,0:T(8,128)(2,1)S(1)} %get-tuple-element.67), channel_id=1, source_target_pairs={{0,16},{16,0},{32,48},{48,32},{64,80},{80,64},{96,112},{112,96},{1... | collective-permute-start | bytes 786440 | tf_op jit(solution)/shard_map/ppermute | solution.py:32
  74.3 30.6 %collective-permute-start.19 = (bf16[512,256]{1,0:T(8,128)(2,1)S(1)}, bf16[512,256]{1,0:T(8,128)(2,1)S(1)}, u32[]{:S(2)}, u32[]{:S(2)}) collective-permute-start(bf16[512,256]{1,0:T(8,128)(2,1)S(1)} %get-tuple-element.67), channel_id=1, source_target_pairs={{0,96},{16,112},{32,0},{48,16},{64,32},{80,48},{96,64},{112,80},{1... | collective-permute-start | bytes 786440 | tf_op jit(solution)/shard_map/ppermute | solution.py:32
  80.1 29.3 %collective-permute-start.22 = (bf16[256,256]{1,0:T(8,128)(2,1)S(1)}, bf16[256,256]{1,0:T(8,128)(2,1)S(1)}, u32[]{:S(2)}, u32[]{:S(2)}) collective-permute-start(bf16[256,256]{1,0:T(8,128)(2,1)S(1)} %slice.188), channel_id=1, source_target_pairs={{0,32},{16,48},{32,64},{48,80},{64,96},{80,112},{96,0},{112,16},{1... | collective-permute-start | bytes 393224 | tf_op jit(solution)/shard_map/ppermute | solution.py:32
  80.2 26.1 %collective-permute-start.20 = (bf16[512,256]{1,0:T(8,128)(2,1)}, bf16[512,256]{1,0:T(8,128)(2,1)S(1)}, u32[]{:S(2)}, u32[]{:S(2)}) collective-permute-start(bf16[512,256]{1,0:T(8,128)(2,1)} %collective-permute-done.17), channel_id=1, source_target_pairs={{0,32},{16,48},{32,64},{48,80},{64,96},{80,112},{96,0},{112,16},{1... | collective-permute-start | bytes 786440 | tf_op jit(solution)/shard_map/ppermute | solution.py:32
  80.9 25.5 %collective-permute-start.21 = (bf16[512,256]{1,0:T(8,128)(2,1)}, bf16[512,256]{1,0:T(8,128)(2,1)}, u32[]{:S(2)}, u32[]{:S(2)}) collective-permute-start(bf16[512,256]{1,0:T(8,128)(2,1)} %collective-permute-done.17), channel_id=1, source_target_pairs={{0,96},{16,112},{32,0},{48,16},{64,32},{80,48},{96,64},{112,80},{1... | collective-permute-start | bytes 786440 | tf_op jit(solution)/shard_map/ppermute | solution.py:32
  99.9 21.0 %collective-permute-start.34 = (bf16[4,128,256]{2,1,0:T(8,128)(2,1)}, bf16[4,128,256]{2,1,0:T(8,128)(2,1)S(1)}, u32[]{:S(2)}, u32[]{:S(2)}) collective-permute-start(bf16[4,128,256]{2,1,0:T(8,128)(2,1)} %get-tuple-element.22), channel_id=1, source_target_pairs={{0,16},{16,0},{32,48},{48,32},{64,80},{80,64},{96,112},{112,96},{1... | collective-permute-start | bytes 786440 | tf_op jit(solution)/shard_map/ppermute | solution.py:32
  104.9 18.7 %collective-permute-start.35 = (bf16[4,128,256]{2,1,0:T(8,128)(2,1)}, bf16[4,128,256]{2,1,0:T(8,128)(2,1)S(1)}, u32[]{:S(2)}, u32[]{:S(2)}) collective-permute-start(bf16[4,128,256]{2,1,0:T(8,128)(2,1)} %get-tuple-element.23), channel_id=1, source_target_pairs={{0,96},{16,112},{32,0},{48,16},{64,32},{80,48},{96,64},{112,80},{1... | collective-permute-start | bytes 786440 | tf_op jit(solution)/shard_map/ppermute | solution.py:32
  106.3 8.0 %collective-permute-start.23 = (bf16[256,256]{1,0:T(8,128)(2,1)S(1)}, bf16[256,256]{1,0:T(8,128)(2,1)S(1)}, u32[]{:S(2)}, u32[]{:S(2)}) collective-permute-start(bf16[256,256]{1,0:T(8,128)(2,1)S(1)} %slice.189), channel_id=1, source_target_pairs={{0,96},{16,112},{32,0},{48,16},{64,32},{80,48},{96,64},{112,80},{1... | collective-permute-start | bytes 393224 | tf_op jit(solution)/shard_map/ppermute | solution.py:32
  106.4 8.5 %collective-permute-start.24 = (bf16[256,256]{1,0:T(8,128)(2,1)S(1)}, bf16[256,256]{1,0:T(8,128)(2,1)S(1)}, u32[]{:S(2)}, u32[]{:S(2)}) collective-permute-start(bf16[256,256]{1,0:T(8,128)(2,1)S(1)} %slice.190), channel_id=1, source_target_pairs={{0,32},{16,48},{32,64},{48,80},{64,96},{80,112},{96,0},{112,16},{1... | collective-permute-start | bytes 393224 | tf_op jit(solution)/shard_map/ppermute | solution.py:32
  109.4 11.4 %collective-permute-start.25 = (bf16[256,256]{1,0:T(8,128)(2,1)S(1)}, bf16[256,256]{1,0:T(8,128)(2,1)S(1)}, u32[]{:S(2)}, u32[]{:S(2)}) collective-permute-start(bf16[256,256]{1,0:T(8,128)(2,1)S(1)} %slice.191), channel_id=1, source_target_pairs={{0,96},{16,112},{32,0},{48,16},{64,32},{80,48},{96,64},{112,80},{1... | collective-permute-start | bytes 393224 | tf_op jit(solution)/shard_map/ppermute | solution.py:32
  114.3 27.8 %collective-permute-start.36 = (bf16[4,128,256]{2,1,0:T(8,128)(2,1)S(1)}, bf16[4,128,256]{2,1,0:T(8,128)(2,1)S(1)}, u32[]{:S(2)}, u32[]{:S(2)}) collective-permute-start(bf16[4,128,256]{2,1,0:T(8,128)(2,1)S(1)} %copy-done.17), channel_id=1, source_target_pairs={{0,32},{16,48},{32,64},{48,80},{64,96},{80,112},{96,0},{112,16},{1... | collective-permute-start | bytes 786440 | tf_op jit(solution)/shard_map/ppermute | solution.py:32
  114.9 27.3 %collective-permute-start.37 = (bf16[4,128,256]{2,1,0:T(8,128)(2,1)}, bf16[4,128,256]{2,1,0:T(8,128)(2,1)S(1)}, u32[]{:S(2)}, u32[]{:S(2)}) collective-permute-start(bf16[4,128,256]{2,1,0:T(8,128)(2,1)} %get-tuple-element.25), channel_id=1, source_target_pairs={{0,112},{16,96},{32,16},{48,0},{64,48},{80,32},{96,80},{112,64},{1... | collective-permute-start | bytes 786440 | tf_op jit(solution)/shard_map/ppermute | solution.py:32
  120.8 21.3 %collective-permute-start.38 = (bf16[4,128,256]{2,1,0:T(8,128)(2,1)}, bf16[4,128,256]{2,1,0:T(8,128)(2,1)S(1)}, u32[]{:S(2)}, u32[]{:S(2)}) collective-permute-start(bf16[4,128,256]{2,1,0:T(8,128)(2,1)} %get-tuple-element.26), channel_id=1, source_target_pairs={{0,48},{16,32},{32,80},{48,64},{64,112},{80,96},{96,16},{112,0},{1... | collective-permute-start | bytes 786440 | tf_op jit(solution)/shard_map/ppermute | solution.py:32
  120.9 21.3 %collective-permute-start.39 = (bf16[4,128,256]{2,1,0:T(8,128)(2,1)}, bf16[4,128,256]{2,1,0:T(8,128)(2,1)S(1)}, u32[]{:S(2)}, u32[]{:S(2)}) collective-permute-start(bf16[4,128,256]{2,1,0:T(8,128)(2,1)} %get-tuple-element.27), channel_id=1, source_target_pairs={{0,64},{16,80},{32,96},{48,112},{64,0},{80,16},{96,32},{112,48},{1... | collective-permute-start | bytes 786440 | tf_op jit(solution)/shard_map/ppermute | solution.py:32
  123.6 18.6 %collective-permute-start.40 = (bf16[4,128,256]{2,1,0:T(8,128)(2,1)}, bf16[4,128,256]{2,1,0:T(8,128)(2,1)S(1)}, u32[]{:S(2)}, u32[]{:S(2)}) collective-permute-start(bf16[4,128,256]{2,1,0:T(8,128)(2,1)} %get-tuple-element.28), channel_id=1, source_target_pairs={{0,80},{16,64},{32,112},{48,96},{64,16},{80,0},{96,48},{112,32},{1... | collective-permute-start | bytes 786440 | tf_op jit(solution)/shard_map/ppermute | solution.py:32
  142.1 44.5 %collective-permute-start.26 = (bf16[32,128,256]{2,1,0:T(8,128)(2,1)}, bf16[32,128,256]{2,1,0:T(8,128)(2,1)S(1)}, u32[]{:S(2)}, u32[]{:S(2)}) collective-permute-start(bf16[32,128,256]{2,1,0:T(8,128)(2,1)} %get-tuple-element.20), channel_id=1, source_target_pairs={{0,1},{1,0},{2,3},{3,2},{4,5},{5,4},{6,7},{7,6},{8,9},{9,8},{10,11... | collective-permute-start | bytes 6291464 | tf_op jit(solution)/shard_map/ppermute | solution.py:36
  149.9 6.9 %collective-permute-start.42 = (f32[96,256]{1,0:T(8,128)S(1)}, f32[96,256]{1,0:T(8,128)S(1)}, u32[]{:S(2)}, u32[]{:S(2)}) collective-permute-start(f32[96,256]{1,0:T(8,128)S(1)} %get-tuple-element.55), channel_id=1, source_target_pairs={{0,2},{1,3},{2,4},{3,5},{4,6},{5,7},{6,0},{7,1},{8,10},{9,11},{10,... | collective-permute-start | bytes 294920 | tf_op jit(solution)/shard_map/ppermute | solution.py:36
  153.0 7.0 %collective-permute-start.43 = (f32[96,256]{1,0:T(8,128)S(1)}, f32[96,256]{1,0:T(8,128)S(1)}, u32[]{:S(2)}, u32[]{:S(2)}) collective-permute-start(f32[96,256]{1,0:T(8,128)S(1)} %get-tuple-element.57), channel_id=1, source_target_pairs={{0,4},{1,5},{2,6},{3,7},{4,0},{5,1},{6,2},{7,3},{8,12},{9,13},{10,... | collective-permute-start | bytes 294920 | tf_op jit(solution)/shard_map/ppermute | solution.py:36
  161.0 8.9 %collective-permute-start.45 = (f32[24,256]{1,0:T(8,128)S(1)}, f32[24,256]{1,0:T(8,128)S(1)}, u32[]{:S(2)}, u32[]{:S(2)}) collective-permute-start(f32[24,256]{1,0:T(8,128)S(1)} %get-tuple-element.64), channel_id=1, source_target_pairs={{0,32},{16,48},{32,64},{48,80},{64,96},{80,112},{96,0},{112,16},{1... | collective-permute-start | bytes 73736 | tf_op jit(solution)/shard_map/ppermute | solution.py:32
  164.8 6.5 %collective-permute-start.46 = (f32[24,256]{1,0:T(8,128)S(1)}, f32[24,256]{1,0:T(8,128)S(1)}, u32[]{:S(2)}, u32[]{:S(2)}) collective-permute-start(f32[24,256]{1,0:T(8,128)S(1)} %get-tuple-element.66), channel_id=1, source_target_pairs={{0,64},{16,80},{32,96},{48,112},{64,0},{80,16},{96,32},{112,48},{1... | collective-permute-start | bytes 73736 | tf_op jit(solution)/shard_map/ppermute | solution.py:32
  182.4 7.4 %collective-permute-start.50 = (f32[24,256]{1,0:T(8,128)S(1)}, f32[24,256]{1,0:T(8,128)S(1)}, u32[]{:S(2)}, u32[]{:S(2)}) collective-permute-start(f32[24,256]{1,0:T(8,128)S(1)} %add.446), channel_id=1, source_target_pairs={{0,32},{16,48},{32,64},{48,80},{64,96},{80,112},{96,0},{112,16},{1... | collective-permute-start | bytes 73736 | tf_op jit(solution)/shard_map/ppermute | solution.py:32
  182.4 7.4 %collective-permute-start.51 = (f32[24,256]{1,0:T(8,128)S(1)}, f32[24,256]{1,0:T(8,128)S(1)}, u32[]{:S(2)}, u32[]{:S(2)}) collective-permute-start(f32[24,256]{1,0:T(8,128)S(1)} %add.446), channel_id=1, source_target_pairs={{0,64},{16,80},{32,96},{48,112},{64,0},{80,16},{96,32},{112,48},{1... | collective-permute-start | bytes 73736 | tf_op jit(solution)/shard_map/ppermute | solution.py:32
  189.2 7.3 %collective-permute-start.27 = (bf16[4,128,256]{2,1,0:T(8,128)(2,1)S(1)}, bf16[4,128,256]{2,1,0:T(8,128)(2,1)S(1)}, u32[]{:S(2)}, u32[]{:S(2)}) collective-permute-start(bf16[4,128,256]{2,1,0:T(8,128)(2,1)S(1)} %get-tuple-element.31), channel_id=1, source_target_pairs={{0,8},{1,9},{2,10},{3,11},{4,12},{5,13},{6,14},{7,15},{8,0},{9,1},... | collective-permute-start | bytes 786440 | tf_op jit(solution)/shard_map/ppermute | solution.py:36
  189.5 9.1 %collective-permute-start.28 = (bf16[4,128,256]{2,1,0:T(8,128)(2,1)S(1)}, bf16[4,128,256]{2,1,0:T(8,128)(2,1)S(1)}, u32[]{:S(2)}, u32[]{:S(2)}) collective-permute-start(bf16[4,128,256]{2,1,0:T(8,128)(2,1)S(1)} %get-tuple-element.37), channel_id=1, source_target_pairs={{0,2},{1,3},{2,4},{3,5},{4,6},{5,7},{6,0},{7,1},{8,10},{9,11},{10,... | collective-permute-start | bytes 786440 | tf_op jit(solution)/shard_map/ppermute | solution.py:36
  189.9 12.2 %collective-permute-start.53 = (f32[96,256]{1,0:T(8,128)S(1)}, f32[96,256]{1,0:T(8,128)S(1)}, u32[]{:S(2)}, u32[]{:S(2)}) collective-permute-start(f32[96,256]{1,0:T(8,128)S(1)} %get-tuple-element.59), channel_id=1, source_target_pairs={{0,2},{1,3},{2,4},{3,5},{4,6},{5,7},{6,0},{7,1},{8,10},{9,11},{10,... | collective-permute-start | bytes 294920 | tf_op jit(solution)/shard_map/ppermute | solution.py:36
  190.5 15.0 %collective-permute-start.54 = (f32[96,256]{1,0:T(8,128)S(1)}, f32[96,256]{1,0:T(8,128)S(1)}, u32[]{:S(2)}, u32[]{:S(2)}) collective-permute-start(f32[96,256]{1,0:T(8,128)S(1)} %get-tuple-element.59), channel_id=1, source_target_pairs={{0,4},{1,5},{2,6},{3,7},{4,0},{5,1},{6,2},{7,3},{8,12},{9,13},{10,... | collective-permute-start | bytes 294920 | tf_op jit(solution)/shard_map/ppermute | solution.py:36
  194.4 11.6 %collective-permute-start.55 = (f32[96,256]{1,0:T(8,128)S(1)}, f32[96,256]{1,0:T(8,128)S(1)}, u32[]{:S(2)}, u32[]{:S(2)}) collective-permute-start(f32[96,256]{1,0:T(8,128)S(1)} %get-tuple-element.59), channel_id=1, source_target_pairs={{0,6},{1,7},{2,0},{3,1},{4,2},{5,3},{6,4},{7,5},{8,14},{9,15},{10,... | collective-permute-start | bytes 294920 | tf_op jit(solution)/shard_map/ppermute | solution.py:36
  196.4 21.1 %collective-permute-start.29 = (bf16[4,128,256]{2,1,0:T(8,128)(2,1)S(1)}, bf16[4,128,256]{2,1,0:T(8,128)(2,1)S(1)}, u32[]{:S(2)}, u32[]{:S(2)}) collective-permute-start(bf16[4,128,256]{2,1,0:T(8,128)(2,1)S(1)} %get-tuple-element.36), channel_id=1, source_target_pairs={{0,10},{1,11},{2,12},{3,13},{4,14},{5,15},{6,8},{7,9},{8,2},{9,3},... | collective-permute-start | bytes 786440 | tf_op jit(solution)/shard_map/ppermute | solution.py:36
  198.6 19.0 %collective-permute-start.30 = (bf16[4,128,256]{2,1,0:T(8,128)(2,1)S(1)}, bf16[4,128,256]{2,1,0:T(8,128)(2,1)S(1)}, u32[]{:S(2)}, u32[]{:S(2)}) collective-permute-start(bf16[4,128,256]{2,1,0:T(8,128)(2,1)S(1)} %get-tuple-element.35), channel_id=1, source_target_pairs={{0,4},{1,5},{2,6},{3,7},{4,0},{5,1},{6,2},{7,3},{8,12},{9,13},{10,... | collective-permute-start | bytes 786440 | tf_op jit(solution)/shard_map/ppermute | solution.py:36
  202.1 15.5 %collective-permute-start.31 = (bf16[4,128,256]{2,1,0:T(8,128)(2,1)S(1)}, bf16[4,128,256]{2,1,0:T(8,128)(2,1)S(1)}, u32[]{:S(2)}, u32[]{:S(2)}) collective-permute-start(bf16[4,128,256]{2,1,0:T(8,128)(2,1)S(1)} %get-tuple-element.34), channel_id=1, source_target_pairs={{0,12},{1,13},{2,14},{3,15},{4,8},{5,9},{6,10},{7,11},{8,4},{9,5},... | collective-permute-start | bytes 786440 | tf_op jit(solution)/shard_map/ppermute | solution.py:36
  205.5 12.0 %collective-permute-start.32 = (bf16[4,128,256]{2,1,0:T(8,128)(2,1)S(1)}, bf16[4,128,256]{2,1,0:T(8,128)(2,1)S(1)}, u32[]{:S(2)}, u32[]{:S(2)}) collective-permute-start(bf16[4,128,256]{2,1,0:T(8,128)(2,1)S(1)} %get-tuple-element.33), channel_id=1, source_target_pairs={{0,6},{1,7},{2,0},{3,1},{4,2},{5,3},{6,4},{7,5},{8,14},{9,15},{10,... | collective-permute-start | bytes 786440 | tf_op jit(solution)/shard_map/ppermute | solution.py:36
  206.0 15.0 %collective-permute-start.33 = (bf16[4,128,256]{2,1,0:T(8,128)(2,1)S(1)}, bf16[4,128,256]{2,1,0:T(8,128)(2,1)S(1)}, u32[]{:S(2)}, u32[]{:S(2)}) collective-permute-start(bf16[4,128,256]{2,1,0:T(8,128)(2,1)S(1)} %get-tuple-element.32), channel_id=1, source_target_pairs={{0,14},{1,15},{2,8},{3,9},{4,10},{5,11},{6,12},{7,13},{8,6},{9,7},... | collective-permute-start | bytes 786440 | tf_op jit(solution)/shard_map/ppermute | solution.py:36
  (39 other events, 468.3 us)
Sparse Core Ops, SparseCore 0:
  9.7 39.9 all-gather.1

commit v2 on v1

v2 whole, which is shorter than its diff:
```python
import functools

import jax
import jax.numpy as jnp
from jax import lax
from jax.experimental import pallas as pl
from jax.experimental.pallas import tpu as pltpu
from jax.sharding import PartitionSpec as P

BF = jnp.bfloat16
F32 = jnp.float32
UNROLL = 56
DEPTH = 3


def row_perm(dy, dz):
    return [(y * 2 + h, ((y + dy) % 4) * 2 + (h ^ dz)) for y in range(4) for h in range(2)]


def col_perm(dx, dz, dc):
    return [
        ((z * 4 + x) * 2 + c, ((z ^ dz) * 4 + (x + dx) % 4) * 2 + (c ^ dc))
        for z in range(2)
        for x in range(4)
        for c in range(2)
    ]


def send_both_z(value):
    pairs = [(r * 16 + c, (r ^ 1) * 16 + (c ^ 8)) for r in range(8) for c in range(16)]
    return lax.ppermute(value, ("row", "col"), pairs)


def send_row(value, dy, dz):
    return lax.ppermute(value, "row", row_perm(dy, dz))


def send_col(value, dx, dz, dc=0):
    return lax.ppermute(value, "col", col_perm(dx, dz, dc))


def gather_row(value):
    pair = jnp.concatenate([value, send_row(value, 0, 1)])
    far, below, above = [send_row(pair, dy, 0) for dy in (2, 1, 3)]
    return [pair, below, above, far]


def tile_kernel(transpose, n_pieces, splits, *refs):
    src, dst, turns = refs[:3]
    pieces = refs[3 : 3 + n_pieces]
    values = refs[3 + n_pieces]
    outs = refs[4 + n_pieces : 4 + n_pieces + len(splits)]
    held, ring, total, rounded, piece_sems, ring_sems, out_sems = refs[4 + n_pieces + len(splits) :]
    count = turns[0]

    def fetch(turn, slot):
        return pltpu.make_async_copy(
            values.at[pl.ds(turn * UNROLL, UNROLL)], ring.at[pl.ds(slot * UNROLL, UNROLL)], ring_sems.at[slot]
        )

    copies = []
    at = 0
    for k, piece in enumerate(pieces):
        copy = pltpu.make_async_copy(piece, held.at[pl.ds(at, piece.shape[0])], piece_sems.at[k])
        copy.start()
        copies.append(copy)
        at += piece.shape[0]
    for slot in range(DEPTH):

        @pl.when(slot < count)
        def _():
            fetch(slot, slot).start()

    def clear(i, carry):
        total[i] = jnp.zeros(total.shape[1:], F32)
        return carry

    lax.fori_loop(0, total.shape[0], clear, 0)
    for copy in copies:
        copy.wait()

    def body(turn, carry):
        slot = lax.rem(turn, DEPTH)
        fetch(turn, slot).wait()
        for u in range(UNROLL):
            s = src[turn * UNROLL + u]
            d = dst[turn * UNROLL + u]
            dims = (((0,), (0,)), ((), ())) if transpose else (((1,), (0,)), ((), ()))
            total[d] += lax.dot_general(ring[slot * UNROLL + u], held[s], dims, preferred_element_type=F32)

        @pl.when(turn + DEPTH < count)
        def _():
            fetch(turn + DEPTH, slot).start()

        return carry

    lax.fori_loop(0, count, body, 0)

    copies = []
    at = 0
    for k, (out, (blocks, kind)) in enumerate(zip(outs, splits)):
        if kind == F32:
            copies.append(pltpu.make_async_copy(total.at[pl.ds(at, blocks)], out, out_sems.at[k]))
            copies[-1].start()
        at += blocks
    at = 0
    to = 0
    for k, (out, (blocks, kind)) in enumerate(zip(outs, splits)):
        if kind != F32:

            def cast(i, carry, at=at, to=to):
                rounded[to + i] = total[at + i].astype(BF)
                return carry

            lax.fori_loop(0, blocks, cast, 0)
            copies.append(pltpu.make_async_copy(rounded.at[pl.ds(to, blocks)], out, out_sems.at[k]))
            copies[-1].start()
            to += blocks
        at += blocks
    for copy in copies:
        copy.wait()


def tile_product(src, dst, turns, pieces, values, splits, transpose, name, vmem=40 << 20):
    _, block, _ = values.shape
    width = pieces[0].shape[-1]
    pieces = [piece.reshape(-1, block, width) for piece in pieces]
    n_src = sum(piece.shape[0] for piece in pieces)
    n_dst = sum(count for count, _ in splits)
    n_rounded = sum(count for count, kind in splits if kind != F32)
    anywhere = pl.BlockSpec(memory_space=pl.ANY)
    return pl.pallas_call(
        functools.partial(tile_kernel, transpose, len(pieces), splits),
        grid_spec=pltpu.PrefetchScalarGridSpec(
            num_scalar_prefetch=3,
            grid=(1,),
            in_specs=[anywhere] * (len(pieces) + 1),
            out_specs=[anywhere] * len(splits),
            scratch_shapes=[
                pltpu.VMEM((n_src, block, width), BF),
                pltpu.VMEM((DEPTH * UNROLL, block, block), BF),
                pltpu.VMEM((n_dst + 1, block, width), F32),
                pltpu.VMEM((n_rounded, block, width), BF),
                pltpu.SemaphoreType.DMA((len(pieces),)),
                pltpu.SemaphoreType.DMA((DEPTH,)),
                pltpu.SemaphoreType.DMA((len(splits),)),
            ],
        ),
        out_shape=[jax.ShapeDtypeStruct((count, block, width), kind) for count, kind in splits],
        compiler_params=pltpu.CompilerParams(vmem_limit_bytes=vmem),
        cost_estimate=pl.CostEstimate(flops=18_000_000_000, bytes_accessed=20 << 20, transcendentals=0),
        name=name,
    )(src, dst, turns, *pieces, values)


def add_cores(own, other):
    width = own.shape[-1]

    def part(d):
        return (own[8 * d : 8 * d + 8] + other[8 * d : 8 * d + 8].astype(F32)).reshape(-1, width)

    return part(0), [part(d).astype(BF) for d in (2, 1, 3)]


def send_x(parts):
    return [send_col(part, d, 0) for part, d in zip(parts, (2, 1, 3))]


def add_x(own, sent):
    total = own + sent[0].astype(F32) + sent[1].astype(F32) + sent[2].astype(F32)
    return total.reshape(2, -1, total.shape[-1])


def add_z(halves):
    return halves[0] + send_col(halves[1].astype(BF), 0, 1).astype(F32)


def add_z_hi(own, sent):
    other = jnp.concatenate(sent).astype(F32)
    return (own + other).reshape(4, -1, own.shape[-1])


def sum_y(parts):
    sent = [send_row(parts[d].astype(BF), d, 0) for d in (2, 1, 3)]
    return parts[0] + sent[0].astype(F32) + sent[1].astype(F32) + sent[2].astype(F32)


def pick(parts, i):
    return lax.dynamic_index_in_dim(parts, i, 0, False)


def sum_cores(value, core):
    halves = value.reshape(2, -1, value.shape[-1])
    return pick(halves, core) + send_col(pick(halves, 1 - core), 0, 0, 1)


def scatter_x(part, x):
    parts = part.reshape(4, -1, part.shape[-1])
    sent = [send_col(pick(parts, (x + d) % 4), d, 0) for d in (2, 1, 3)]
    return pick(parts, x) + sent[0] + sent[1] + sent[2]


def exchange_y(part):
    far, above, below = [send_row(part, d, 0) for d in (2, 1, 3)]
    return (part + far) + (above + below)


def exchange_z(part):
    high, low, both = send_row(part, 0, 1), send_col(part, 0, 1), send_both_z(part)
    return (part + high) + (low + both)


def gather_x(part, x):
    far, above, below = [send_col(part, d, 0) for d in (2, 1, 3)]
    parts = jnp.stack([part, above, far, below])
    return jnp.concatenate([pick(parts, (x - j) % 4) for j in range(4)])


def fdot(left, right):
    return jnp.dot(left, right.astype(F32), precision=lax.Precision.HIGHEST, preferred_element_type=F32)


def local(
    features,
    cotangent,
    w_self1,
    w_neigh1,
    w_self2,
    w_neigh2,
    tile_rows,
    tile_cols,
    tile_values,
    tile_live,
):
    values = tile_values[0, 0]
    slots = values.shape[0]
    live = tile_live[0, 0]
    rows_here = tile_rows[0, 0]
    cols_here = tile_cols[0, 0]
    row_at = lax.axis_index("row")
    col_at = lax.axis_index("col")
    y, z_hi = row_at // 2, row_at % 2
    z_lo, x, core = col_at // 8, (col_at // 2) % 4, col_at % 2

    owner = cols_here // 4
    dy = (owner // 2 - y) % 4
    dz = (owner % 2) ^ z_hi
    place = jnp.where(dy == 0, 0, jnp.where(dy == 3, 2, jnp.where(dy == 1, 4, 6))) + dz
    col_place = place * 4 + cols_here % 4
    col_sum_place = dz * 16 + dy * 4 + cols_here % 4
    owner = rows_here // 4
    dx = ((owner // 2) % 4 - x) % 4
    dz = (owner // 8) ^ z_lo
    row_place = ((owner % 2) ^ core) * 32 + (dx * 2 + dz) * 4 + rows_here % 4
    alive = jnp.arange(slots, dtype=jnp.int32) < live
    row_target = jnp.where(alive, row_place, 64)
    col_target = jnp.where(alive, col_sum_place, 32)
    turns = ((live + UNROLL - 1) // UNROLL).reshape(1)

    forward_splits = ((32, F32), (32, BF))
    back_splits = ((16, F32), (8, BF), (8, BF))

    gathered_c = lax.all_gather(cotangent, "col", axis=0, tiled=True)
    gathered_x = gather_row(features)
    own, other = tile_product(
        col_place, row_target, turns, gathered_x, values, forward_splits, False, "neighbour_sum_one"
    )
    mine, parts = add_cores(own, send_col(other, 0, 0, 1))
    last, gathered_c = lax.optimization_barrier((parts[2], gathered_c))
    sent = send_x([parts[0], parts[1], last])
    back_own, *back_parts = tile_product(
        rows_here, col_target, turns, [gathered_c], values, back_splits, True, "neighbour_sum_back"
    )
    sent, back_parts = lax.optimization_barrier((sent, back_parts))
    back_parts = [send_row(part, 0, 1) for part in back_parts]
    agg1 = add_z(add_x(mine, sent))
    z1 = jnp.dot(features, w_self1, preferred_element_type=F32) + fdot(agg1, w_neigh1)
    h1 = jax.nn.silu(z1).astype(BF)
    gathered_h = gather_row(h1)
    gathered_h, back_parts = lax.optimization_barrier((gathered_h, back_parts))
    back_parts = add_z_hi(back_own, back_parts)
    gathered_h, back_parts = lax.optimization_barrier((gathered_h, back_parts))
    back = sum_y(back_parts)
    own, other = tile_product(
        col_place, row_target, turns, gathered_h, values, forward_splits, False, "neighbour_sum_two"
    )
    own, other, back = lax.optimization_barrier((own, other, back))
    other = send_col(other, 0, 0, 1)
    dh1 = jnp.dot(cotangent, w_self2.T, preferred_element_type=F32) + fdot(back, w_neigh2.T)
    sigma = jax.nn.sigmoid(z1)
    dz1 = (dh1 * (sigma + z1 * sigma * (1.0 - sigma))).astype(BF)
    local_self2 = jnp.dot(h1.T, cotangent, preferred_element_type=F32)
    local_neigh2 = jnp.dot(
        h1.T.astype(F32), back, precision=lax.Precision.HIGHEST, preferred_element_type=F32
    )
    local_self1 = jnp.dot(features.T, dz1, preferred_element_type=F32)
    local_neigh1 = fdot(agg1.T, dz1)
    grads = jnp.concatenate([local_self1, local_neigh1, local_self2, local_neigh2])
    mine, parts = add_cores(own, other)
    sent = send_x(parts)
    grads = exchange_y(scatter_x(sum_cores(grads, core), x))
    sent, grads = lax.optimization_barrier((sent, grads))
    grads = exchange_z(grads)
    agg2 = add_z(add_x(mine, sent))
    output = (jnp.dot(h1, w_self2, preferred_element_type=F32) + fdot(agg2, w_neigh2)).astype(BF)
    grads = gather_x(grads, x)
    other = send_col(grads, 0, 0, 1)
    grads = jnp.where(core == 0, jnp.concatenate([grads, other]), jnp.concatenate([other, grads]))
    return (output, grads[:128], grads[128:256], grads[256:512], grads[512:])


def solution(mesh):
    return jax.shard_map(
        local,
        mesh=mesh,
        in_specs=(
            P(("row", "col"), None),
            P(("row", "col"), None),
            P(),
            P(),
            P(),
            P(),
            P("row", "col", None),
            P("row", "col", None),
            P("row", "col", None, None, None),
            P("row", "col"),
        ),
        out_specs=(P(("row", "col"), None), P(), P(), P(), P()),
        check_vma=False,
    )
```

time: 232 us -> 206 us (0.89)
  starting transfers between devices: 97.7 us -> 56.9 us
  waiting for transfers between devices: 50.7 us -> 77.4 us
  Pallas kernels: 45.4 us -> 31.5 us
  local copies, waits for them, and re-layouts: 4.03 us -> 6.87 us
    ppermute x32 -> x17, waiting for transfers between devices: 16 us -> 45.6 us  [send_row(): return lax.ppermute(value, 'row', row_perm(dy, dz))]
    ppermute x32 -> x17, starting transfers between devices: 60.4 us -> 31 us  [send_row(): return lax.ppermute(value, 'row', row_perm(dy, dz))]
    pallas_call x3, Pallas kernels: 45.4 us -> 31.5 us  [tile_product(): pl.pallas_call(functools.partial(tile_kernel, transpose, len(pieces), spl...]
    ppermute x25 -> x19, starting transfers between devices: 37.3 us -> 23.7 us  [send_col(): return lax.ppermute(value, 'col', col_perm(dx, dz, dc))]
    ppermute x25 -> x19, waiting for transfers between devices: 34 us -> 25.8 us  [send_col(): return lax.ppermute(value, 'col', col_perm(dx, dz, dc))]
    all_gather x1, waiting for transfers between devices: 0.01 us -> 4.17 us  [local(): gathered_c = lax.all_gather(cotangent, 'col', axis=0, tiled=True)]
    unnamed x58 -> x41, local copies, waits for them, and re-layouts: 1.46 us -> 4.4 us
  transfers between devices with their start and end apart: 58 -> 38, of which waited for: 20 -> 23; matrix products, arithmetic and copies ran while one was open for 8% -> 7% of each run, Pallas kernels for 20% -> 15%
where the time goes in v2:
time: 206 us; the launch traced here: 205 us
  waiting for transfers between devices  77.4 us (38%)
  starting transfers between devices  56.9 us (28%)
  Pallas kernels  31.5 us (15%)
  between operations  15.3 us (7%)
  other arithmetic  11.5 us (6%)
  local copies, waits for them, and re-layouts  6.87 us (3%)
  matrix products  5.84 us (3%)
    ppermute x17, waiting for transfers between devices, send_row(): return lax.ppermute(value, 'row', row_perm(dy, dz))  45.6 us
    pallas_call x3, Pallas kernels, tile_product(): pl.pallas_call(functools.partial(tile_kernel, transpose, len(pieces), spl...  31.5 us
    ppermute x17, starting transfers between devices, send_row(): return lax.ppermute(value, 'row', row_perm(dy, dz))  31 us
    ppermute x19, waiting for transfers between devices, send_col(): return lax.ppermute(value, 'col', col_perm(dx, dz, dc))  25.8 us
    ppermute x19, starting transfers between devices, send_col(): return lax.ppermute(value, 'col', col_perm(dx, dz, dc))  23.7 us
    convert_element_type x2, other arithmetic, add_cores(): return (part(0), [part(d).astype(BF) for d in (2, 1, 3)])  4.65 us
    unnamed x41, local copies, waits for them, and re-layouts  4.4 us
    all_gather x1, waiting for transfers between devices, local(): gathered_c = lax.all_gather(cotangent, 'col', axis=0, tiled=True)  4.17 us
  transfers between devices with their start and end apart: 38, of which 23 were waited for; matrix products, arithmetic and copies ran while one was open for 7% of the time, Pallas kernels for 15%

profile of v2, /device:TPU:0, one launch (start us, length us, event | category | flops | bytes accessed | tf_op | source)
XLA Modules:
  0.0 205.4 jit_solution(12416297728054713318)
XLA Ops:
  7.9 4.0 %collective-permute-start = (bf16[512,128]{1,0:T(8,128)(2,1)}, bf16[512,128]{1,0:T(8,128)(2,1)S(1)}, u32[]{:S(2)}, u32[]{:S(2)}) collective-permute-start(bf16[512,128]{1,0:T(8,128)(2,1)} %param.10), channel_id=1, source_target_pairs={{0,16},{16,0},{32,48},{48,32},{64,80},{80,64},{96,112},{112,96},{1... | collective-permute-start | bytes 393224 | tf_op jit(solution)/shard_map/ppermute | solution.py:35
  13.5 2.1 %collective-permute-done = bf16[512,128]{1,0:T(8,128)(2,1)S(1)} collective-permute-done((bf16[512,128]{1,0:T(8,128)(2,1)}, bf16[512,128]{1,0:T(8,128)(2,1)S(1)}, u32[]{:S(2)}, u32[]{:S(2)}) %collective-permute-start) | collective-permute-done | bytes 131104 | tf_op jit(solution)/shard_map/ppermute | solution.py:35
  15.7 1.6 collective-permute-start.1
  17.3 1.7 collective-permute-start.2
  19.0 2.0 collective-permute-start.3
  22.5 2.6 %collective-permute-done.1 = bf16[1024,128]{1,0:T(8,128)(2,1)S(1)} collective-permute-done((bf16[1024,128]{1,0:T(8,128)(2,1)S(1)}, bf16[1024,128]{1,0:T(8,128)(2,1)S(1)}, u32[]{:S(2)}, u32[]{:S(2)}) %collective-permute-start.1) | collective-permute-done | bytes 262176 | tf_op jit(solution)/shard_map/ppermute | solution.py:35
  25.1 4.4 %collective-permute-done.2 = bf16[1024,128]{1,0:T(8,128)(2,1)S(1)} collective-permute-done((bf16[1024,128]{1,0:T(8,128)(2,1)S(1)}, bf16[1024,128]{1,0:T(8,128)(2,1)S(1)}, u32[]{:S(2)}, u32[]{:S(2)}) %collective-permute-start.2) | collective-permute-done | bytes 262176 | tf_op jit(solution)/shard_map/ppermute | solution.py:35
  29.5 1.8 collective-permute-done.3
  31.3 8.1 %neighbour_sum_one.1 = (f32[32,128,128]{2,1,0:T(8,128)S(1)}, bf16[32,128,128]{2,1,0:T(8,128)(2,1)S(1)}) custom-call(s32[448]{0:T(512)S(1)} %get-tuple-element.102.refs_0_, s32[448]{0:T(512)S(1)} %get-tuple-element.101.refs_1_, s32[1]{0:T(128)} %bitcast.3.refs_2_, bf16[8,128,128]{2,1,0:T(8,128)(2,1)S(1)} %bitcast.102, bf16[8,128,128]{2,1,0:T(8,128)(2,1)S(1)} %bitcast.106, ...), custom_call_target="tpu_custom_call" | custom-call | flops 17999998976 | bytes 20971520 | tf_op jit(solution)/shard_map/neighbour_sum_one/pallas_call | solution.py:132
  39.5 2.6 %collective-permute-done.4 = bf16[32,128,128]{2,1,0:T(8,128)(2,1)S(1)} collective-permute-done((bf16[32,128,128]{2,1,0:T(8,128)(2,1)S(1)}, bf16[32,128,128]{2,1,0:T(8,128)(2,1)S(1)}, u32[]{:S(2)}, u32[]{:S(2)}) %collective-permute-start.4) | collective-permute-done | bytes 1048608 | tf_op jit(solution)/shard_map/ppermute | solution.py:39
  43.4 3.1 %collective-permute-start.6 = (bf16[1024,128]{1,0:T(8,128)(2,1)}, bf16[1024,128]{1,0:T(8,128)(2,1)}, u32[]{:S(2)}, u32[]{:S(2)}) collective-permute-start(bf16[1024,128]{1,0:T(8,128)(2,1)} %bitcast.11), channel_id=1, source_target_pairs={{0,2},{1,3},{2,4},{3,5},{4,6},{5,7},{6,0},{7,1},{8,10},{9,11},{10,... | collective-permute-start | bytes 786440 | tf_op jit(solution)/shard_map/ppermute | solution.py:39
  46.5 4.2 %all-gather.2.cloned.1.call-done = bf16[8192,256]{1,0:T(8,128)(2,1)} async-done(((bf16[512,256]{1,0:T(8,128)(2,1)}), bf16[8192,256]{1,0:T(8,128)(2,1)}) %all-gather.2.cloned.1.call-update) | async-done | bytes 4194320 | tf_op jit(solution)/shard_map/all_gather | solution.py:263
  50.6 2.0 collective-permute-start.7
  52.6 2.2 %copy-done.3 = bf16[8192,256]{1,0:T(8,128)(2,1)S(1)} copy-done((bf16[8192,256]{1,0:T(8,128)(2,1)S(1)}, bf16[8192,256]{1,0:T(8,128)(2,1)}, u32[]{:S(2)}) %copy-start.3) | copy-done | bytes 4194328
  54.8 11.6 %neighbour_sum_back.1 = (f32[16,128,256]{2,1,0:T(8,128)S(1)}, bf16[8,128,256]{2,1,0:T(8,128)(2,1)}, bf16[8,128,256]{2,1,0:T(8,128)(2,1)S(1)}) custom-call(s32[448]{0:T(512)S(1)} %bitcast.104, s32[448]{0:T(512)S(1)} %get-tuple-element.77.refs_1_, s32[1]{0:T(128)} %bitcast.3.refs_2_, bf16[64,128,256]{2,1,0:T(8,128)(2,1)S(1)} %bitcast.105, ...), custom_call_target="tpu_custom_call" | custom-call | flops 17999998976 | bytes 20971520 | tf_op jit(solution)/shard_map/neighbour_sum_back/pallas_call | solution.py:132
  66.5 1.2 fusion.8
  68.1 5.3 %collective-permute-done.8 = bf16[512,128]{1,0:T(8,128)(2,1)S(1)} collective-permute-done((bf16[512,128]{1,0:T(8,128)(2,1)S(1)}, bf16[512,128]{1,0:T(8,128)(2,1)S(1)}, u32[]{:S(2)}, u32[]{:S(2)}) %collective-permute-start.8) | collective-permute-done | bytes 131104 | tf_op jit(solution)/shard_map/ppermute | solution.py:39
  73.4 1.2 fusion.11
  74.6 3.5 %collective-permute-start.13 = (bf16[8,128,256]{2,1,0:T(8,128)(2,1)}, bf16[8,128,256]{2,1,0:T(8,128)(2,1)}, u32[]{:S(2)}, u32[]{:S(2)}) collective-permute-start(bf16[8,128,256]{2,1,0:T(8,128)(2,1)} %get-tuple-element.46), channel_id=1, source_target_pairs={{0,16},{16,0},{32,48},{48,32},{64,80},{80,64},{96,112},{112,96},{1... | collective-permute-start | bytes 1572872 | tf_op jit(solution)/shard_map/ppermute | solution.py:35
  78.2 7.2 %collective-permute-done.9 = bf16[512,256]{1,0:T(8,128)(2,1)S(1)} collective-permute-done((bf16[512,256]{1,0:T(8,128)(2,1)S(1)}, bf16[512,256]{1,0:T(8,128)(2,1)S(1)}, u32[]{:S(2)}, u32[]{:S(2)}) %collective-permute-start.9) | collective-permute-done | bytes 262176 | tf_op jit(solution)/shard_map/ppermute | solution.py:35
  86.2 2.5 %collective-permute-start.11 = (bf16[1024,256]{1,0:T(8,128)(2,1)S(1)}, bf16[1024,256]{1,0:T(8,128)(2,1)}, u32[]{:S(2)}, u32[]{:S(2)}) collective-permute-start(bf16[1024,256]{1,0:T(8,128)(2,1)S(1)} %pad_maximum_fusion.1), channel_id=1, source_target_pairs={{0,96},{16,112},{32,0},{48,16},{64,32},{80,48},{96,64},{112,80},{1... | collective-permute-start | bytes 1572872 | tf_op jit(solution)/shard_map/ppermute | solution.py:35
  88.7 2.9 %collective-permute-start.12 = (bf16[1024,256]{1,0:T(8,128)(2,1)S(1)}, bf16[1024,256]{1,0:T(8,128)(2,1)}, u32[]{:S(2)}, u32[]{:S(2)}) collective-permute-start(bf16[1024,256]{1,0:T(8,128)(2,1)S(1)} %pad_maximum_fusion.1), channel_id=1, source_target_pairs={{0,64},{16,80},{32,96},{48,112},{64,0},{80,16},{96,32},{112,48},{1... | collective-permute-start | bytes 1572872 | tf_op jit(solution)/shard_map/ppermute | solution.py:35
  91.6 1.2 fusion.40
  92.8 3.9 %collective-permute-done.13 = bf16[8,128,256]{2,1,0:T(8,128)(2,1)} collective-permute-done((bf16[8,128,256]{2,1,0:T(8,128)(2,1)}, bf16[8,128,256]{2,1,0:T(8,128)(2,1)}, u32[]{:S(2)}, u32[]{:S(2)}) %collective-permute-start.13) | collective-permute-done | bytes 524320 | tf_op jit(solution)/shard_map/ppermute | solution.py:35
  96.7 9.5 %collective-permute-done.14 = bf16[8,128,256]{2,1,0:T(8,128)(2,1)} collective-permute-done((bf16[8,128,256]{2,1,0:T(8,128)(2,1)S(1)}, bf16[8,128,256]{2,1,0:T(8,128)(2,1)}, u32[]{:S(2)}, u32[]{:S(2)}) %collective-permute-start.14) | collective-permute-done | bytes 524320 | tf_op jit(solution)/shard_map/ppermute | solution.py:35
  106.2 2.8 %collective-permute-done.11 = bf16[1024,256]{1,0:T(8,128)(2,1)} collective-permute-done((bf16[1024,256]{1,0:T(8,128)(2,1)S(1)}, bf16[1024,256]{1,0:T(8,128)(2,1)}, u32[]{:S(2)}, u32[]{:S(2)}) %collective-permute-start.11) | collective-permute-done | bytes 524320 | tf_op jit(solution)/shard_map/ppermute | solution.py:35
  109.1 1.9 collective-permute-done.12
  111.0 1.5 convert_add_fusion
  112.9 2.5 %collective-permute-start.16 = (bf16[512,256]{1,0:T(8,128)(2,1)S(1)}, bf16[512,256]{1,0:T(8,128)(2,1)S(1)}, u32[]{:S(2)}, u32[]{:S(2)}) collective-permute-start(bf16[512,256]{1,0:T(8,128)(2,1)S(1)} %get-tuple-element.89), channel_id=1, source_target_pairs={{0,32},{16,48},{32,64},{48,80},{64,96},{80,112},{96,0},{112,16},{1... | collective-permute-start | bytes 786440 | tf_op jit(solution)/shard_map/ppermute | solution.py:35
  116.5 11.8 %neighbour_sum_two.1 = (f32[32,128,256]{2,1,0:T(8,128)S(1)}, bf16[32,128,256]{2,1,0:T(8,128)(2,1)S(1)}) custom-call(s32[448]{0:T(512)S(1)} %get-tuple-element.102.refs_0_, s32[448]{0:T(512)S(1)} %get-tuple-element.101.refs_1_, s32[1]{0:T(128)} %bitcast.3.refs_2_, bf16[8,128,256]{2,1,0:T(8,128)(2,1)S(1)} %bitcast.101, bf16[8,128,256]{2,1,0:T(8,128)(2,1)} %bitcast.16.refs_4_, ...), custom_call_target="tpu_custom_call" | custom-call | flops 17999998976 | bytes 20971520 | tf_op jit(solution)/shard_map/neighbour_sum_two/pallas_call | solution.py:132
  132.6 2.1 %collective-permute-done.22 = f32[384,256]{1,0:T(8,128)} collective-permute-done((f32[384,256]{1,0:T(8,128)}, f32[384,256]{1,0:T(8,128)}, u32[]{:S(2)}, u32[]{:S(2)}) %collective-permute-start.22) | collective-permute-done | bytes 393248 | tf_op jit(solution)/shard_map/ppermute | solution.py:39
  135.8 1.7 collective-permute-start.23
  137.5 5.5 %collective-permute-start.24 = (f32[96,256]{1,0:T(8,128)S(1)}, f32[96,256]{1,0:T(8,128)S(1)}, u32[]{:S(2)}, u32[]{:S(2)}) collective-permute-start(f32[96,256]{1,0:T(8,128)S(1)} %get-tuple-element.98), channel_id=1, source_target_pairs={{0,2},{1,3},{2,4},{3,5},{4,6},{5,7},{6,0},{7,1},{8,10},{9,11},{10,... | collective-permute-start | bytes 294920 | tf_op jit(solution)/shard_map/ppermute | solution.py:39
  143.0 3.5 %add_convert_fusion = (bf16[8,128,256]{2,1,0:T(8,128)(2,1)S(1)}, bf16[8,128,256]{2,1,0:T(8,128)(2,1)S(1)}, bf16[8,128,256]{2,1,0:T(8,128)(2,1)S(1)}, f32[8,128,256]{2,1,0:T(8,128)S(1)}) fusion(f32[32,128,256]{2,1,0:T(8,128)} %copy-done.1, bf16[32,128,256]{2,1,0:T(8,128)(2,1)} %collective-permute-done.18), kind=kLoop, calls=%fused_computation.11 | loop fusion | flops 2883584 | bytes 8912896 | tf_op jit(solution)/shard_map/convert_element_type | solution.py:162
  146.5 2.1 %collective-permute-start.19 = (bf16[1024,256]{1,0:T(8,128)(2,1)S(1)}, bf16[1024,256]{1,0:T(8,128)(2,1)S(1)}, u32[]{:S(2)}, u32[]{:S(2)}) collective-permute-start(bf16[1024,256]{1,0:T(8,128)(2,1)S(1)} %bitcast.117), channel_id=1, source_target_pairs={{0,4},{1,5},{2,6},{3,7},{4,0},{5,1},{6,2},{7,3},{8,12},{9,13},{10,... | collective-permute-start | bytes 1572872 | tf_op jit(solution)/shard_map/ppermute | solution.py:39
  148.7 3.2 %collective-permute-start.21 = (bf16[1024,256]{1,0:T(8,128)(2,1)S(1)}, bf16[1024,256]{1,0:T(8,128)(2,1)S(1)}, u32[]{:S(2)}, u32[]{:S(2)}) collective-permute-start(bf16[1024,256]{1,0:T(8,128)(2,1)S(1)} %bitcast.115), channel_id=1, source_target_pairs={{0,6},{1,7},{2,0},{3,1},{4,2},{5,3},{6,4},{7,5},{8,14},{9,15},{10,... | collective-permute-start | bytes 1572872 | tf_op jit(solution)/shard_map/ppermute | solution.py:39
  151.9 2.6 %collective-permute-start.26 = (f32[96,256]{1,0:T(8,128)S(1)}, f32[96,256]{1,0:T(8,128)S(1)}, u32[]{:S(2)}, u32[]{:S(2)}) collective-permute-start(f32[96,256]{1,0:T(8,128)S(1)} %fusion.14), channel_id=1, source_target_pairs={{0,64},{16,80},{32,96},{48,112},{64,0},{80,16},{96,32},{112,48},{1... | collective-permute-start | bytes 294920 | tf_op jit(solution)/shard_map/ppermute | solution.py:35
  154.6 4.5 %collective-permute-done.26 = f32[96,256]{1,0:T(8,128)S(1)} collective-permute-done((f32[96,256]{1,0:T(8,128)S(1)}, f32[96,256]{1,0:T(8,128)S(1)}, u32[]{:S(2)}, u32[]{:S(2)}) %collective-permute-start.26) | collective-permute-done | bytes 98336 | tf_op jit(solution)/shard_map/ppermute | solution.py:35
  160.4 3.3 %collective-permute-done.28 = f32[96,256]{1,0:T(8,128)S(1)} collective-permute-done((f32[96,256]{1,0:T(8,128)S(1)}, f32[96,256]{1,0:T(8,128)S(1)}, u32[]{:S(2)}, u32[]{:S(2)}) %collective-permute-start.28) | collective-permute-done | bytes 98336 | tf_op jit(solution)/shard_map/ppermute | solution.py:35
  163.7 9.0 %collective-permute-done.20 = bf16[1024,256]{1,0:T(8,128)(2,1)S(1)} collective-permute-done((bf16[1024,256]{1,0:T(8,128)(2,1)S(1)}, bf16[1024,256]{1,0:T(8,128)(2,1)S(1)}, u32[]{:S(2)}, u32[]{:S(2)}) %collective-permute-start.20) | collective-permute-done | bytes 524320 | tf_op jit(solution)/shard_map/ppermute | solution.py:39
  172.7 4.6 %collective-permute-start.30 = (f32[96,256]{1,0:T(8,128)S(1)}, f32[96,256]{1,0:T(8,128)S(1)}, u32[]{:S(2)}, u32[]{:S(2)}) collective-permute-start(f32[96,256]{1,0:T(8,128)S(1)} %add_add_fusion.1), channel_id=1, source_target_pairs={{0,16},{16,0},{32,48},{48,32},{64,80},{80,64},{96,112},{112,96},{1... | collective-permute-start | bytes 294920 | tf_op jit(solution)/shard_map/ppermute | solution.py:35
  177.3 2.1 %collective-permute-start.32 = (f32[96,256]{1,0:T(8,128)S(1)}, f32[96,256]{1,0:T(8,128)}, u32[]{:S(2)}, u32[]{:S(2)}) collective-permute-start(f32[96,256]{1,0:T(8,128)S(1)} %add_add_fusion.1), channel_id=1, source_target_pairs={{0,24},{1,25},{2,26},{3,27},{4,28},{5,29},{6,30},{7,31},{8,16},{9,... | collective-permute-start | bytes 294920 | tf_op jit(solution)/shard_map/ppermute | solution.py:31
  180.4 1.6 collective-permute-done.31
  182.0 1.2 collective-permute-done.32
  184.6 2.0 collective-permute-start.34
  186.6 1.3 collective-permute-start.35
  188.1 1.8 collective-permute-start.29
  192.5 3.1 %collective-permute-done.29 = bf16[512,256]{1,0:T(8,128)(2,1)S(1)} collective-permute-done((bf16[512,256]{1,0:T(8,128)(2,1)S(1)}, bf16[512,256]{1,0:T(8,128)(2,1)S(1)}, u32[]{:S(2)}, u32[]{:S(2)}) %collective-permute-start.29) | collective-permute-done | bytes 262176 | tf_op jit(solution)/shard_map/ppermute | solution.py:39
  (110 shorter events, 21.7 us)
Async XLA Ops:
  7.2 122.1 %copy-start = (bf16[256,256]{1,0:T(8,128)(2,1)S(1)}, bf16[256,256]{1,0:T(8,128)(2,1)}, u32[]{:S(2)}) copy-start(bf16[256,256]{1,0:T(8,128)(2,1)} %param.14) | copy-start | bytes 393220
  7.2 43.5 %all-gather.2.cloned.1.call-start = ((), (), s32[]{:S(2)}) async-start(), calls=%async_computation | async-start | bytes 4456448 | tf_op jit(solution)/shard_map/all_gather | solution.py:263
  7.9 7.7 %collective-permute-start = (bf16[512,128]{1,0:T(8,128)(2,1)}, bf16[512,128]{1,0:T(8,128)(2,1)S(1)}, u32[]{:S(2)}, u32[]{:S(2)}) collective-permute-start(bf16[512,128]{1,0:T(8,128)(2,1)} %param.10), channel_id=1, source_target_pairs={{0,16},{16,0},{32,48},{48,32},{64,80},{80,64},{96,112},{112,96},{1... | collective-permute-start | bytes 393224 | tf_op jit(solution)/shard_map/ppermute | solution.py:35
  15.7 9.4 %collective-permute-start.1 = (bf16[1024,128]{1,0:T(8,128)(2,1)S(1)}, bf16[1024,128]{1,0:T(8,128)(2,1)S(1)}, u32[]{:S(2)}, u32[]{:S(2)}) collective-permute-start(bf16[1024,128]{1,0:T(8,128)(2,1)S(1)} %constant_dynamic-update-slice_fusion), channel_id=1, source_target_pairs={{0,32},{16,48},{32,64},{48,80},{64,96},{80,112},{96,0},{112,16},{1... | collective-permute-start | bytes 786440 | tf_op jit(solution)/shard_map/ppermute | solution.py:35
  17.3 12.2 %collective-permute-start.2 = (bf16[1024,128]{1,0:T(8,128)(2,1)S(1)}, bf16[1024,128]{1,0:T(8,128)(2,1)S(1)}, u32[]{:S(2)}, u32[]{:S(2)}) collective-permute-start(bf16[1024,128]{1,0:T(8,128)(2,1)S(1)} %constant_dynamic-update-slice_fusion), channel_id=1, source_target_pairs={{0,96},{16,112},{32,0},{48,16},{64,32},{80,48},{96,64},{112,80},{1... | collective-permute-start | bytes 786440 | tf_op jit(solution)/shard_map/ppermute | solution.py:35
  19.0 12.3 %collective-permute-start.3 = (bf16[1024,128]{1,0:T(8,128)(2,1)S(1)}, bf16[1024,128]{1,0:T(8,128)(2,1)S(1)}, u32[]{:S(2)}, u32[]{:S(2)}) collective-permute-start(bf16[1024,128]{1,0:T(8,128)(2,1)S(1)} %constant_dynamic-update-slice_fusion), channel_id=1, source_target_pairs={{0,64},{16,80},{32,96},{48,112},{64,0},{80,16},{96,32},{112,48},{1... | collective-permute-start | bytes 786440 | tf_op jit(solution)/shard_map/ppermute | solution.py:35
  39.4 2.7 %collective-permute-start.4 = (bf16[32,128,128]{2,1,0:T(8,128)(2,1)S(1)}, bf16[32,128,128]{2,1,0:T(8,128)(2,1)S(1)}, u32[]{:S(2)}, u32[]{:S(2)}) collective-permute-start(bf16[32,128,128]{2,1,0:T(8,128)(2,1)S(1)} %get-tuple-element.38), channel_id=1, source_target_pairs={{0,1},{1,0},{2,3},{3,2},{4,5},{5,4},{6,7},{7,6},{8,9},{9,8},{10,11... | collective-permute-start | bytes 3145736 | tf_op jit(solution)/shard_map/ppermute | solution.py:39
  42.2 10.5 %copy-start.2 = (s32[1,1,448]{2,1,0:T(1,128)S(1)}, s32[1,1,448]{2,1,0:T(1,128)}, u32[]{:S(2)}) copy-start(s32[1,1,448]{2,1,0:T(1,128)} %param.16) | copy-start | bytes 5380
  43.4 23.1 %collective-permute-start.5 = (bf16[1024,128]{1,0:T(8,128)(2,1)}, bf16[1024,128]{1,0:T(8,128)(2,1)}, u32[]{:S(2)}, u32[]{:S(2)}) collective-permute-start(bf16[1024,128]{1,0:T(8,128)(2,1)} %bitcast.10), channel_id=1, source_target_pairs={{0,4},{1,5},{2,6},{3,7},{4,0},{5,1},{6,2},{7,3},{8,12},{9,13},{10,... | collective-permute-start | bytes 786440 | tf_op jit(solution)/shard_map/ppermute | solution.py:39
  43.4 23.1 %collective-permute-start.6 = (bf16[1024,128]{1,0:T(8,128)(2,1)}, bf16[1024,128]{1,0:T(8,128)(2,1)}, u32[]{:S(2)}, u32[]{:S(2)}) collective-permute-start(bf16[1024,128]{1,0:T(8,128)(2,1)} %bitcast.11), channel_id=1, source_target_pairs={{0,2},{1,3},{2,4},{3,5},{4,6},{5,7},{6,0},{7,1},{8,10},{9,11},{10,... | collective-permute-start | bytes 786440 | tf_op jit(solution)/shard_map/ppermute | solution.py:39
  50.6 15.9 %collective-permute-start.7 = (bf16[1024,128]{1,0:T(8,128)(2,1)}, bf16[1024,128]{1,0:T(8,128)(2,1)S(1)}, u32[]{:S(2)}, u32[]{:S(2)}) collective-permute-start(bf16[1024,128]{1,0:T(8,128)(2,1)} %bitcast.12), channel_id=1, source_target_pairs={{0,6},{1,7},{2,0},{3,1},{4,2},{5,3},{6,4},{7,5},{8,14},{9,15},{10,... | collective-permute-start | bytes 786440 | tf_op jit(solution)/shard_map/ppermute | solution.py:39
  52.6 2.2 %copy-start.3 = (bf16[8192,256]{1,0:T(8,128)(2,1)S(1)}, bf16[8192,256]{1,0:T(8,128)(2,1)}, u32[]{:S(2)}) copy-start(bf16[8192,256]{1,0:T(8,128)(2,1)} %all-gather.2.cloned.1.call-done) | copy-start | bytes 12582916
  54.8 11.7 %copy-start.4 = (f32[8,128,128]{2,1,0:T(8,128)S(1)}, f32[8,128,128]{2,1,0:T(8,128)}, u32[]{:S(2)}) copy-start(f32[8,128,128]{2,1,0:T(8,128)} %get-tuple-element.86) | copy-start | bytes 1572868
  66.5 6.9 %copy-start.14 = (bf16[128,256]{1,0:T(8,128)(2,1)S(1)}, bf16[128,256]{1,0:T(8,128)(2,1)}, u32[]{:S(2)}) copy-start(bf16[128,256]{1,0:T(8,128)(2,1)} %param.13) | copy-start | bytes 196612
  67.7 10.5 %copy-start.5 = (f32[1024,128]{1,0:T(8,128)}, f32[1024,128]{1,0:T(8,128)S(1)}, u32[]{:S(2)}) copy-start(f32[1024,128]{1,0:T(8,128)S(1)} %fusion.8) | copy-start | bytes 1572868
  67.8 5.6 %collective-permute-start.8 = (bf16[512,128]{1,0:T(8,128)(2,1)S(1)}, bf16[512,128]{1,0:T(8,128)(2,1)S(1)}, u32[]{:S(2)}, u32[]{:S(2)}) collective-permute-start(bf16[512,128]{1,0:T(8,128)(2,1)S(1)} %slice.168), channel_id=1, source_target_pairs={{0,8},{1,9},{2,10},{3,11},{4,12},{5,13},{6,14},{7,15},{8,0},{9,1},... | collective-permute-start | bytes 393224 | tf_op jit(solution)/shard_map/ppermute | solution.py:39
  73.4 4.8 %copy-start.11 = (bf16[512,128]{1,0:T(8,128)(2,1)}, bf16[512,128]{1,0:T(8,128)(2,1)S(1)}, u32[]{:S(2)}) copy-start(bf16[512,128]{1,0:T(8,128)(2,1)S(1)} %collective-permute-done.8) | copy-start | bytes 393220
  74.6 10.7 %collective-permute-start.9 = (bf16[512,256]{1,0:T(8,128)(2,1)S(1)}, bf16[512,256]{1,0:T(8,128)(2,1)S(1)}, u32[]{:S(2)}, u32[]{:S(2)}) collective-permute-start(bf16[512,256]{1,0:T(8,128)(2,1)S(1)} %get-tuple-element.99), channel_id=1, source_target_pairs={{0,16},{16,0},{32,48},{48,32},{64,80},{80,64},{96,112},{112,96},{1... | collective-permute-start | bytes 786440 | tf_op jit(solution)/shard_map/ppermute | solution.py:35
  74.6 22.1 %collective-permute-start.13 = (bf16[8,128,256]{2,1,0:T(8,128)(2,1)}, bf16[8,128,256]{2,1,0:T(8,128)(2,1)}, u32[]{:S(2)}, u32[]{:S(2)}) collective-permute-start(bf16[8,128,256]{2,1,0:T(8,128)(2,1)} %get-tuple-element.46), channel_id=1, source_target_pairs={{0,16},{16,0},{32,48},{48,32},{64,80},{80,64},{96,112},{112,96},{1... | collective-permute-start | bytes 1572872 | tf_op jit(solution)/shard_map/ppermute | solution.py:35
  78.2 28.1 %collective-permute-start.14 = (bf16[8,128,256]{2,1,0:T(8,128)(2,1)S(1)}, bf16[8,128,256]{2,1,0:T(8,128)(2,1)}, u32[]{:S(2)}, u32[]{:S(2)}) collective-permute-start(bf16[8,128,256]{2,1,0:T(8,128)(2,1)S(1)} %get-tuple-element.47), channel_id=1, source_target_pairs={{0,16},{16,0},{32,48},{48,32},{64,80},{80,64},{96,112},{112,96},{1... | collective-permute-start | bytes 1572872 | tf_op jit(solution)/shard_map/ppermute | solution.py:35
  85.4 20.8 %collective-permute-start.10 = (bf16[1024,256]{1,0:T(8,128)(2,1)S(1)}, bf16[1024,256]{1,0:T(8,128)(2,1)}, u32[]{:S(2)}, u32[]{:S(2)}) collective-permute-start(bf16[1024,256]{1,0:T(8,128)(2,1)S(1)} %pad_maximum_fusion.1), channel_id=1, source_target_pairs={{0,32},{16,48},{32,64},{48,80},{64,96},{80,112},{96,0},{112,16},{1... | collective-permute-start | bytes 1572872 | tf_op jit(solution)/shard_map/ppermute | solution.py:35
  86.2 22.8 %collective-permute-start.11 = (bf16[1024,256]{1,0:T(8,128)(2,1)S(1)}, bf16[1024,256]{1,0:T(8,128)(2,1)}, u32[]{:S(2)}, u32[]{:S(2)}) collective-permute-start(bf16[1024,256]{1,0:T(8,128)(2,1)S(1)} %pad_maximum_fusion.1), channel_id=1, source_target_pairs={{0,96},{16,112},{32,0},{48,16},{64,32},{80,48},{96,64},{112,80},{1... | collective-permute-start | bytes 1572872 | tf_op jit(solution)/shard_map/ppermute | solution.py:35
  88.7 22.2 %collective-permute-start.12 = (bf16[1024,256]{1,0:T(8,128)(2,1)S(1)}, bf16[1024,256]{1,0:T(8,128)(2,1)}, u32[]{:S(2)}, u32[]{:S(2)}) collective-permute-start(bf16[1024,256]{1,0:T(8,128)(2,1)S(1)} %pad_maximum_fusion.1), channel_id=1, source_target_pairs={{0,64},{16,80},{32,96},{48,112},{64,0},{80,16},{96,32},{112,48},{1... | collective-permute-start | bytes 1572872 | tf_op jit(solution)/shard_map/ppermute | solution.py:35
  112.6 15.8 %collective-permute-start.15 = (bf16[512,256]{1,0:T(8,128)(2,1)S(1)}, bf16[512,256]{1,0:T(8,128)(2,1)S(1)}, u32[]{:S(2)}, u32[]{:S(2)}) collective-permute-start(bf16[512,256]{1,0:T(8,128)(2,1)S(1)} %get-tuple-element.87), channel_id=1, source_target_pairs={{0,64},{16,80},{32,96},{48,112},{64,0},{80,16},{96,32},{112,48},{1... | collective-permute-start | bytes 786440 | tf_op jit(solution)/shard_map/ppermute | solution.py:35
  112.9 15.5 %collective-permute-start.16 = (bf16[512,256]{1,0:T(8,128)(2,1)S(1)}, bf16[512,256]{1,0:T(8,128)(2,1)S(1)}, u32[]{:S(2)}, u32[]{:S(2)}) collective-permute-start(bf16[512,256]{1,0:T(8,128)(2,1)S(1)} %get-tuple-element.89), channel_id=1, source_target_pairs={{0,32},{16,48},{32,64},{48,80},{64,96},{80,112},{96,0},{112,16},{1... | collective-permute-start | bytes 786440 | tf_op jit(solution)/shard_map/ppermute | solution.py:35
  115.4 13.0 %collective-permute-start.17 = (bf16[512,256]{1,0:T(8,128)(2,1)S(1)}, bf16[512,256]{1,0:T(8,128)(2,1)S(1)}, u32[]{:S(2)}, u32[]{:S(2)}) collective-permute-start(bf16[512,256]{1,0:T(8,128)(2,1)S(1)} %get-tuple-element.88), channel_id=1, source_target_pairs={{0,96},{16,112},{32,0},{48,16},{64,32},{80,48},{96,64},{112,80},{1... | collective-permute-start | bytes 786440 | tf_op jit(solution)/shard_map/ppermute | solution.py:35
  116.5 12.3 %copy-start.10 = (bf16[256,256]{1,0:T(8,128)(2,1)S(1)}, bf16[256,256]{1,0:T(8,128)(2,1)}, u32[]{:S(2)}) copy-start(bf16[256,256]{1,0:T(8,128)(2,1)} %param.15) | copy-start | bytes 393220
  128.3 2.0 copy-start.1
  128.5 1.9 copy-start.8
  128.5 14.5 %collective-permute-start.18 = (bf16[32,128,256]{2,1,0:T(8,128)(2,1)S(1)}, bf16[32,128,256]{2,1,0:T(8,128)(2,1)}, u32[]{:S(2)}, u32[]{:S(2)}) collective-permute-start(bf16[32,128,256]{2,1,0:T(8,128)(2,1)S(1)} %get-tuple-element.63), channel_id=1, source_target_pairs={{0,1},{1,0},{2,3},{3,2},{4,5},{5,4},{6,7},{7,6},{8,9},{9,8},{10,11... | collective-permute-start | bytes 6291464 | tf_op jit(solution)/shard_map/ppermute | solution.py:39
  132.6 2.1 %collective-permute-start.22 = (f32[384,256]{1,0:T(8,128)}, f32[384,256]{1,0:T(8,128)}, u32[]{:S(2)}, u32[]{:S(2)}) collective-permute-start(f32[384,256]{1,0:T(8,128)} %dynamic-slice_bitcast_fusion), channel_id=1, source_target_pairs={{0,1},{1,0},{2,3},{3,2},{4,5},{5,4},{6,7},{7,6},{8,9},{9,8},{10,11... | collective-permute-start | bytes 1179656 | tf_op jit(solution)/shard_map/ppermute | solution.py:39
  135.8 12.9 %collective-permute-start.23 = (f32[96,256]{1,0:T(8,128)S(1)}, f32[96,256]{1,0:T(8,128)S(1)}, u32[]{:S(2)}, u32[]{:S(2)}) collective-permute-start(f32[96,256]{1,0:T(8,128)S(1)} %get-tuple-element.96), channel_id=1, source_target_pairs={{0,4},{1,5},{2,6},{3,7},{4,0},{5,1},{6,2},{7,3},{8,12},{9,13},{10,... | collective-permute-start | bytes 294920 | tf_op jit(solution)/shard_map/ppermute | solution.py:39
  137.5 14.4 %collective-permute-start.24 = (f32[96,256]{1,0:T(8,128)S(1)}, f32[96,256]{1,0:T(8,128)S(1)}, u32[]{:S(2)}, u32[]{:S(2)}) collective-permute-start(f32[96,256]{1,0:T(8,128)S(1)} %get-tuple-element.98), channel_id=1, source_target_pairs={{0,2},{1,3},{2,4},{3,5},{4,6},{5,7},{6,0},{7,1},{8,10},{9,11},{10,... | collective-permute-start | bytes 294920 | tf_op jit(solution)/shard_map/ppermute | solution.py:39
  143.0 8.9 %collective-permute-start.25 = (f32[96,256]{1,0:T(8,128)S(1)}, f32[96,256]{1,0:T(8,128)S(1)}, u32[]{:S(2)}, u32[]{:S(2)}) collective-permute-start(f32[96,256]{1,0:T(8,128)S(1)} %get-tuple-element.97), channel_id=1, source_target_pairs={{0,6},{1,7},{2,0},{3,1},{4,2},{5,3},{6,4},{7,5},{8,14},{9,15},{10,... | collective-permute-start | bytes 294920 | tf_op jit(solution)/shard_map/ppermute | solution.py:39
  146.5 17.2 %collective-permute-start.19 = (bf16[1024,256]{1,0:T(8,128)(2,1)S(1)}, bf16[1024,256]{1,0:T(8,128)(2,1)S(1)}, u32[]{:S(2)}, u32[]{:S(2)}) collective-permute-start(bf16[1024,256]{1,0:T(8,128)(2,1)S(1)} %bitcast.117), channel_id=1, source_target_pairs={{0,4},{1,5},{2,6},{3,7},{4,0},{5,1},{6,2},{7,3},{8,12},{9,13},{10,... | collective-permute-start | bytes 1572872 | tf_op jit(solution)/shard_map/ppermute | solution.py:39
  148.6 24.1 %collective-permute-start.20 = (bf16[1024,256]{1,0:T(8,128)(2,1)S(1)}, bf16[1024,256]{1,0:T(8,128)(2,1)S(1)}, u32[]{:S(2)}, u32[]{:S(2)}) collective-permute-start(bf16[1024,256]{1,0:T(8,128)(2,1)S(1)} %bitcast.116), channel_id=1, source_target_pairs={{0,2},{1,3},{2,4},{3,5},{4,6},{5,7},{6,0},{7,1},{8,10},{9,11},{10,... | collective-permute-start | bytes 1572872 | tf_op jit(solution)/shard_map/ppermute | solution.py:39
  148.7 24.0 %collective-permute-start.21 = (bf16[1024,256]{1,0:T(8,128)(2,1)S(1)}, bf16[1024,256]{1,0:T(8,128)(2,1)S(1)}, u32[]{:S(2)}, u32[]{:S(2)}) collective-permute-start(bf16[1024,256]{1,0:T(8,128)(2,1)S(1)} %bitcast.115), channel_id=1, source_target_pairs={{0,6},{1,7},{2,0},{3,1},{4,2},{5,3},{6,4},{7,5},{8,14},{9,15},{10,... | collective-permute-start | bytes 1572872 | tf_op jit(solution)/shard_map/ppermute | solution.py:39
  151.9 7.2 %collective-permute-start.26 = (f32[96,256]{1,0:T(8,128)S(1)}, f32[96,256]{1,0:T(8,128)S(1)}, u32[]{:S(2)}, u32[]{:S(2)}) collective-permute-start(f32[96,256]{1,0:T(8,128)S(1)} %fusion.14), channel_id=1, source_target_pairs={{0,64},{16,80},{32,96},{48,112},{64,0},{80,16},{96,32},{112,48},{1... | collective-permute-start | bytes 294920 | tf_op jit(solution)/shard_map/ppermute | solution.py:35
  154.5 5.8 %collective-permute-start.27 = (f32[96,256]{1,0:T(8,128)S(1)}, f32[96,256]{1,0:T(8,128)S(1)}, u32[]{:S(2)}, u32[]{:S(2)}) collective-permute-start(f32[96,256]{1,0:T(8,128)S(1)} %fusion.14), channel_id=1, source_target_pairs={{0,32},{16,48},{32,64},{48,80},{64,96},{80,112},{96,0},{112,16},{1... | collective-permute-start | bytes 294920 | tf_op jit(solution)/shard_map/ppermute | solution.py:35
  159.1 4.6 %collective-permute-start.28 = (f32[96,256]{1,0:T(8,128)S(1)}, f32[96,256]{1,0:T(8,128)S(1)}, u32[]{:S(2)}, u32[]{:S(2)}) collective-permute-start(f32[96,256]{1,0:T(8,128)S(1)} %fusion.14), channel_id=1, source_target_pairs={{0,96},{16,112},{32,0},{48,16},{64,32},{80,48},{96,64},{112,80},{1... | collective-permute-start | bytes 294920 | tf_op jit(solution)/shard_map/ppermute | solution.py:35
  172.7 7.7 %collective-permute-start.30 = (f32[96,256]{1,0:T(8,128)S(1)}, f32[96,256]{1,0:T(8,128)S(1)}, u32[]{:S(2)}, u32[]{:S(2)}) collective-permute-start(f32[96,256]{1,0:T(8,128)S(1)} %add_add_fusion.1), channel_id=1, source_target_pairs={{0,16},{16,0},{32,48},{48,32},{64,80},{80,64},{96,112},{112,96},{1... | collective-permute-start | bytes 294920 | tf_op jit(solution)/shard_map/ppermute | solution.py:35
  177.3 4.7 %collective-permute-start.31 = (f32[96,256]{1,0:T(8,128)S(1)}, f32[96,256]{1,0:T(8,128)}, u32[]{:S(2)}, u32[]{:S(2)}) collective-permute-start(f32[96,256]{1,0:T(8,128)S(1)} %add_add_fusion.1), channel_id=1, source_target_pairs={{0,8},{1,9},{2,10},{3,11},{4,12},{5,13},{6,14},{7,15},{8,0},{9,1},... | collective-permute-start | bytes 294920 | tf_op jit(solution)/shard_map/ppermute | solution.py:39
  177.3 5.9 %collective-permute-start.32 = (f32[96,256]{1,0:T(8,128)S(1)}, f32[96,256]{1,0:T(8,128)}, u32[]{:S(2)}, u32[]{:S(2)}) collective-permute-start(f32[96,256]{1,0:T(8,128)S(1)} %add_add_fusion.1), channel_id=1, source_target_pairs={{0,24},{1,25},{2,26},{3,27},{4,28},{5,29},{6,30},{7,31},{8,16},{9,... | collective-permute-start | bytes 294920 | tf_op jit(solution)/shard_map/ppermute | solution.py:31
  184.2 6.9 %collective-permute-start.33 = (f32[96,256]{1,0:T(8,128)S(1)}, f32[96,256]{1,0:T(8,128)S(1)}, u32[]{:S(2)}, u32[]{:S(2)}) collective-permute-start(f32[96,256]{1,0:T(8,128)S(1)} %add_add_fusion), channel_id=1, source_target_pairs={{0,2},{1,3},{2,4},{3,5},{4,6},{5,7},{6,0},{7,1},{8,10},{9,11},{10,... | collective-permute-start | bytes 294920 | tf_op jit(solution)/shard_map/ppermute | solution.py:39
  184.6 6.6 %collective-permute-start.34 = (f32[96,256]{1,0:T(8,128)S(1)}, f32[96,256]{1,0:T(8,128)S(1)}, u32[]{:S(2)}, u32[]{:S(2)}) collective-permute-start(f32[96,256]{1,0:T(8,128)S(1)} %add_add_fusion), channel_id=1, source_target_pairs={{0,4},{1,5},{2,6},{3,7},{4,0},{5,1},{6,2},{7,3},{8,12},{9,13},{10,... | collective-permute-start | bytes 294920 | tf_op jit(solution)/shard_map/ppermute | solution.py:39
  186.6 5.5 %collective-permute-start.35 = (f32[96,256]{1,0:T(8,128)S(1)}, f32[96,256]{1,0:T(8,128)S(1)}, u32[]{:S(2)}, u32[]{:S(2)}) collective-permute-start(f32[96,256]{1,0:T(8,128)S(1)} %add_add_fusion), channel_id=1, source_target_pairs={{0,6},{1,7},{2,0},{3,1},{4,2},{5,3},{6,4},{7,5},{8,14},{9,15},{10,... | collective-permute-start | bytes 294920 | tf_op jit(solution)/shard_map/ppermute | solution.py:39
  188.1 7.5 %collective-permute-start.29 = (bf16[512,256]{1,0:T(8,128)(2,1)S(1)}, bf16[512,256]{1,0:T(8,128)(2,1)S(1)}, u32[]{:S(2)}, u32[]{:S(2)}) collective-permute-start(bf16[512,256]{1,0:T(8,128)(2,1)S(1)} %slice.167), channel_id=1, source_target_pairs={{0,8},{1,9},{2,10},{3,11},{4,12},{5,13},{6,14},{7,15},{8,0},{9,1},... | collective-permute-start | bytes 786440 | tf_op jit(solution)/shard_map/ppermute | solution.py:39
  192.2 4.5 %collective-permute-start.36 = (f32[384,256]{1,0:T(8,128)S(1)}, f32[384,256]{1,0:T(8,128)S(1)}, u32[]{:S(2)}, u32[]{:S(2)}) collective-permute-start(f32[384,256]{1,0:T(8,128)S(1)} %pad_maximum_fusion.3), channel_id=1, source_target_pairs={{0,1},{1,0},{2,3},{3,2},{4,5},{5,4},{6,7},{7,6},{8,9},{9,8},{10,11... | collective-permute-start | bytes 1179656 | tf_op jit(solution)/shard_map/ppermute | solution.py:39
  (6 other events, 8.9 us)
Sparse Core Ops, SparseCore 0:
  9.7 40.8 all-gather.1

commit v3 on v2

--- a/solution.py
+++ b/solution.py
@@ -41,7 +41,7 @@
 
 def gather_row(value):
     pair = jnp.concatenate([value, send_row(value, 0, 1)])
-    far, below, above = [send_row(pair, dy, 0) for dy in (2, 1, 3)]
+    below, above, far = [send_row(pair, dy, 0) for dy in (1, 3, 2)]
     return [pair, below, above, far]
 
 
@@ -159,11 +159,11 @@
     def part(d):
         return (own[8 * d : 8 * d + 8] + other[8 * d : 8 * d + 8].astype(F32)).reshape(-1, width)
 
-    return part(0), [part(d).astype(BF) for d in (2, 1, 3)]
+    return part(0), [part(d).astype(BF) for d in (1, 3, 2)]
 
 
 def send_x(parts):
-    return [send_col(part, d, 0) for part, d in zip(parts, (2, 1, 3))]
+    return [send_col(part, d, 0) for part, d in zip(parts, (1, 3, 2))]
 
 
 def add_x(own, sent):
@@ -181,7 +181,7 @@
 
 
 def sum_y(parts):
-    sent = [send_row(parts[d].astype(BF), d, 0) for d in (2, 1, 3)]
+    sent = [send_row(parts[d].astype(BF), d, 0) for d in (1, 3, 2)]
     return parts[0] + sent[0].astype(F32) + sent[1].astype(F32) + sent[2].astype(F32)
 
 

time: 206 us -> 202 us (0.981)
  starting transfers between devices: 56.9 us -> 73.5 us
  Pallas kernels: 31.5 us -> 19.2 us
  waiting for transfers between devices: 77.4 us -> 69 us
    pallas_call x3, Pallas kernels: 31.5 us -> 19.2 us  [tile_product(): pl.pallas_call(functools.partial(tile_kernel, transpose, len(pieces), spl...]
    ppermute x19, starting transfers between devices: 23.7 us -> 33 us  [send_col(): return lax.ppermute(value, 'col', col_perm(dx, dz, dc))]
    ppermute x17, starting transfers between devices: 31 us -> 39.2 us  [send_row(): return lax.ppermute(value, 'row', row_perm(dy, dz))]
    ppermute x17, waiting for transfers between devices: 45.6 us -> 39.6 us  [send_row(): return lax.ppermute(value, 'row', row_perm(dy, dz))]
    ppermute x19, waiting for transfers between devices: 25.8 us -> 23.5 us  [send_col(): return lax.ppermute(value, 'col', col_perm(dx, dz, dc))]
  transfers between devices with their start and end apart: 38 -> 38, of which waited for: 23 -> 26; matrix products, arithmetic and copies ran while one was open for 7% -> 7% of each run, Pallas kernels for 15% -> 10%
where the time goes in v3:
time: 202 us; the launch traced here: 201 us
  starting transfers between devices  73.5 us (36%)
  waiting for transfers between devices  69 us (34%)
  Pallas kernels  19.2 us (10%)
  between operations  15.3 us (8%)
  other arithmetic  11.5 us (6%)
  local copies, waits for them, and re-layouts  6.25 us (3%)
  matrix products  5.85 us (3%)
    ppermute x17, waiting for transfers between devices, send_row(): return lax.ppermute(value, 'row', row_perm(dy, dz))  39.6 us
    ppermute x17, starting transfers between devices, send_row(): return lax.ppermute(value, 'row', row_perm(dy, dz))  39.2 us
    ppermute x19, starting transfers between devices, send_col(): return lax.ppermute(value, 'col', col_perm(dx, dz, dc))  33 us
    ppermute x19, waiting for transfers between devices, send_col(): return lax.ppermute(value, 'col', col_perm(dx, dz, dc))  23.5 us
    pallas_call x3, Pallas kernels, tile_product(): pl.pallas_call(functools.partial(tile_kernel, transpose, len(pieces), spl...  19.2 us
    convert_element_type x2, other arithmetic, add_cores(): return (part(0), [part(d).astype(BF) for d in (1, 3, 2)])  4.65 us
  transfers between devices with their start and end apart: 38, of which 26 were waited for; matrix products, arithmetic and copies ran while one was open for 7% of the time, Pallas kernels for 10%

profile of v3, /device:TPU:0, one launch (start us, length us, event | category | flops | bytes accessed | tf_op | source)
XLA Modules:
  0.0 200.7 jit_solution(3623072732883761851)
XLA Ops:
  7.9 4.0 %collective-permute-start = (bf16[512,128]{1,0:T(8,128)(2,1)}, bf16[512,128]{1,0:T(8,128)(2,1)S(1)}, u32[]{:S(2)}, u32[]{:S(2)}) collective-permute-start(bf16[512,128]{1,0:T(8,128)(2,1)} %param.10), channel_id=1, source_target_pairs={{0,16},{16,0},{32,48},{48,32},{64,80},{80,64},{96,112},{112,96},{1... | collective-permute-start | bytes 393224 | tf_op jit(solution)/shard_map/ppermute | solution.py:35
  13.5 2.1 %collective-permute-done = bf16[512,128]{1,0:T(8,128)(2,1)S(1)} collective-permute-done((bf16[512,128]{1,0:T(8,128)(2,1)}, bf16[512,128]{1,0:T(8,128)(2,1)S(1)}, u32[]{:S(2)}, u32[]{:S(2)}) %collective-permute-start) | collective-permute-done | bytes 131104 | tf_op jit(solution)/shard_map/ppermute | solution.py:35
  15.7 1.6 collective-permute-start.1
  17.3 1.7 collective-permute-start.2
  19.0 2.0 collective-permute-start.3
  22.5 2.6 %collective-permute-done.1 = bf16[1024,128]{1,0:T(8,128)(2,1)S(1)} collective-permute-done((bf16[1024,128]{1,0:T(8,128)(2,1)S(1)}, bf16[1024,128]{1,0:T(8,128)(2,1)S(1)}, u32[]{:S(2)}, u32[]{:S(2)}) %collective-permute-start.1) | collective-permute-done | bytes 262176 | tf_op jit(solution)/shard_map/ppermute | solution.py:35
  25.1 4.4 %collective-permute-done.2 = bf16[1024,128]{1,0:T(8,128)(2,1)S(1)} collective-permute-done((bf16[1024,128]{1,0:T(8,128)(2,1)S(1)}, bf16[1024,128]{1,0:T(8,128)(2,1)S(1)}, u32[]{:S(2)}, u32[]{:S(2)}) %collective-permute-start.2) | collective-permute-done | bytes 262176 | tf_op jit(solution)/shard_map/ppermute | solution.py:35
  29.5 1.8 collective-permute-done.3
  31.3 5.0 %neighbour_sum_one.1 = (f32[32,128,128]{2,1,0:T(8,128)S(1)}, bf16[32,128,128]{2,1,0:T(8,128)(2,1)S(1)}) custom-call(s32[448]{0:T(512)S(1)} %get-tuple-element.102.refs_0_, s32[448]{0:T(512)S(1)} %get-tuple-element.101.refs_1_, s32[1]{0:T(128)} %bitcast.3.refs_2_, bf16[8,128,128]{2,1,0:T(8,128)(2,1)S(1)} %bitcast.102, bf16[8,128,128]{2,1,0:T(8,128)(2,1)S(1)} %bitcast.106, ...), custom_call_target="tpu_custom_call" | custom-call | flops 17999998976 | bytes 20971520 | tf_op jit(solution)/shard_map/neighbour_sum_one/pallas_call | solution.py:132
  36.4 2.6 %collective-permute-done.4 = bf16[32,128,128]{2,1,0:T(8,128)(2,1)S(1)} collective-permute-done((bf16[32,128,128]{2,1,0:T(8,128)(2,1)S(1)}, bf16[32,128,128]{2,1,0:T(8,128)(2,1)S(1)}, u32[]{:S(2)}, u32[]{:S(2)}) %collective-permute-start.4) | collective-permute-done | bytes 1048608 | tf_op jit(solution)/shard_map/ppermute | solution.py:39
  40.2 5.6 %collective-permute-start.5 = (bf16[1024,128]{1,0:T(8,128)(2,1)}, bf16[1024,128]{1,0:T(8,128)(2,1)}, u32[]{:S(2)}, u32[]{:S(2)}) collective-permute-start(bf16[1024,128]{1,0:T(8,128)(2,1)} %bitcast.10), channel_id=1, source_target_pairs={{0,2},{1,3},{2,4},{3,5},{4,6},{5,7},{6,0},{7,1},{8,10},{9,11},{10,... | collective-permute-start | bytes 786440 | tf_op jit(solution)/shard_map/ppermute | solution.py:39
  45.9 3.8 %all-gather.2.cloned.1.call-done = bf16[8192,256]{1,0:T(8,128)(2,1)} async-done(((bf16[512,256]{1,0:T(8,128)(2,1)}), bf16[8192,256]{1,0:T(8,128)(2,1)}) %all-gather.2.cloned.1.call-update) | async-done | bytes 4194320 | tf_op jit(solution)/shard_map/all_gather | solution.py:263
  49.7 3.2 %collective-permute-start.7 = (bf16[1024,128]{1,0:T(8,128)(2,1)}, bf16[1024,128]{1,0:T(8,128)(2,1)S(1)}, u32[]{:S(2)}, u32[]{:S(2)}) collective-permute-start(bf16[1024,128]{1,0:T(8,128)(2,1)} %bitcast.12), channel_id=1, source_target_pairs={{0,4},{1,5},{2,6},{3,7},{4,0},{5,1},{6,2},{7,3},{8,12},{9,13},{10,... | collective-permute-start | bytes 786440 | tf_op jit(solution)/shard_map/ppermute | solution.py:39
  52.9 2.2 %copy-done.3 = bf16[8192,256]{1,0:T(8,128)(2,1)S(1)} copy-done((bf16[8192,256]{1,0:T(8,128)(2,1)S(1)}, bf16[8192,256]{1,0:T(8,128)(2,1)}, u32[]{:S(2)}) %copy-start.3) | copy-done | bytes 4194328
  55.1 6.9 %neighbour_sum_back.1 = (f32[16,128,256]{2,1,0:T(8,128)S(1)}, bf16[8,128,256]{2,1,0:T(8,128)(2,1)}, bf16[8,128,256]{2,1,0:T(8,128)(2,1)S(1)}) custom-call(s32[448]{0:T(512)S(1)} %bitcast.104, s32[448]{0:T(512)S(1)} %get-tuple-element.77.refs_1_, s32[1]{0:T(128)} %bitcast.3.refs_2_, bf16[64,128,256]{2,1,0:T(8,128)(2,1)S(1)} %bitcast.105, ...), custom_call_target="tpu_custom_call" | custom-call | flops 17999998976 | bytes 20971520 | tf_op jit(solution)/shard_map/neighbour_sum_back/pallas_call | solution.py:132
  63.4 3.7 %collective-permute-start.8 = (bf16[512,128]{1,0:T(8,128)(2,1)S(1)}, bf16[512,128]{1,0:T(8,128)(2,1)S(1)}, u32[]{:S(2)}, u32[]{:S(2)}) collective-permute-start(bf16[512,128]{1,0:T(8,128)(2,1)S(1)} %slice.168), channel_id=1, source_target_pairs={{0,8},{1,9},{2,10},{3,11},{4,12},{5,13},{6,14},{7,15},{8,0},{9,1},... | collective-permute-start | bytes 393224 | tf_op jit(solution)/shard_map/ppermute | solution.py:39
  67.3 2.7 %collective-permute-done.8 = bf16[512,128]{1,0:T(8,128)(2,1)S(1)} collective-permute-done((bf16[512,128]{1,0:T(8,128)(2,1)S(1)}, bf16[512,128]{1,0:T(8,128)(2,1)S(1)}, u32[]{:S(2)}, u32[]{:S(2)}) %collective-permute-start.8) | collective-permute-done | bytes 131104 | tf_op jit(solution)/shard_map/ppermute | solution.py:39
  70.1 1.2 fusion.11
  71.3 7.6 %collective-permute-start.9 = (bf16[512,256]{1,0:T(8,128)(2,1)S(1)}, bf16[512,256]{1,0:T(8,128)(2,1)S(1)}, u32[]{:S(2)}, u32[]{:S(2)}) collective-permute-start(bf16[512,256]{1,0:T(8,128)(2,1)S(1)} %get-tuple-element.99), channel_id=1, source_target_pairs={{0,16},{16,0},{32,48},{48,32},{64,80},{80,64},{96,112},{112,96},{1... | collective-permute-start | bytes 786440 | tf_op jit(solution)/shard_map/ppermute | solution.py:35
  78.9 3.5 %collective-permute-start.14 = (bf16[8,128,256]{2,1,0:T(8,128)(2,1)S(1)}, bf16[8,128,256]{2,1,0:T(8,128)(2,1)}, u32[]{:S(2)}, u32[]{:S(2)}) collective-permute-start(bf16[8,128,256]{2,1,0:T(8,128)(2,1)S(1)} %get-tuple-element.47), channel_id=1, source_target_pairs={{0,16},{16,0},{32,48},{48,32},{64,80},{80,64},{96,112},{112,96},{1... | collective-permute-start | bytes 1572872 | tf_op jit(solution)/shard_map/ppermute | solution.py:35
  82.4 3.7 %collective-permute-done.9 = bf16[512,256]{1,0:T(8,128)(2,1)S(1)} collective-permute-done((bf16[512,256]{1,0:T(8,128)(2,1)S(1)}, bf16[512,256]{1,0:T(8,128)(2,1)S(1)}, u32[]{:S(2)}, u32[]{:S(2)}) %collective-permute-start.9) | collective-permute-done | bytes 262176 | tf_op jit(solution)/shard_map/ppermute | solution.py:35
  86.4 3.3 %collective-permute-start.11 = (bf16[1024,256]{1,0:T(8,128)(2,1)S(1)}, bf16[1024,256]{1,0:T(8,128)(2,1)}, u32[]{:S(2)}, u32[]{:S(2)}) collective-permute-start(bf16[1024,256]{1,0:T(8,128)(2,1)S(1)} %pad_maximum_fusion.1), channel_id=1, source_target_pairs={{0,96},{16,112},{32,0},{48,16},{64,32},{80,48},{96,64},{112,80},{1... | collective-permute-start | bytes 1572872 | tf_op jit(solution)/shard_map/ppermute | solution.py:35
  89.8 1.4 collective-permute-start.12
  92.4 5.0 %collective-permute-done.13 = bf16[8,128,256]{2,1,0:T(8,128)(2,1)} collective-permute-done((bf16[8,128,256]{2,1,0:T(8,128)(2,1)}, bf16[8,128,256]{2,1,0:T(8,128)(2,1)}, u32[]{:S(2)}, u32[]{:S(2)}) %collective-permute-start.13) | collective-permute-done | bytes 524320 | tf_op jit(solution)/shard_map/ppermute | solution.py:35
  97.4 7.6 %collective-permute-done.14 = bf16[8,128,256]{2,1,0:T(8,128)(2,1)} collective-permute-done((bf16[8,128,256]{2,1,0:T(8,128)(2,1)S(1)}, bf16[8,128,256]{2,1,0:T(8,128)(2,1)}, u32[]{:S(2)}, u32[]{:S(2)}) %collective-permute-start.14) | collective-permute-done | bytes 524320 | tf_op jit(solution)/shard_map/ppermute | solution.py:35
  105.0 4.3 %collective-permute-done.12 = bf16[1024,256]{1,0:T(8,128)(2,1)} collective-permute-done((bf16[1024,256]{1,0:T(8,128)(2,1)S(1)}, bf16[1024,256]{1,0:T(8,128)(2,1)}, u32[]{:S(2)}, u32[]{:S(2)}) %collective-permute-start.12) | collective-permute-done | bytes 524320 | tf_op jit(solution)/shard_map/ppermute | solution.py:35
  109.3 1.5 convert_add_fusion
  110.9 1.5 collective-permute-start.15
  112.4 1.8 collective-permute-start.16
  114.9 7.3 %neighbour_sum_two.1 = (f32[32,128,256]{2,1,0:T(8,128)S(1)}, bf16[32,128,256]{2,1,0:T(8,128)(2,1)S(1)}) custom-call(s32[448]{0:T(512)S(1)} %get-tuple-element.102.refs_0_, s32[448]{0:T(512)S(1)} %get-tuple-element.101.refs_1_, s32[1]{0:T(128)} %bitcast.3.refs_2_, bf16[8,128,256]{2,1,0:T(8,128)(2,1)S(1)} %bitcast.101, bf16[8,128,256]{2,1,0:T(8,128)(2,1)} %bitcast.16.refs_4_, ...), custom_call_target="tpu_custom_call" | custom-call | flops 17999998976 | bytes 20971520 | tf_op jit(solution)/shard_map/neighbour_sum_two/pallas_call | solution.py:132
  127.2 1.7 collective-permute-done.22
  130.0 6.6 %collective-permute-start.23 = (f32[96,256]{1,0:T(8,128)S(1)}, f32[96,256]{1,0:T(8,128)S(1)}, u32[]{:S(2)}, u32[]{:S(2)}) collective-permute-start(f32[96,256]{1,0:T(8,128)S(1)} %get-tuple-element.96), channel_id=1, source_target_pairs={{0,4},{1,5},{2,6},{3,7},{4,0},{5,1},{6,2},{7,3},{8,12},{9,13},{10,... | collective-permute-start | bytes 294920 | tf_op jit(solution)/shard_map/ppermute | solution.py:39
  136.6 2.0 collective-permute-start.24
  138.5 1.9 collective-permute-start.25
  140.4 3.5 %add_convert_fusion = (bf16[8,128,256]{2,1,0:T(8,128)(2,1)S(1)}, bf16[8,128,256]{2,1,0:T(8,128)(2,1)S(1)}, bf16[8,128,256]{2,1,0:T(8,128)(2,1)S(1)}, f32[8,128,256]{2,1,0:T(8,128)S(1)}) fusion(f32[32,128,256]{2,1,0:T(8,128)} %copy-done.1, bf16[32,128,256]{2,1,0:T(8,128)(2,1)} %collective-permute-done.18), kind=kLoop, calls=%fused_computation.11 | loop fusion | flops 2883584 | bytes 8912896 | tf_op jit(solution)/shard_map/convert_element_type | solution.py:162
  144.1 3.1 %collective-permute-start.20 = (bf16[1024,256]{1,0:T(8,128)(2,1)S(1)}, bf16[1024,256]{1,0:T(8,128)(2,1)S(1)}, u32[]{:S(2)}, u32[]{:S(2)}) collective-permute-start(bf16[1024,256]{1,0:T(8,128)(2,1)S(1)} %bitcast.116), channel_id=1, source_target_pairs={{0,6},{1,7},{2,0},{3,1},{4,2},{5,3},{6,4},{7,5},{8,14},{9,15},{10,... | collective-permute-start | bytes 1572872 | tf_op jit(solution)/shard_map/ppermute | solution.py:39
  147.5 4.8 %collective-permute-start.26 = (f32[96,256]{1,0:T(8,128)S(1)}, f32[96,256]{1,0:T(8,128)S(1)}, u32[]{:S(2)}, u32[]{:S(2)}) collective-permute-start(f32[96,256]{1,0:T(8,128)S(1)} %fusion.14), channel_id=1, source_target_pairs={{0,64},{16,80},{32,96},{48,112},{64,0},{80,16},{96,32},{112,48},{1... | collective-permute-start | bytes 294920 | tf_op jit(solution)/shard_map/ppermute | solution.py:35
  152.3 2.8 %collective-permute-done.26 = f32[96,256]{1,0:T(8,128)S(1)} collective-permute-done((f32[96,256]{1,0:T(8,128)S(1)}, f32[96,256]{1,0:T(8,128)S(1)}, u32[]{:S(2)}, u32[]{:S(2)}) %collective-permute-start.26) | collective-permute-done | bytes 98336 | tf_op jit(solution)/shard_map/ppermute | solution.py:35
  155.1 2.4 %collective-permute-start.28 = (f32[96,256]{1,0:T(8,128)S(1)}, f32[96,256]{1,0:T(8,128)S(1)}, u32[]{:S(2)}, u32[]{:S(2)}) collective-permute-start(f32[96,256]{1,0:T(8,128)S(1)} %fusion.14), channel_id=1, source_target_pairs={{0,96},{16,112},{32,0},{48,16},{64,32},{80,48},{96,64},{112,80},{1... | collective-permute-start | bytes 294920 | tf_op jit(solution)/shard_map/ppermute | solution.py:35
  158.1 1.6 collective-permute-done.28
  160.3 8.8 %collective-permute-done.20 = bf16[1024,256]{1,0:T(8,128)(2,1)S(1)} collective-permute-done((bf16[1024,256]{1,0:T(8,128)(2,1)S(1)}, bf16[1024,256]{1,0:T(8,128)(2,1)S(1)}, u32[]{:S(2)}, u32[]{:S(2)}) %collective-permute-start.20) | collective-permute-done | bytes 524320 | tf_op jit(solution)/shard_map/ppermute | solution.py:39
  169.8 2.6 %collective-permute-start.30 = (f32[96,256]{1,0:T(8,128)S(1)}, f32[96,256]{1,0:T(8,128)S(1)}, u32[]{:S(2)}, u32[]{:S(2)}) collective-permute-start(f32[96,256]{1,0:T(8,128)S(1)} %add_add_fusion.1), channel_id=1, source_target_pairs={{0,16},{16,0},{32,48},{48,32},{64,80},{80,64},{96,112},{112,96},{1... | collective-permute-start | bytes 294920 | tf_op jit(solution)/shard_map/ppermute | solution.py:35
  172.6 1.3 collective-permute-start.32
  173.9 2.1 %collective-permute-done.30 = f32[96,256]{1,0:T(8,128)S(1)} collective-permute-done((f32[96,256]{1,0:T(8,128)S(1)}, f32[96,256]{1,0:T(8,128)S(1)}, u32[]{:S(2)}, u32[]{:S(2)}) %collective-permute-start.30) | collective-permute-done | bytes 98336 | tf_op jit(solution)/shard_map/ppermute | solution.py:35
  177.1 1.4 collective-permute-done.32
  180.4 3.5 %collective-permute-start.34 = (f32[96,256]{1,0:T(8,128)S(1)}, f32[96,256]{1,0:T(8,128)S(1)}, u32[]{:S(2)}, u32[]{:S(2)}) collective-permute-start(f32[96,256]{1,0:T(8,128)S(1)} %add_add_fusion), channel_id=1, source_target_pairs={{0,4},{1,5},{2,6},{3,7},{4,0},{5,1},{6,2},{7,3},{8,12},{9,13},{10,... | collective-permute-start | bytes 294920 | tf_op jit(solution)/shard_map/ppermute | solution.py:39
  185.4 2.2 %collective-permute-done.34 = f32[96,256]{1,0:T(8,128)S(1)} collective-permute-done((f32[96,256]{1,0:T(8,128)S(1)}, f32[96,256]{1,0:T(8,128)S(1)}, u32[]{:S(2)}, u32[]{:S(2)}) %collective-permute-start.34) | collective-permute-done | bytes 98336 | tf_op jit(solution)/shard_map/ppermute | solution.py:39
  189.1 1.8 collective-permute-done.29
  (110 shorter events, 25.6 us)
Async XLA Ops:
  7.2 116.8 %copy-start = (bf16[256,256]{1,0:T(8,128)(2,1)S(1)}, bf16[256,256]{1,0:T(8,128)(2,1)}, u32[]{:S(2)}) copy-start(bf16[256,256]{1,0:T(8,128)(2,1)} %param.14) | copy-start | bytes 393220
  7.2 42.5 %all-gather.2.cloned.1.call-start = ((), (), s32[]{:S(2)}) async-start(), calls=%async_computation | async-start | bytes 4456448 | tf_op jit(solution)/shard_map/all_gather | solution.py:263
  7.9 7.7 %collective-permute-start = (bf16[512,128]{1,0:T(8,128)(2,1)}, bf16[512,128]{1,0:T(8,128)(2,1)S(1)}, u32[]{:S(2)}, u32[]{:S(2)}) collective-permute-start(bf16[512,128]{1,0:T(8,128)(2,1)} %param.10), channel_id=1, source_target_pairs={{0,16},{16,0},{32,48},{48,32},{64,80},{80,64},{96,112},{112,96},{1... | collective-permute-start | bytes 393224 | tf_op jit(solution)/shard_map/ppermute | solution.py:35
  15.7 9.4 %collective-permute-start.1 = (bf16[1024,128]{1,0:T(8,128)(2,1)S(1)}, bf16[1024,128]{1,0:T(8,128)(2,1)S(1)}, u32[]{:S(2)}, u32[]{:S(2)}) collective-permute-start(bf16[1024,128]{1,0:T(8,128)(2,1)S(1)} %constant_dynamic-update-slice_fusion), channel_id=1, source_target_pairs={{0,32},{16,48},{32,64},{48,80},{64,96},{80,112},{96,0},{112,16},{1... | collective-permute-start | bytes 786440 | tf_op jit(solution)/shard_map/ppermute | solution.py:35
  17.3 12.2 %collective-permute-start.2 = (bf16[1024,128]{1,0:T(8,128)(2,1)S(1)}, bf16[1024,128]{1,0:T(8,128)(2,1)S(1)}, u32[]{:S(2)}, u32[]{:S(2)}) collective-permute-start(bf16[1024,128]{1,0:T(8,128)(2,1)S(1)} %constant_dynamic-update-slice_fusion), channel_id=1, source_target_pairs={{0,96},{16,112},{32,0},{48,16},{64,32},{80,48},{96,64},{112,80},{1... | collective-permute-start | bytes 786440 | tf_op jit(solution)/shard_map/ppermute | solution.py:35
  19.0 12.3 %collective-permute-start.3 = (bf16[1024,128]{1,0:T(8,128)(2,1)S(1)}, bf16[1024,128]{1,0:T(8,128)(2,1)S(1)}, u32[]{:S(2)}, u32[]{:S(2)}) collective-permute-start(bf16[1024,128]{1,0:T(8,128)(2,1)S(1)} %constant_dynamic-update-slice_fusion), channel_id=1, source_target_pairs={{0,64},{16,80},{32,96},{48,112},{64,0},{80,16},{96,32},{112,48},{1... | collective-permute-start | bytes 786440 | tf_op jit(solution)/shard_map/ppermute | solution.py:35
  36.3 2.7 %collective-permute-start.4 = (bf16[32,128,128]{2,1,0:T(8,128)(2,1)S(1)}, bf16[32,128,128]{2,1,0:T(8,128)(2,1)S(1)}, u32[]{:S(2)}, u32[]{:S(2)}) collective-permute-start(bf16[32,128,128]{2,1,0:T(8,128)(2,1)S(1)} %get-tuple-element.38), channel_id=1, source_target_pairs={{0,1},{1,0},{2,3},{3,2},{4,5},{5,4},{6,7},{7,6},{8,9},{9,8},{10,11... | collective-permute-start | bytes 3145736 | tf_op jit(solution)/shard_map/ppermute | solution.py:39
  39.0 13.9 %copy-start.2 = (s32[1,1,448]{2,1,0:T(1,128)S(1)}, s32[1,1,448]{2,1,0:T(1,128)}, u32[]{:S(2)}) copy-start(s32[1,1,448]{2,1,0:T(1,128)} %param.16) | copy-start | bytes 5380
  40.2 21.9 %collective-permute-start.5 = (bf16[1024,128]{1,0:T(8,128)(2,1)}, bf16[1024,128]{1,0:T(8,128)(2,1)}, u32[]{:S(2)}, u32[]{:S(2)}) collective-permute-start(bf16[1024,128]{1,0:T(8,128)(2,1)} %bitcast.10), channel_id=1, source_target_pairs={{0,2},{1,3},{2,4},{3,5},{4,6},{5,7},{6,0},{7,1},{8,10},{9,11},{10,... | collective-permute-start | bytes 786440 | tf_op jit(solution)/shard_map/ppermute | solution.py:39
  45.9 16.2 %collective-permute-start.6 = (bf16[1024,128]{1,0:T(8,128)(2,1)}, bf16[1024,128]{1,0:T(8,128)(2,1)}, u32[]{:S(2)}, u32[]{:S(2)}) collective-permute-start(bf16[1024,128]{1,0:T(8,128)(2,1)} %bitcast.11), channel_id=1, source_target_pairs={{0,6},{1,7},{2,0},{3,1},{4,2},{5,3},{6,4},{7,5},{8,14},{9,15},{10,... | collective-permute-start | bytes 786440 | tf_op jit(solution)/shard_map/ppermute | solution.py:39
  49.7 12.4 %collective-permute-start.7 = (bf16[1024,128]{1,0:T(8,128)(2,1)}, bf16[1024,128]{1,0:T(8,128)(2,1)S(1)}, u32[]{:S(2)}, u32[]{:S(2)}) collective-permute-start(bf16[1024,128]{1,0:T(8,128)(2,1)} %bitcast.12), channel_id=1, source_target_pairs={{0,4},{1,5},{2,6},{3,7},{4,0},{5,1},{6,2},{7,3},{8,12},{9,13},{10,... | collective-permute-start | bytes 786440 | tf_op jit(solution)/shard_map/ppermute | solution.py:39
  52.9 2.2 %copy-start.3 = (bf16[8192,256]{1,0:T(8,128)(2,1)S(1)}, bf16[8192,256]{1,0:T(8,128)(2,1)}, u32[]{:S(2)}) copy-start(bf16[8192,256]{1,0:T(8,128)(2,1)} %all-gather.2.cloned.1.call-done) | copy-start | bytes 12582916
  55.1 7.0 %copy-start.4 = (f32[8,128,128]{2,1,0:T(8,128)S(1)}, f32[8,128,128]{2,1,0:T(8,128)}, u32[]{:S(2)}) copy-start(f32[8,128,128]{2,1,0:T(8,128)} %get-tuple-element.86) | copy-start | bytes 1572868
  62.1 5.1 %copy-start.7 = (bf16[512,128]{1,0:T(8,128)(2,1)S(1)}, bf16[512,128]{1,0:T(8,128)(2,1)}, u32[]{:S(2)}) copy-start(bf16[512,128]{1,0:T(8,128)(2,1)} %param.10) | copy-start | bytes 393220
  62.1 5.1 %copy-start.13 = (bf16[128,256]{1,0:T(8,128)(2,1)S(1)}, bf16[128,256]{1,0:T(8,128)(2,1)}, u32[]{:S(2)}) copy-start(bf16[128,256]{1,0:T(8,128)(2,1)} %param.12) | copy-start | bytes 196612
  62.1 8.0 %copy-start.14 = (bf16[128,256]{1,0:T(8,128)(2,1)S(1)}, bf16[128,256]{1,0:T(8,128)(2,1)}, u32[]{:S(2)}) copy-start(bf16[128,256]{1,0:T(8,128)(2,1)} %param.13) | copy-start | bytes 196612
  63.3 19.1 %copy-start.5 = (f32[1024,128]{1,0:T(8,128)}, f32[1024,128]{1,0:T(8,128)S(1)}, u32[]{:S(2)}) copy-start(f32[1024,128]{1,0:T(8,128)S(1)} %fusion.8) | copy-start | bytes 1572868
  63.4 6.7 %collective-permute-start.8 = (bf16[512,128]{1,0:T(8,128)(2,1)S(1)}, bf16[512,128]{1,0:T(8,128)(2,1)S(1)}, u32[]{:S(2)}, u32[]{:S(2)}) collective-permute-start(bf16[512,128]{1,0:T(8,128)(2,1)S(1)} %slice.168), channel_id=1, source_target_pairs={{0,8},{1,9},{2,10},{3,11},{4,12},{5,13},{6,14},{7,15},{8,0},{9,1},... | collective-permute-start | bytes 393224 | tf_op jit(solution)/shard_map/ppermute | solution.py:39
  70.1 12.3 %copy-start.11 = (bf16[512,128]{1,0:T(8,128)(2,1)}, bf16[512,128]{1,0:T(8,128)(2,1)S(1)}, u32[]{:S(2)}) copy-start(bf16[512,128]{1,0:T(8,128)(2,1)S(1)} %collective-permute-done.8) | copy-start | bytes 393220
  71.3 14.8 %collective-permute-start.9 = (bf16[512,256]{1,0:T(8,128)(2,1)S(1)}, bf16[512,256]{1,0:T(8,128)(2,1)S(1)}, u32[]{:S(2)}, u32[]{:S(2)}) collective-permute-start(bf16[512,256]{1,0:T(8,128)(2,1)S(1)} %get-tuple-element.99), channel_id=1, source_target_pairs={{0,16},{16,0},{32,48},{48,32},{64,80},{80,64},{96,112},{112,96},{1... | collective-permute-start | bytes 786440 | tf_op jit(solution)/shard_map/ppermute | solution.py:35
  78.9 18.6 %collective-permute-start.13 = (bf16[8,128,256]{2,1,0:T(8,128)(2,1)}, bf16[8,128,256]{2,1,0:T(8,128)(2,1)}, u32[]{:S(2)}, u32[]{:S(2)}) collective-permute-start(bf16[8,128,256]{2,1,0:T(8,128)(2,1)} %get-tuple-element.46), channel_id=1, source_target_pairs={{0,16},{16,0},{32,48},{48,32},{64,80},{80,64},{96,112},{112,96},{1... | collective-permute-start | bytes 1572872 | tf_op jit(solution)/shard_map/ppermute | solution.py:35
  78.9 26.1 %collective-permute-start.14 = (bf16[8,128,256]{2,1,0:T(8,128)(2,1)S(1)}, bf16[8,128,256]{2,1,0:T(8,128)(2,1)}, u32[]{:S(2)}, u32[]{:S(2)}) collective-permute-start(bf16[8,128,256]{2,1,0:T(8,128)(2,1)S(1)} %get-tuple-element.47), channel_id=1, source_target_pairs={{0,16},{16,0},{32,48},{48,32},{64,80},{80,64},{96,112},{112,96},{1... | collective-permute-start | bytes 1572872 | tf_op jit(solution)/shard_map/ppermute | solution.py:35
  86.1 18.9 %collective-permute-start.10 = (bf16[1024,256]{1,0:T(8,128)(2,1)S(1)}, bf16[1024,256]{1,0:T(8,128)(2,1)}, u32[]{:S(2)}, u32[]{:S(2)}) collective-permute-start(bf16[1024,256]{1,0:T(8,128)(2,1)S(1)} %pad_maximum_fusion.1), channel_id=1, source_target_pairs={{0,32},{16,48},{32,64},{48,80},{64,96},{80,112},{96,0},{112,16},{1... | collective-permute-start | bytes 1572872 | tf_op jit(solution)/shard_map/ppermute | solution.py:35
  86.4 18.6 %collective-permute-start.11 = (bf16[1024,256]{1,0:T(8,128)(2,1)S(1)}, bf16[1024,256]{1,0:T(8,128)(2,1)}, u32[]{:S(2)}, u32[]{:S(2)}) collective-permute-start(bf16[1024,256]{1,0:T(8,128)(2,1)S(1)} %pad_maximum_fusion.1), channel_id=1, source_target_pairs={{0,96},{16,112},{32,0},{48,16},{64,32},{80,48},{96,64},{112,80},{1... | collective-permute-start | bytes 1572872 | tf_op jit(solution)/shard_map/ppermute | solution.py:35
  89.8 19.5 %collective-permute-start.12 = (bf16[1024,256]{1,0:T(8,128)(2,1)S(1)}, bf16[1024,256]{1,0:T(8,128)(2,1)}, u32[]{:S(2)}, u32[]{:S(2)}) collective-permute-start(bf16[1024,256]{1,0:T(8,128)(2,1)S(1)} %pad_maximum_fusion.1), channel_id=1, source_target_pairs={{0,64},{16,80},{32,96},{48,112},{64,0},{80,16},{96,32},{112,48},{1... | collective-permute-start | bytes 1572872 | tf_op jit(solution)/shard_map/ppermute | solution.py:35
  110.9 11.3 %collective-permute-start.15 = (bf16[512,256]{1,0:T(8,128)(2,1)S(1)}, bf16[512,256]{1,0:T(8,128)(2,1)S(1)}, u32[]{:S(2)}, u32[]{:S(2)}) collective-permute-start(bf16[512,256]{1,0:T(8,128)(2,1)S(1)} %get-tuple-element.87), channel_id=1, source_target_pairs={{0,32},{16,48},{32,64},{48,80},{64,96},{80,112},{96,0},{112,16},{1... | collective-permute-start | bytes 786440 | tf_op jit(solution)/shard_map/ppermute | solution.py:35
  112.4 9.8 %collective-permute-start.16 = (bf16[512,256]{1,0:T(8,128)(2,1)S(1)}, bf16[512,256]{1,0:T(8,128)(2,1)S(1)}, u32[]{:S(2)}, u32[]{:S(2)}) collective-permute-start(bf16[512,256]{1,0:T(8,128)(2,1)S(1)} %get-tuple-element.89), channel_id=1, source_target_pairs={{0,96},{16,112},{32,0},{48,16},{64,32},{80,48},{96,64},{112,80},{1... | collective-permute-start | bytes 786440 | tf_op jit(solution)/shard_map/ppermute | solution.py:35
  114.2 8.9 %collective-permute-start.17 = (bf16[512,256]{1,0:T(8,128)(2,1)S(1)}, bf16[512,256]{1,0:T(8,128)(2,1)S(1)}, u32[]{:S(2)}, u32[]{:S(2)}) collective-permute-start(bf16[512,256]{1,0:T(8,128)(2,1)S(1)} %get-tuple-element.88), channel_id=1, source_target_pairs={{0,64},{16,80},{32,96},{48,112},{64,0},{80,16},{96,32},{112,48},{1... | collective-permute-start | bytes 786440 | tf_op jit(solution)/shard_map/ppermute | solution.py:35
  114.9 8.7 %copy-start.10 = (bf16[256,256]{1,0:T(8,128)(2,1)S(1)}, bf16[256,256]{1,0:T(8,128)(2,1)}, u32[]{:S(2)}) copy-start(bf16[256,256]{1,0:T(8,128)(2,1)} %param.15) | copy-start | bytes 393220
  123.3 17.1 %collective-permute-start.18 = (bf16[32,128,256]{2,1,0:T(8,128)(2,1)S(1)}, bf16[32,128,256]{2,1,0:T(8,128)(2,1)}, u32[]{:S(2)}, u32[]{:S(2)}) collective-permute-start(bf16[32,128,256]{2,1,0:T(8,128)(2,1)S(1)} %get-tuple-element.63), channel_id=1, source_target_pairs={{0,1},{1,0},{2,3},{3,2},{4,5},{5,4},{6,7},{7,6},{8,9},{9,8},{10,11... | collective-permute-start | bytes 6291464 | tf_op jit(solution)/shard_map/ppermute | solution.py:39
  126.8 2.2 %collective-permute-start.22 = (f32[384,256]{1,0:T(8,128)}, f32[384,256]{1,0:T(8,128)}, u32[]{:S(2)}, u32[]{:S(2)}) collective-permute-start(f32[384,256]{1,0:T(8,128)} %dynamic-slice_bitcast_fusion), channel_id=1, source_target_pairs={{0,1},{1,0},{2,3},{3,2},{4,5},{5,4},{6,7},{7,6},{8,9},{9,8},{10,11... | collective-permute-start | bytes 1179656 | tf_op jit(solution)/shard_map/ppermute | solution.py:39
  130.0 17.2 %collective-permute-start.23 = (f32[96,256]{1,0:T(8,128)S(1)}, f32[96,256]{1,0:T(8,128)S(1)}, u32[]{:S(2)}, u32[]{:S(2)}) collective-permute-start(f32[96,256]{1,0:T(8,128)S(1)} %get-tuple-element.96), channel_id=1, source_target_pairs={{0,4},{1,5},{2,6},{3,7},{4,0},{5,1},{6,2},{7,3},{8,12},{9,13},{10,... | collective-permute-start | bytes 294920 | tf_op jit(solution)/shard_map/ppermute | solution.py:39
  136.6 10.8 %collective-permute-start.24 = (f32[96,256]{1,0:T(8,128)S(1)}, f32[96,256]{1,0:T(8,128)S(1)}, u32[]{:S(2)}, u32[]{:S(2)}) collective-permute-start(f32[96,256]{1,0:T(8,128)S(1)} %get-tuple-element.98), channel_id=1, source_target_pairs={{0,2},{1,3},{2,4},{3,5},{4,6},{5,7},{6,0},{7,1},{8,10},{9,11},{10,... | collective-permute-start | bytes 294920 | tf_op jit(solution)/shard_map/ppermute | solution.py:39
  138.5 8.9 %collective-permute-start.25 = (f32[96,256]{1,0:T(8,128)S(1)}, f32[96,256]{1,0:T(8,128)S(1)}, u32[]{:S(2)}, u32[]{:S(2)}) collective-permute-start(f32[96,256]{1,0:T(8,128)S(1)} %get-tuple-element.97), channel_id=1, source_target_pairs={{0,6},{1,7},{2,0},{3,1},{4,2},{5,3},{6,4},{7,5},{8,14},{9,15},{10,... | collective-permute-start | bytes 294920 | tf_op jit(solution)/shard_map/ppermute | solution.py:39
  143.9 16.4 %collective-permute-start.19 = (bf16[1024,256]{1,0:T(8,128)(2,1)S(1)}, bf16[1024,256]{1,0:T(8,128)(2,1)S(1)}, u32[]{:S(2)}, u32[]{:S(2)}) collective-permute-start(bf16[1024,256]{1,0:T(8,128)(2,1)S(1)} %bitcast.117), channel_id=1, source_target_pairs={{0,2},{1,3},{2,4},{3,5},{4,6},{5,7},{6,0},{7,1},{8,10},{9,11},{10,... | collective-permute-start | bytes 1572872 | tf_op jit(solution)/shard_map/ppermute | solution.py:39
  144.1 24.9 %collective-permute-start.20 = (bf16[1024,256]{1,0:T(8,128)(2,1)S(1)}, bf16[1024,256]{1,0:T(8,128)(2,1)S(1)}, u32[]{:S(2)}, u32[]{:S(2)}) collective-permute-start(bf16[1024,256]{1,0:T(8,128)(2,1)S(1)} %bitcast.116), channel_id=1, source_target_pairs={{0,6},{1,7},{2,0},{3,1},{4,2},{5,3},{6,4},{7,5},{8,14},{9,15},{10,... | collective-permute-start | bytes 1572872 | tf_op jit(solution)/shard_map/ppermute | solution.py:39
  147.2 22.6 %collective-permute-start.21 = (bf16[1024,256]{1,0:T(8,128)(2,1)S(1)}, bf16[1024,256]{1,0:T(8,128)(2,1)S(1)}, u32[]{:S(2)}, u32[]{:S(2)}) collective-permute-start(bf16[1024,256]{1,0:T(8,128)(2,1)S(1)} %bitcast.115), channel_id=1, source_target_pairs={{0,4},{1,5},{2,6},{3,7},{4,0},{5,1},{6,2},{7,3},{8,12},{9,13},{10,... | collective-permute-start | bytes 1572872 | tf_op jit(solution)/shard_map/ppermute | solution.py:39
  147.5 7.6 %collective-permute-start.26 = (f32[96,256]{1,0:T(8,128)S(1)}, f32[96,256]{1,0:T(8,128)S(1)}, u32[]{:S(2)}, u32[]{:S(2)}) collective-permute-start(f32[96,256]{1,0:T(8,128)S(1)} %fusion.14), channel_id=1, source_target_pairs={{0,64},{16,80},{32,96},{48,112},{64,0},{80,16},{96,32},{112,48},{1... | collective-permute-start | bytes 294920 | tf_op jit(solution)/shard_map/ppermute | solution.py:35
  152.3 5.8 %collective-permute-start.27 = (f32[96,256]{1,0:T(8,128)S(1)}, f32[96,256]{1,0:T(8,128)S(1)}, u32[]{:S(2)}, u32[]{:S(2)}) collective-permute-start(f32[96,256]{1,0:T(8,128)S(1)} %fusion.14), channel_id=1, source_target_pairs={{0,32},{16,48},{32,64},{48,80},{64,96},{80,112},{96,0},{112,16},{1... | collective-permute-start | bytes 294920 | tf_op jit(solution)/shard_map/ppermute | solution.py:35
  155.1 4.6 %collective-permute-start.28 = (f32[96,256]{1,0:T(8,128)S(1)}, f32[96,256]{1,0:T(8,128)S(1)}, u32[]{:S(2)}, u32[]{:S(2)}) collective-permute-start(f32[96,256]{1,0:T(8,128)S(1)} %fusion.14), channel_id=1, source_target_pairs={{0,96},{16,112},{32,0},{48,16},{64,32},{80,48},{96,64},{112,80},{1... | collective-permute-start | bytes 294920 | tf_op jit(solution)/shard_map/ppermute | solution.py:35
  169.8 6.2 %collective-permute-start.30 = (f32[96,256]{1,0:T(8,128)S(1)}, f32[96,256]{1,0:T(8,128)S(1)}, u32[]{:S(2)}, u32[]{:S(2)}) collective-permute-start(f32[96,256]{1,0:T(8,128)S(1)} %add_add_fusion.1), channel_id=1, source_target_pairs={{0,16},{16,0},{32,48},{48,32},{64,80},{80,64},{96,112},{112,96},{1... | collective-permute-start | bytes 294920 | tf_op jit(solution)/shard_map/ppermute | solution.py:35
  172.4 4.7 %collective-permute-start.31 = (f32[96,256]{1,0:T(8,128)S(1)}, f32[96,256]{1,0:T(8,128)}, u32[]{:S(2)}, u32[]{:S(2)}) collective-permute-start(f32[96,256]{1,0:T(8,128)S(1)} %add_add_fusion.1), channel_id=1, source_target_pairs={{0,8},{1,9},{2,10},{3,11},{4,12},{5,13},{6,14},{7,15},{8,0},{9,1},... | collective-permute-start | bytes 294920 | tf_op jit(solution)/shard_map/ppermute | solution.py:39
  172.6 5.9 %collective-permute-start.32 = (f32[96,256]{1,0:T(8,128)S(1)}, f32[96,256]{1,0:T(8,128)}, u32[]{:S(2)}, u32[]{:S(2)}) collective-permute-start(f32[96,256]{1,0:T(8,128)S(1)} %add_add_fusion.1), channel_id=1, source_target_pairs={{0,24},{1,25},{2,26},{3,27},{4,28},{5,29},{6,30},{7,31},{8,16},{9,... | collective-permute-start | bytes 294920 | tf_op jit(solution)/shard_map/ppermute | solution.py:31
  179.5 5.9 %collective-permute-start.33 = (f32[96,256]{1,0:T(8,128)S(1)}, f32[96,256]{1,0:T(8,128)S(1)}, u32[]{:S(2)}, u32[]{:S(2)}) collective-permute-start(f32[96,256]{1,0:T(8,128)S(1)} %add_add_fusion), channel_id=1, source_target_pairs={{0,2},{1,3},{2,4},{3,5},{4,6},{5,7},{6,0},{7,1},{8,10},{9,11},{10,... | collective-permute-start | bytes 294920 | tf_op jit(solution)/shard_map/ppermute | solution.py:39
  180.4 7.2 %collective-permute-start.34 = (f32[96,256]{1,0:T(8,128)S(1)}, f32[96,256]{1,0:T(8,128)S(1)}, u32[]{:S(2)}, u32[]{:S(2)}) collective-permute-start(f32[96,256]{1,0:T(8,128)S(1)} %add_add_fusion), channel_id=1, source_target_pairs={{0,4},{1,5},{2,6},{3,7},{4,0},{5,1},{6,2},{7,3},{8,12},{9,13},{10,... | collective-permute-start | bytes 294920 | tf_op jit(solution)/shard_map/ppermute | solution.py:39
  184.0 4.6 %collective-permute-start.35 = (f32[96,256]{1,0:T(8,128)S(1)}, f32[96,256]{1,0:T(8,128)S(1)}, u32[]{:S(2)}, u32[]{:S(2)}) collective-permute-start(f32[96,256]{1,0:T(8,128)S(1)} %add_add_fusion), channel_id=1, source_target_pairs={{0,6},{1,7},{2,0},{3,1},{4,2},{5,3},{6,4},{7,5},{8,14},{9,15},{10,... | collective-permute-start | bytes 294920 | tf_op jit(solution)/shard_map/ppermute | solution.py:39
  184.5 6.5 %collective-permute-start.29 = (bf16[512,256]{1,0:T(8,128)(2,1)S(1)}, bf16[512,256]{1,0:T(8,128)(2,1)S(1)}, u32[]{:S(2)}, u32[]{:S(2)}) collective-permute-start(bf16[512,256]{1,0:T(8,128)(2,1)S(1)} %slice.167), channel_id=1, source_target_pairs={{0,8},{1,9},{2,10},{3,11},{4,12},{5,13},{6,14},{7,15},{8,0},{9,1},... | collective-permute-start | bytes 786440 | tf_op jit(solution)/shard_map/ppermute | solution.py:39
  188.8 3.3 %collective-permute-start.36 = (f32[384,256]{1,0:T(8,128)S(1)}, f32[384,256]{1,0:T(8,128)S(1)}, u32[]{:S(2)}, u32[]{:S(2)}) collective-permute-start(f32[384,256]{1,0:T(8,128)S(1)} %pad_maximum_fusion.3), channel_id=1, source_target_pairs={{0,1},{1,0},{2,3},{3,2},{4,5},{5,4},{6,7},{7,6},{8,9},{9,8},{10,11... | collective-permute-start | bytes 1179656 | tf_op jit(solution)/shard_map/ppermute | solution.py:39
  (6 other events, 8.9 us)
Sparse Core Ops, SparseCore 0:
  9.7 39.9 all-gather.1

commit v4 on v3

--- a/solution.py
+++ b/solution.py
@@ -196,12 +196,12 @@
 
 def scatter_x(part, x):
     parts = part.reshape(4, -1, part.shape[-1])
-    sent = [send_col(pick(parts, (x + d) % 4), d, 0) for d in (2, 1, 3)]
+    sent = [send_col(pick(parts, (x + d) % 4), d, 0) for d in (1, 3, 2)]
     return pick(parts, x) + sent[0] + sent[1] + sent[2]
 
 
 def exchange_y(part):
-    far, above, below = [send_row(part, d, 0) for d in (2, 1, 3)]
+    above, below, far = [send_row(part, d, 0) for d in (1, 3, 2)]
     return (part + far) + (above + below)
 
 
@@ -211,7 +211,7 @@
 
 
 def gather_x(part, x):
-    far, above, below = [send_col(part, d, 0) for d in (2, 1, 3)]
+    above, below, far = [send_col(part, d, 0) for d in (1, 3, 2)]
     parts = jnp.stack([part, above, far, below])
     return jnp.concatenate([pick(parts, (x - j) % 4) for j in range(4)])
 
@@ -295,7 +295,7 @@
     )
     local_self1 = jnp.dot(features.T, dz1, preferred_element_type=F32)
     local_neigh1 = fdot(agg1.T, dz1)
-    grads = jnp.concatenate([local_self1, local_neigh1, local_self2, local_neigh2])
+    grads = jnp.concatenate([local_self1, local_self2, local_neigh1, local_neigh2])
     mine, parts = add_cores(own, other)
     sent = send_x(parts)
     grads = exchange_y(scatter_x(sum_cores(grads, core), x))
@@ -305,8 +305,10 @@
     output = (jnp.dot(h1, w_self2, preferred_element_type=F32) + fdot(agg2, w_neigh2)).astype(BF)
     grads = gather_x(grads, x)
     other = send_col(grads, 0, 0, 1)
-    grads = jnp.where(core == 0, jnp.concatenate([grads, other]), jnp.concatenate([other, grads]))
-    return (output, grads[:128], grads[128:256], grads[256:512], grads[512:])
+    own_first = core == 0
+    grads_self = jnp.where(own_first, grads, other)
+    grads_neigh = jnp.where(own_first, other, grads)
+    return (output, grads_self[:128], grads_neigh[:128], grads_self[128:], grads_neigh[128:])
 
 
 def solution(mesh):

time: 202 us -> 203 us (level)
  starting transfers between devices: 73.5 us -> 60.6 us
  Pallas kernels: 19.2 us -> 28.4 us
  waiting for transfers between devices: 69 us -> 73 us
    pallas_call x3, Pallas kernels: 19.2 us -> 28.4 us  [tile_product(): pl.pallas_call(functools.partial(tile_kernel, transpose, len(pieces), spl...]
    ppermute x19, starting transfers between devices: 33 us -> 24.8 us  [send_col(): return lax.ppermute(value, 'col', col_perm(dx, dz, dc))]
    ppermute x17, starting transfers between devices: 39.2 us -> 35.3 us  [send_row(): return lax.ppermute(value, 'row', row_perm(dy, dz))]
    ppermute x17, waiting for transfers between devices: 39.6 us -> 42.3 us  [send_row(): return lax.ppermute(value, 'row', row_perm(dy, dz))]
    unnamed x41 -> x33, local copies, waits for them, and re-layouts: 3.78 us -> 4.22 us
  transfers between devices with their start and end apart: 38 -> 38, of which waited for: 26 -> 24; matrix products, arithmetic and copies ran while one was open for 7% -> 7% of each run, Pallas kernels for 10% -> 14%
where the time goes in v4:
time: 203 us
  waiting for transfers between devices  73 us (36%)
  starting transfers between devices  60.6 us (30%)
  Pallas kernels  28.4 us (14%)
  between operations  15.2 us (7%)
  other arithmetic  11.5 us (6%)
  local copies, waits for them, and re-layouts  7.94 us (4%)
  matrix products  5.81 us (3%)
    ppermute x17, waiting for transfers between devices, send_row(): return lax.ppermute(value, 'row', row_perm(dy, dz))  42.3 us
    ppermute x17, starting transfers between devices, send_row(): return lax.ppermute(value, 'row', row_perm(dy, dz))  35.3 us
    pallas_call x3, Pallas kernels, tile_product(): pl.pallas_call(functools.partial(tile_kernel, transpose, len(pieces), spl...  28.4 us
    ppermute x19, waiting for transfers between devices, send_col(): return lax.ppermute(value, 'col', col_perm(dx, dz, dc))  24.8 us
    ppermute x19, starting transfers between devices, send_col(): return lax.ppermute(value, 'col', col_perm(dx, dz, dc))  24.8 us
    convert_element_type x2, other arithmetic, add_cores(): return (part(0), [part(d).astype(BF) for d in (1, 3, 2)])  4.65 us
    unnamed x33, local copies, waits for them, and re-layouts  4.22 us
  transfers between devices with their start and end apart: 38, of which 24 were waited for; matrix products, arithmetic and copies ran while one was open for 7% of the time, Pallas kernels for 14%

profile of v4, /device:TPU:0, one launch (start us, length us, event | category | flops | bytes accessed | tf_op | source)
XLA Modules:
  0.0 202.5 jit_solution(347430976874280815)
XLA Ops:
  7.9 4.0 %collective-permute-start = (bf16[512,128]{1,0:T(8,128)(2,1)}, bf16[512,128]{1,0:T(8,128)(2,1)S(1)}, u32[]{:S(2)}, u32[]{:S(2)}) collective-permute-start(bf16[512,128]{1,0:T(8,128)(2,1)} %param.10), channel_id=1, source_target_pairs={{0,16},{16,0},{32,48},{48,32},{64,80},{80,64},{96,112},{112,96},{1... | collective-permute-start | bytes 393224 | tf_op jit(solution)/shard_map/ppermute | solution.py:35
  13.5 2.1 %collective-permute-done = bf16[512,128]{1,0:T(8,128)(2,1)S(1)} collective-permute-done((bf16[512,128]{1,0:T(8,128)(2,1)}, bf16[512,128]{1,0:T(8,128)(2,1)S(1)}, u32[]{:S(2)}, u32[]{:S(2)}) %collective-permute-start) | collective-permute-done | bytes 131104 | tf_op jit(solution)/shard_map/ppermute | solution.py:35
  15.7 1.6 collective-permute-start.1
  17.3 1.7 collective-permute-start.2
  19.0 2.0 collective-permute-start.3
  22.5 2.6 %collective-permute-done.1 = bf16[1024,128]{1,0:T(8,128)(2,1)S(1)} collective-permute-done((bf16[1024,128]{1,0:T(8,128)(2,1)S(1)}, bf16[1024,128]{1,0:T(8,128)(2,1)S(1)}, u32[]{:S(2)}, u32[]{:S(2)}) %collective-permute-start.1) | collective-permute-done | bytes 262176 | tf_op jit(solution)/shard_map/ppermute | solution.py:35
  25.1 4.4 %collective-permute-done.2 = bf16[1024,128]{1,0:T(8,128)(2,1)S(1)} collective-permute-done((bf16[1024,128]{1,0:T(8,128)(2,1)S(1)}, bf16[1024,128]{1,0:T(8,128)(2,1)S(1)}, u32[]{:S(2)}, u32[]{:S(2)}) %collective-permute-start.2) | collective-permute-done | bytes 262176 | tf_op jit(solution)/shard_map/ppermute | solution.py:35
  29.5 1.8 collective-permute-done.3
  31.3 7.3 %neighbour_sum_one.1 = (f32[32,128,128]{2,1,0:T(8,128)S(1)}, bf16[32,128,128]{2,1,0:T(8,128)(2,1)S(1)}) custom-call(s32[448]{0:T(512)S(1)} %get-tuple-element.94.refs_0_, s32[448]{0:T(512)S(1)} %get-tuple-element.93.refs_1_, s32[1]{0:T(128)} %bitcast.3.refs_2_, bf16[8,128,128]{2,1,0:T(8,128)(2,1)S(1)} %bitcast.98, bf16[8,128,128]{2,1,0:T(8,128)(2,1)S(1)} %bitcast.102, ...), custom_call_target="tpu_custom_call" | custom-call | flops 17999998976 | bytes 20971520 | tf_op jit(solution)/shard_map/neighbour_sum_one/pallas_call | solution.py:132
  38.7 2.6 %collective-permute-done.4 = bf16[32,128,128]{2,1,0:T(8,128)(2,1)S(1)} collective-permute-done((bf16[32,128,128]{2,1,0:T(8,128)(2,1)S(1)}, bf16[32,128,128]{2,1,0:T(8,128)(2,1)S(1)}, u32[]{:S(2)}, u32[]{:S(2)}) %collective-permute-start.4) | collective-permute-done | bytes 1048608 | tf_op jit(solution)/shard_map/ppermute | solution.py:39
  42.6 2.6 %collective-permute-start.5 = (bf16[1024,128]{1,0:T(8,128)(2,1)}, bf16[1024,128]{1,0:T(8,128)(2,1)}, u32[]{:S(2)}, u32[]{:S(2)}) collective-permute-start(bf16[1024,128]{1,0:T(8,128)(2,1)} %bitcast.10), channel_id=1, source_target_pairs={{0,2},{1,3},{2,4},{3,5},{4,6},{5,7},{6,0},{7,1},{8,10},{9,11},{10,... | collective-permute-start | bytes 786440 | tf_op jit(solution)/shard_map/ppermute | solution.py:39
  45.1 1.8 collective-permute-start.6
  46.9 3.1 %all-gather.2.cloned.1.call-done = bf16[8192,256]{1,0:T(8,128)(2,1)} async-done(((bf16[512,256]{1,0:T(8,128)(2,1)}), bf16[8192,256]{1,0:T(8,128)(2,1)}) %all-gather.2.cloned.1.call-update) | async-done | bytes 4194320 | tf_op jit(solution)/shard_map/all_gather | solution.py:263
  50.1 3.0 %collective-permute-start.7 = (bf16[1024,128]{1,0:T(8,128)(2,1)}, bf16[1024,128]{1,0:T(8,128)(2,1)S(1)}, u32[]{:S(2)}, u32[]{:S(2)}) collective-permute-start(bf16[1024,128]{1,0:T(8,128)(2,1)} %bitcast.12), channel_id=1, source_target_pairs={{0,4},{1,5},{2,6},{3,7},{4,0},{5,1},{6,2},{7,3},{8,12},{9,13},{10,... | collective-permute-start | bytes 786440 | tf_op jit(solution)/shard_map/ppermute | solution.py:39
  53.0 2.2 %copy-done.3 = bf16[8192,256]{1,0:T(8,128)(2,1)S(1)} copy-done((bf16[8192,256]{1,0:T(8,128)(2,1)S(1)}, bf16[8192,256]{1,0:T(8,128)(2,1)}, u32[]{:S(2)}) %copy-start.3) | copy-done | bytes 4194328
  55.2 10.4 %neighbour_sum_back.1 = (f32[16,128,256]{2,1,0:T(8,128)S(1)}, bf16[8,128,256]{2,1,0:T(8,128)(2,1)}, bf16[8,128,256]{2,1,0:T(8,128)(2,1)S(1)}) custom-call(s32[448]{0:T(512)S(1)} %bitcast.100, s32[448]{0:T(512)S(1)} %get-tuple-element.69.refs_1_, s32[1]{0:T(128)} %bitcast.3.refs_2_, bf16[64,128,256]{2,1,0:T(8,128)(2,1)S(1)} %bitcast.101, ...), custom_call_target="tpu_custom_call" | custom-call | flops 17999998976 | bytes 20971520 | tf_op jit(solution)/shard_map/neighbour_sum_back/pallas_call | solution.py:132
  68.6 3.4 %collective-permute-done.8 = bf16[512,128]{1,0:T(8,128)(2,1)S(1)} collective-permute-done((bf16[512,128]{1,0:T(8,128)(2,1)S(1)}, bf16[512,128]{1,0:T(8,128)(2,1)S(1)}, u32[]{:S(2)}, u32[]{:S(2)}) %collective-permute-start.8) | collective-permute-done | bytes 131104 | tf_op jit(solution)/shard_map/ppermute | solution.py:39
  73.3 3.9 %collective-permute-start.9 = (bf16[512,256]{1,0:T(8,128)(2,1)S(1)}, bf16[512,256]{1,0:T(8,128)(2,1)S(1)}, u32[]{:S(2)}, u32[]{:S(2)}) collective-permute-start(bf16[512,256]{1,0:T(8,128)(2,1)S(1)} %get-tuple-element.91), channel_id=1, source_target_pairs={{0,16},{16,0},{32,48},{48,32},{64,80},{80,64},{96,112},{112,96},{1... | collective-permute-start | bytes 786440 | tf_op jit(solution)/shard_map/ppermute | solution.py:35
  77.3 3.5 %collective-permute-start.14 = (bf16[8,128,256]{2,1,0:T(8,128)(2,1)S(1)}, bf16[8,128,256]{2,1,0:T(8,128)(2,1)}, u32[]{:S(2)}, u32[]{:S(2)}) collective-permute-start(bf16[8,128,256]{2,1,0:T(8,128)(2,1)S(1)} %get-tuple-element.47), channel_id=1, source_target_pairs={{0,16},{16,0},{32,48},{48,32},{64,80},{80,64},{96,112},{112,96},{1... | collective-permute-start | bytes 1572872 | tf_op jit(solution)/shard_map/ppermute | solution.py:35
  80.8 3.6 %collective-permute-done.9 = bf16[512,256]{1,0:T(8,128)(2,1)S(1)} collective-permute-done((bf16[512,256]{1,0:T(8,128)(2,1)S(1)}, bf16[512,256]{1,0:T(8,128)(2,1)S(1)}, u32[]{:S(2)}, u32[]{:S(2)}) %collective-permute-start.9) | collective-permute-done | bytes 262176 | tf_op jit(solution)/shard_map/ppermute | solution.py:35
  84.4 4.0 %collective-permute-start.10 = (bf16[1024,256]{1,0:T(8,128)(2,1)S(1)}, bf16[1024,256]{1,0:T(8,128)(2,1)}, u32[]{:S(2)}, u32[]{:S(2)}) collective-permute-start(bf16[1024,256]{1,0:T(8,128)(2,1)S(1)} %pad_maximum_fusion.1), channel_id=1, source_target_pairs={{0,32},{16,48},{32,64},{48,80},{64,96},{80,112},{96,0},{112,16},{1... | collective-permute-start | bytes 1572872 | tf_op jit(solution)/shard_map/ppermute | solution.py:35
  89.0 1.9 collective-permute-start.12
  92.2 3.5 %collective-permute-done.13 = bf16[8,128,256]{2,1,0:T(8,128)(2,1)} collective-permute-done((bf16[8,128,256]{2,1,0:T(8,128)(2,1)}, bf16[8,128,256]{2,1,0:T(8,128)(2,1)}, u32[]{:S(2)}, u32[]{:S(2)}) %collective-permute-start.13) | collective-permute-done | bytes 524320 | tf_op jit(solution)/shard_map/ppermute | solution.py:35
  95.7 10.1 %collective-permute-done.14 = bf16[8,128,256]{2,1,0:T(8,128)(2,1)} collective-permute-done((bf16[8,128,256]{2,1,0:T(8,128)(2,1)S(1)}, bf16[8,128,256]{2,1,0:T(8,128)(2,1)}, u32[]{:S(2)}, u32[]{:S(2)}) %collective-permute-start.14) | collective-permute-done | bytes 524320 | tf_op jit(solution)/shard_map/ppermute | solution.py:35
  105.8 4.3 %collective-permute-done.11 = bf16[1024,256]{1,0:T(8,128)(2,1)} collective-permute-done((bf16[1024,256]{1,0:T(8,128)(2,1)S(1)}, bf16[1024,256]{1,0:T(8,128)(2,1)}, u32[]{:S(2)}, u32[]{:S(2)}) %collective-permute-start.11) | collective-permute-done | bytes 524320 | tf_op jit(solution)/shard_map/ppermute | solution.py:35
  110.2 1.9 collective-permute-done.12
  112.1 1.5 convert_add_fusion
  115.0 2.1 %collective-permute-start.16 = (bf16[512,256]{1,0:T(8,128)(2,1)S(1)}, bf16[512,256]{1,0:T(8,128)(2,1)S(1)}, u32[]{:S(2)}, u32[]{:S(2)}) collective-permute-start(bf16[512,256]{1,0:T(8,128)(2,1)S(1)} %get-tuple-element.81), channel_id=1, source_target_pairs={{0,96},{16,112},{32,0},{48,16},{64,32},{80,48},{96,64},{112,80},{1... | collective-permute-start | bytes 786440 | tf_op jit(solution)/shard_map/ppermute | solution.py:35
  117.2 10.7 %neighbour_sum_two.1 = (f32[32,128,256]{2,1,0:T(8,128)S(1)}, bf16[32,128,256]{2,1,0:T(8,128)(2,1)S(1)}) custom-call(s32[448]{0:T(512)S(1)} %get-tuple-element.94.refs_0_, s32[448]{0:T(512)S(1)} %get-tuple-element.93.refs_1_, s32[1]{0:T(128)} %bitcast.3.refs_2_, bf16[8,128,256]{2,1,0:T(8,128)(2,1)S(1)} %bitcast.97, bf16[8,128,256]{2,1,0:T(8,128)(2,1)} %bitcast.16.refs_4_, ...), custom_call_target="tpu_custom_call" | custom-call | flops 17999998976 | bytes 20971520 | tf_op jit(solution)/shard_map/neighbour_sum_two/pallas_call | solution.py:132
  132.2 2.1 %collective-permute-done.22 = f32[384,256]{1,0:T(8,128)} collective-permute-done((f32[384,256]{1,0:T(8,128)}, f32[384,256]{1,0:T(8,128)}, u32[]{:S(2)}, u32[]{:S(2)}) %collective-permute-start.22) | collective-permute-done | bytes 393248 | tf_op jit(solution)/shard_map/ppermute | solution.py:39
  135.4 3.2 %collective-permute-start.24 = (f32[96,256]{1,0:T(8,128)S(1)}, f32[96,256]{1,0:T(8,128)S(1)}, u32[]{:S(2)}, u32[]{:S(2)}) collective-permute-start(f32[96,256]{1,0:T(8,128)S(1)} %get-tuple-element.90), channel_id=1, source_target_pairs={{0,6},{1,7},{2,0},{3,1},{4,2},{5,3},{6,4},{7,5},{8,14},{9,15},{10,... | collective-permute-start | bytes 294920 | tf_op jit(solution)/shard_map/ppermute | solution.py:39
  139.3 3.5 %add_convert_fusion = (bf16[8,128,256]{2,1,0:T(8,128)(2,1)S(1)}, bf16[8,128,256]{2,1,0:T(8,128)(2,1)S(1)}, bf16[8,128,256]{2,1,0:T(8,128)(2,1)S(1)}, f32[8,128,256]{2,1,0:T(8,128)S(1)}) fusion(f32[32,128,256]{2,1,0:T(8,128)} %copy-done.1, bf16[32,128,256]{2,1,0:T(8,128)(2,1)} %collective-permute-done.18), kind=kLoop, calls=%fused_computation.11 | loop fusion | flops 2883584 | bytes 8912896 | tf_op jit(solution)/shard_map/convert_element_type | solution.py:162
  142.8 1.5 collective-permute-start.19
  144.3 1.8 collective-permute-start.20
  146.1 1.6 collective-permute-start.21
  147.7 4.6 %collective-permute-start.26 = (f32[96,256]{1,0:T(8,128)S(1)}, f32[96,256]{1,0:T(8,128)S(1)}, u32[]{:S(2)}, u32[]{:S(2)}) collective-permute-start(f32[96,256]{1,0:T(8,128)S(1)} %fusion.14), channel_id=1, source_target_pairs={{0,64},{16,80},{32,96},{48,112},{64,0},{80,16},{96,32},{112,48},{1... | collective-permute-start | bytes 294920 | tf_op jit(solution)/shard_map/ppermute | solution.py:35
  152.4 3.3 %collective-permute-done.26 = f32[96,256]{1,0:T(8,128)S(1)} collective-permute-done((f32[96,256]{1,0:T(8,128)S(1)}, f32[96,256]{1,0:T(8,128)S(1)}, u32[]{:S(2)}, u32[]{:S(2)}) %collective-permute-start.26) | collective-permute-done | bytes 98336 | tf_op jit(solution)/shard_map/ppermute | solution.py:35
  156.8 1.5 collective-permute-done.27
  158.2 2.1 %collective-permute-done.28 = f32[96,256]{1,0:T(8,128)S(1)} collective-permute-done((f32[96,256]{1,0:T(8,128)S(1)}, f32[96,256]{1,0:T(8,128)S(1)}, u32[]{:S(2)}, u32[]{:S(2)}) %collective-permute-start.28) | collective-permute-done | bytes 98336 | tf_op jit(solution)/shard_map/ppermute | solution.py:35
  160.3 8.4 %collective-permute-done.19 = bf16[1024,256]{1,0:T(8,128)(2,1)S(1)} collective-permute-done((bf16[1024,256]{1,0:T(8,128)(2,1)S(1)}, bf16[1024,256]{1,0:T(8,128)(2,1)S(1)}, u32[]{:S(2)}, u32[]{:S(2)}) %collective-permute-start.19) | collective-permute-done | bytes 524320 | tf_op jit(solution)/shard_map/ppermute | solution.py:39
  168.7 2.8 %collective-permute-start.30 = (f32[96,256]{1,0:T(8,128)S(1)}, f32[96,256]{1,0:T(8,128)S(1)}, u32[]{:S(2)}, u32[]{:S(2)}) collective-permute-start(f32[96,256]{1,0:T(8,128)S(1)} %add_add_fusion.1), channel_id=1, source_target_pairs={{0,16},{16,0},{32,48},{48,32},{64,80},{80,64},{96,112},{112,96},{1... | collective-permute-start | bytes 294920 | tf_op jit(solution)/shard_map/ppermute | solution.py:35
  171.5 2.1 %collective-permute-start.31 = (f32[96,256]{1,0:T(8,128)S(1)}, f32[96,256]{1,0:T(8,128)}, u32[]{:S(2)}, u32[]{:S(2)}) collective-permute-start(f32[96,256]{1,0:T(8,128)S(1)} %add_add_fusion.1), channel_id=1, source_target_pairs={{0,8},{1,9},{2,10},{3,11},{4,12},{5,13},{6,14},{7,15},{8,0},{9,1},... | collective-permute-start | bytes 294920 | tf_op jit(solution)/shard_map/ppermute | solution.py:39
  175.1 2.3 %collective-permute-done.31 = f32[96,256]{1,0:T(8,128)} collective-permute-done((f32[96,256]{1,0:T(8,128)S(1)}, f32[96,256]{1,0:T(8,128)}, u32[]{:S(2)}, u32[]{:S(2)}) %collective-permute-start.31) | collective-permute-done | bytes 98336 | tf_op jit(solution)/shard_map/ppermute | solution.py:39
  177.4 2.2 %collective-permute-done.32 = f32[96,256]{1,0:T(8,128)} collective-permute-done((f32[96,256]{1,0:T(8,128)S(1)}, f32[96,256]{1,0:T(8,128)}, u32[]{:S(2)}, u32[]{:S(2)}) %collective-permute-start.32) | collective-permute-done | bytes 98336 | tf_op jit(solution)/shard_map/ppermute | solution.py:31
  180.6 1.5 collective-permute-start.33
  182.1 2.7 %collective-permute-start.34 = (f32[96,256]{1,0:T(8,128)S(1)}, f32[96,256]{1,0:T(8,128)S(1)}, u32[]{:S(2)}, u32[]{:S(2)}) collective-permute-start(f32[96,256]{1,0:T(8,128)S(1)} %add_add_fusion), channel_id=1, source_target_pairs={{0,4},{1,5},{2,6},{3,7},{4,0},{5,1},{6,2},{7,3},{8,12},{9,13},{10,... | collective-permute-start | bytes 294920 | tf_op jit(solution)/shard_map/ppermute | solution.py:39
  186.5 1.9 collective-permute-done.34
  189.8 1.9 collective-permute-done.29
  (104 shorter events, 28.4 us)
Async XLA Ops:
  7.2 121.6 %copy-start = (bf16[256,256]{1,0:T(8,128)(2,1)S(1)}, bf16[256,256]{1,0:T(8,128)(2,1)}, u32[]{:S(2)}) copy-start(bf16[256,256]{1,0:T(8,128)(2,1)} %param.14) | copy-start | bytes 393220
  7.2 42.9 %all-gather.2.cloned.1.call-start = ((), (), s32[]{:S(2)}) async-start(), calls=%async_computation | async-start | bytes 4456448 | tf_op jit(solution)/shard_map/all_gather | solution.py:263
  7.9 7.7 %collective-permute-start = (bf16[512,128]{1,0:T(8,128)(2,1)}, bf16[512,128]{1,0:T(8,128)(2,1)S(1)}, u32[]{:S(2)}, u32[]{:S(2)}) collective-permute-start(bf16[512,128]{1,0:T(8,128)(2,1)} %param.10), channel_id=1, source_target_pairs={{0,16},{16,0},{32,48},{48,32},{64,80},{80,64},{96,112},{112,96},{1... | collective-permute-start | bytes 393224 | tf_op jit(solution)/shard_map/ppermute | solution.py:35
  15.7 9.4 %collective-permute-start.1 = (bf16[1024,128]{1,0:T(8,128)(2,1)S(1)}, bf16[1024,128]{1,0:T(8,128)(2,1)S(1)}, u32[]{:S(2)}, u32[]{:S(2)}) collective-permute-start(bf16[1024,128]{1,0:T(8,128)(2,1)S(1)} %constant_dynamic-update-slice_fusion), channel_id=1, source_target_pairs={{0,32},{16,48},{32,64},{48,80},{64,96},{80,112},{96,0},{112,16},{1... | collective-permute-start | bytes 786440 | tf_op jit(solution)/shard_map/ppermute | solution.py:35
  17.3 12.2 %collective-permute-start.2 = (bf16[1024,128]{1,0:T(8,128)(2,1)S(1)}, bf16[1024,128]{1,0:T(8,128)(2,1)S(1)}, u32[]{:S(2)}, u32[]{:S(2)}) collective-permute-start(bf16[1024,128]{1,0:T(8,128)(2,1)S(1)} %constant_dynamic-update-slice_fusion), channel_id=1, source_target_pairs={{0,96},{16,112},{32,0},{48,16},{64,32},{80,48},{96,64},{112,80},{1... | collective-permute-start | bytes 786440 | tf_op jit(solution)/shard_map/ppermute | solution.py:35
  19.0 12.3 %collective-permute-start.3 = (bf16[1024,128]{1,0:T(8,128)(2,1)S(1)}, bf16[1024,128]{1,0:T(8,128)(2,1)S(1)}, u32[]{:S(2)}, u32[]{:S(2)}) collective-permute-start(bf16[1024,128]{1,0:T(8,128)(2,1)S(1)} %constant_dynamic-update-slice_fusion), channel_id=1, source_target_pairs={{0,64},{16,80},{32,96},{48,112},{64,0},{80,16},{96,32},{112,48},{1... | collective-permute-start | bytes 786440 | tf_op jit(solution)/shard_map/ppermute | solution.py:35
  38.6 2.7 %collective-permute-start.4 = (bf16[32,128,128]{2,1,0:T(8,128)(2,1)S(1)}, bf16[32,128,128]{2,1,0:T(8,128)(2,1)S(1)}, u32[]{:S(2)}, u32[]{:S(2)}) collective-permute-start(bf16[32,128,128]{2,1,0:T(8,128)(2,1)S(1)} %get-tuple-element.38), channel_id=1, source_target_pairs={{0,1},{1,0},{2,3},{3,2},{4,5},{5,4},{6,7},{7,6},{8,9},{9,8},{10,11... | collective-permute-start | bytes 3145736 | tf_op jit(solution)/shard_map/ppermute | solution.py:39
  41.4 11.7 %copy-start.2 = (s32[1,1,448]{2,1,0:T(1,128)S(1)}, s32[1,1,448]{2,1,0:T(1,128)}, u32[]{:S(2)}) copy-start(s32[1,1,448]{2,1,0:T(1,128)} %param.16) | copy-start | bytes 5380
  42.6 23.1 %collective-permute-start.5 = (bf16[1024,128]{1,0:T(8,128)(2,1)}, bf16[1024,128]{1,0:T(8,128)(2,1)}, u32[]{:S(2)}, u32[]{:S(2)}) collective-permute-start(bf16[1024,128]{1,0:T(8,128)(2,1)} %bitcast.10), channel_id=1, source_target_pairs={{0,2},{1,3},{2,4},{3,5},{4,6},{5,7},{6,0},{7,1},{8,10},{9,11},{10,... | collective-permute-start | bytes 786440 | tf_op jit(solution)/shard_map/ppermute | solution.py:39
  45.1 20.6 %collective-permute-start.6 = (bf16[1024,128]{1,0:T(8,128)(2,1)}, bf16[1024,128]{1,0:T(8,128)(2,1)}, u32[]{:S(2)}, u32[]{:S(2)}) collective-permute-start(bf16[1024,128]{1,0:T(8,128)(2,1)} %bitcast.11), channel_id=1, source_target_pairs={{0,6},{1,7},{2,0},{3,1},{4,2},{5,3},{6,4},{7,5},{8,14},{9,15},{10,... | collective-permute-start | bytes 786440 | tf_op jit(solution)/shard_map/ppermute | solution.py:39
  50.1 15.7 %collective-permute-start.7 = (bf16[1024,128]{1,0:T(8,128)(2,1)}, bf16[1024,128]{1,0:T(8,128)(2,1)S(1)}, u32[]{:S(2)}, u32[]{:S(2)}) collective-permute-start(bf16[1024,128]{1,0:T(8,128)(2,1)} %bitcast.12), channel_id=1, source_target_pairs={{0,4},{1,5},{2,6},{3,7},{4,0},{5,1},{6,2},{7,3},{8,12},{9,13},{10,... | collective-permute-start | bytes 786440 | tf_op jit(solution)/shard_map/ppermute | solution.py:39
  53.0 2.2 %copy-start.3 = (bf16[8192,256]{1,0:T(8,128)(2,1)S(1)}, bf16[8192,256]{1,0:T(8,128)(2,1)}, u32[]{:S(2)}) copy-start(bf16[8192,256]{1,0:T(8,128)(2,1)} %all-gather.2.cloned.1.call-done) | copy-start | bytes 12582916
  55.2 10.5 %copy-start.4 = (f32[8,128,128]{2,1,0:T(8,128)S(1)}, f32[8,128,128]{2,1,0:T(8,128)}, u32[]{:S(2)}) copy-start(f32[8,128,128]{2,1,0:T(8,128)} %get-tuple-element.78) | copy-start | bytes 1572868
  65.7 2.7 %copy-start.7 = (bf16[512,128]{1,0:T(8,128)(2,1)S(1)}, bf16[512,128]{1,0:T(8,128)(2,1)}, u32[]{:S(2)}) copy-start(bf16[512,128]{1,0:T(8,128)(2,1)} %param.10) | copy-start | bytes 393220
  65.7 2.7 %copy-start.13 = (bf16[128,256]{1,0:T(8,128)(2,1)S(1)}, bf16[128,256]{1,0:T(8,128)(2,1)}, u32[]{:S(2)}) copy-start(bf16[128,256]{1,0:T(8,128)(2,1)} %param.12) | copy-start | bytes 196612
  65.7 6.4 %copy-start.14 = (bf16[128,256]{1,0:T(8,128)(2,1)S(1)}, bf16[128,256]{1,0:T(8,128)(2,1)}, u32[]{:S(2)}) copy-start(bf16[128,256]{1,0:T(8,128)(2,1)} %param.13) | copy-start | bytes 196612
  67.0 13.8 %copy-start.5 = (f32[1024,128]{1,0:T(8,128)}, f32[1024,128]{1,0:T(8,128)S(1)}, u32[]{:S(2)}) copy-start(f32[1024,128]{1,0:T(8,128)S(1)} %fusion.8) | copy-start | bytes 1572868
  67.0 5.0 %collective-permute-start.8 = (bf16[512,128]{1,0:T(8,128)(2,1)S(1)}, bf16[512,128]{1,0:T(8,128)(2,1)S(1)}, u32[]{:S(2)}, u32[]{:S(2)}) collective-permute-start(bf16[512,128]{1,0:T(8,128)(2,1)S(1)} %slice.168), channel_id=1, source_target_pairs={{0,8},{1,9},{2,10},{3,11},{4,12},{5,13},{6,14},{7,15},{8,0},{9,1},... | collective-permute-start | bytes 393224 | tf_op jit(solution)/shard_map/ppermute | solution.py:39
  72.0 8.7 %copy-start.11 = (bf16[512,128]{1,0:T(8,128)(2,1)}, bf16[512,128]{1,0:T(8,128)(2,1)S(1)}, u32[]{:S(2)}) copy-start(bf16[512,128]{1,0:T(8,128)(2,1)S(1)} %collective-permute-done.8) | copy-start | bytes 393220
  73.3 11.1 %collective-permute-start.9 = (bf16[512,256]{1,0:T(8,128)(2,1)S(1)}, bf16[512,256]{1,0:T(8,128)(2,1)S(1)}, u32[]{:S(2)}, u32[]{:S(2)}) collective-permute-start(bf16[512,256]{1,0:T(8,128)(2,1)S(1)} %get-tuple-element.91), channel_id=1, source_target_pairs={{0,16},{16,0},{32,48},{48,32},{64,80},{80,64},{96,112},{112,96},{1... | collective-permute-start | bytes 786440 | tf_op jit(solution)/shard_map/ppermute | solution.py:35
  77.2 18.5 %collective-permute-start.13 = (bf16[8,128,256]{2,1,0:T(8,128)(2,1)}, bf16[8,128,256]{2,1,0:T(8,128)(2,1)}, u32[]{:S(2)}, u32[]{:S(2)}) collective-permute-start(bf16[8,128,256]{2,1,0:T(8,128)(2,1)} %get-tuple-element.46), channel_id=1, source_target_pairs={{0,16},{16,0},{32,48},{48,32},{64,80},{80,64},{96,112},{112,96},{1... | collective-permute-start | bytes 1572872 | tf_op jit(solution)/shard_map/ppermute | solution.py:35
  77.3 28.6 %collective-permute-start.14 = (bf16[8,128,256]{2,1,0:T(8,128)(2,1)S(1)}, bf16[8,128,256]{2,1,0:T(8,128)(2,1)}, u32[]{:S(2)}, u32[]{:S(2)}) collective-permute-start(bf16[8,128,256]{2,1,0:T(8,128)(2,1)S(1)} %get-tuple-element.47), channel_id=1, source_target_pairs={{0,16},{16,0},{32,48},{48,32},{64,80},{80,64},{96,112},{112,96},{1... | collective-permute-start | bytes 1572872 | tf_op jit(solution)/shard_map/ppermute | solution.py:35
  84.4 21.4 %collective-permute-start.10 = (bf16[1024,256]{1,0:T(8,128)(2,1)S(1)}, bf16[1024,256]{1,0:T(8,128)(2,1)}, u32[]{:S(2)}, u32[]{:S(2)}) collective-permute-start(bf16[1024,256]{1,0:T(8,128)(2,1)S(1)} %pad_maximum_fusion.1), channel_id=1, source_target_pairs={{0,32},{16,48},{32,64},{48,80},{64,96},{80,112},{96,0},{112,16},{1... | collective-permute-start | bytes 1572872 | tf_op jit(solution)/shard_map/ppermute | solution.py:35
  88.4 21.7 %collective-permute-start.11 = (bf16[1024,256]{1,0:T(8,128)(2,1)S(1)}, bf16[1024,256]{1,0:T(8,128)(2,1)}, u32[]{:S(2)}, u32[]{:S(2)}) collective-permute-start(bf16[1024,256]{1,0:T(8,128)(2,1)S(1)} %pad_maximum_fusion.1), channel_id=1, source_target_pairs={{0,96},{16,112},{32,0},{48,16},{64,32},{80,48},{96,64},{112,80},{1... | collective-permute-start | bytes 1572872 | tf_op jit(solution)/shard_map/ppermute | solution.py:35
  89.0 23.1 %collective-permute-start.12 = (bf16[1024,256]{1,0:T(8,128)(2,1)S(1)}, bf16[1024,256]{1,0:T(8,128)(2,1)}, u32[]{:S(2)}, u32[]{:S(2)}) collective-permute-start(bf16[1024,256]{1,0:T(8,128)(2,1)S(1)} %pad_maximum_fusion.1), channel_id=1, source_target_pairs={{0,64},{16,80},{32,96},{48,112},{64,0},{80,16},{96,32},{112,48},{1... | collective-permute-start | bytes 1572872 | tf_op jit(solution)/shard_map/ppermute | solution.py:35
  113.8 14.1 %collective-permute-start.15 = (bf16[512,256]{1,0:T(8,128)(2,1)S(1)}, bf16[512,256]{1,0:T(8,128)(2,1)S(1)}, u32[]{:S(2)}, u32[]{:S(2)}) collective-permute-start(bf16[512,256]{1,0:T(8,128)(2,1)S(1)} %get-tuple-element.79), channel_id=1, source_target_pairs={{0,32},{16,48},{32,64},{48,80},{64,96},{80,112},{96,0},{112,16},{1... | collective-permute-start | bytes 786440 | tf_op jit(solution)/shard_map/ppermute | solution.py:35
  115.0 12.9 %collective-permute-start.16 = (bf16[512,256]{1,0:T(8,128)(2,1)S(1)}, bf16[512,256]{1,0:T(8,128)(2,1)S(1)}, u32[]{:S(2)}, u32[]{:S(2)}) collective-permute-start(bf16[512,256]{1,0:T(8,128)(2,1)S(1)} %get-tuple-element.81), channel_id=1, source_target_pairs={{0,96},{16,112},{32,0},{48,16},{64,32},{80,48},{96,64},{112,80},{1... | collective-permute-start | bytes 786440 | tf_op jit(solution)/shard_map/ppermute | solution.py:35
  117.1 10.9 %collective-permute-start.17 = (bf16[512,256]{1,0:T(8,128)(2,1)S(1)}, bf16[512,256]{1,0:T(8,128)(2,1)S(1)}, u32[]{:S(2)}, u32[]{:S(2)}) collective-permute-start(bf16[512,256]{1,0:T(8,128)(2,1)S(1)} %get-tuple-element.80), channel_id=1, source_target_pairs={{0,64},{16,80},{32,96},{48,112},{64,0},{80,16},{96,32},{112,48},{1... | collective-permute-start | bytes 786440 | tf_op jit(solution)/shard_map/ppermute | solution.py:35
  117.2 11.2 %copy-start.10 = (bf16[256,256]{1,0:T(8,128)(2,1)S(1)}, bf16[256,256]{1,0:T(8,128)(2,1)}, u32[]{:S(2)}) copy-start(bf16[256,256]{1,0:T(8,128)(2,1)} %param.15) | copy-start | bytes 393220
  128.1 11.3 %collective-permute-start.18 = (bf16[32,128,256]{2,1,0:T(8,128)(2,1)S(1)}, bf16[32,128,256]{2,1,0:T(8,128)(2,1)}, u32[]{:S(2)}, u32[]{:S(2)}) collective-permute-start(bf16[32,128,256]{2,1,0:T(8,128)(2,1)S(1)} %get-tuple-element.63), channel_id=1, source_target_pairs={{0,1},{1,0},{2,3},{3,2},{4,5},{5,4},{6,7},{7,6},{8,9},{9,8},{10,11... | collective-permute-start | bytes 6291464 | tf_op jit(solution)/shard_map/ppermute | solution.py:39
  132.1 2.1 %collective-permute-start.22 = (f32[384,256]{1,0:T(8,128)}, f32[384,256]{1,0:T(8,128)}, u32[]{:S(2)}, u32[]{:S(2)}) collective-permute-start(f32[384,256]{1,0:T(8,128)} %dynamic-slice_bitcast_fusion), channel_id=1, source_target_pairs={{0,1},{1,0},{2,3},{3,2},{4,5},{5,4},{6,7},{7,6},{8,9},{9,8},{10,11... | collective-permute-start | bytes 1179656 | tf_op jit(solution)/shard_map/ppermute | solution.py:39
  135.3 10.8 %collective-permute-start.23 = (f32[96,256]{1,0:T(8,128)S(1)}, f32[96,256]{1,0:T(8,128)S(1)}, u32[]{:S(2)}, u32[]{:S(2)}) collective-permute-start(f32[96,256]{1,0:T(8,128)S(1)} %get-tuple-element.88), channel_id=1, source_target_pairs={{0,2},{1,3},{2,4},{3,5},{4,6},{5,7},{6,0},{7,1},{8,10},{9,11},{10,... | collective-permute-start | bytes 294920 | tf_op jit(solution)/shard_map/ppermute | solution.py:39
  135.4 12.3 %collective-permute-start.24 = (f32[96,256]{1,0:T(8,128)S(1)}, f32[96,256]{1,0:T(8,128)S(1)}, u32[]{:S(2)}, u32[]{:S(2)}) collective-permute-start(f32[96,256]{1,0:T(8,128)S(1)} %get-tuple-element.90), channel_id=1, source_target_pairs={{0,6},{1,7},{2,0},{3,1},{4,2},{5,3},{6,4},{7,5},{8,14},{9,15},{10,... | collective-permute-start | bytes 294920 | tf_op jit(solution)/shard_map/ppermute | solution.py:39
  138.6 9.1 %collective-permute-start.25 = (f32[96,256]{1,0:T(8,128)S(1)}, f32[96,256]{1,0:T(8,128)S(1)}, u32[]{:S(2)}, u32[]{:S(2)}) collective-permute-start(f32[96,256]{1,0:T(8,128)S(1)} %get-tuple-element.89), channel_id=1, source_target_pairs={{0,4},{1,5},{2,6},{3,7},{4,0},{5,1},{6,2},{7,3},{8,12},{9,13},{10,... | collective-permute-start | bytes 294920 | tf_op jit(solution)/shard_map/ppermute | solution.py:39
  142.8 25.9 %collective-permute-start.19 = (bf16[1024,256]{1,0:T(8,128)(2,1)S(1)}, bf16[1024,256]{1,0:T(8,128)(2,1)S(1)}, u32[]{:S(2)}, u32[]{:S(2)}) collective-permute-start(bf16[1024,256]{1,0:T(8,128)(2,1)S(1)} %bitcast.113), channel_id=1, source_target_pairs={{0,2},{1,3},{2,4},{3,5},{4,6},{5,7},{6,0},{7,1},{8,10},{9,11},{10,... | collective-permute-start | bytes 1572872 | tf_op jit(solution)/shard_map/ppermute | solution.py:39
  144.3 24.4 %collective-permute-start.20 = (bf16[1024,256]{1,0:T(8,128)(2,1)S(1)}, bf16[1024,256]{1,0:T(8,128)(2,1)S(1)}, u32[]{:S(2)}, u32[]{:S(2)}) collective-permute-start(bf16[1024,256]{1,0:T(8,128)(2,1)S(1)} %bitcast.112), channel_id=1, source_target_pairs={{0,6},{1,7},{2,0},{3,1},{4,2},{5,3},{6,4},{7,5},{8,14},{9,15},{10,... | collective-permute-start | bytes 1572872 | tf_op jit(solution)/shard_map/ppermute | solution.py:39
  146.1 22.6 %collective-permute-start.21 = (bf16[1024,256]{1,0:T(8,128)(2,1)S(1)}, bf16[1024,256]{1,0:T(8,128)(2,1)S(1)}, u32[]{:S(2)}, u32[]{:S(2)}) collective-permute-start(bf16[1024,256]{1,0:T(8,128)(2,1)S(1)} %bitcast.111), channel_id=1, source_target_pairs={{0,4},{1,5},{2,6},{3,7},{4,0},{5,1},{6,2},{7,3},{8,12},{9,13},{10,... | collective-permute-start | bytes 1572872 | tf_op jit(solution)/shard_map/ppermute | solution.py:39
  147.7 7.9 %collective-permute-start.26 = (f32[96,256]{1,0:T(8,128)S(1)}, f32[96,256]{1,0:T(8,128)S(1)}, u32[]{:S(2)}, u32[]{:S(2)}) collective-permute-start(f32[96,256]{1,0:T(8,128)S(1)} %fusion.14), channel_id=1, source_target_pairs={{0,64},{16,80},{32,96},{48,112},{64,0},{80,16},{96,32},{112,48},{1... | collective-permute-start | bytes 294920 | tf_op jit(solution)/shard_map/ppermute | solution.py:35
  152.4 5.8 %collective-permute-start.27 = (f32[96,256]{1,0:T(8,128)S(1)}, f32[96,256]{1,0:T(8,128)S(1)}, u32[]{:S(2)}, u32[]{:S(2)}) collective-permute-start(f32[96,256]{1,0:T(8,128)S(1)} %fusion.14), channel_id=1, source_target_pairs={{0,32},{16,48},{32,64},{48,80},{64,96},{80,112},{96,0},{112,16},{1... | collective-permute-start | bytes 294920 | tf_op jit(solution)/shard_map/ppermute | solution.py:35
  155.7 4.6 %collective-permute-start.28 = (f32[96,256]{1,0:T(8,128)S(1)}, f32[96,256]{1,0:T(8,128)S(1)}, u32[]{:S(2)}, u32[]{:S(2)}) collective-permute-start(f32[96,256]{1,0:T(8,128)S(1)} %fusion.14), channel_id=1, source_target_pairs={{0,96},{16,112},{32,0},{48,16},{64,32},{80,48},{96,64},{112,80},{1... | collective-permute-start | bytes 294920 | tf_op jit(solution)/shard_map/ppermute | solution.py:35
  168.7 6.4 %collective-permute-start.30 = (f32[96,256]{1,0:T(8,128)S(1)}, f32[96,256]{1,0:T(8,128)S(1)}, u32[]{:S(2)}, u32[]{:S(2)}) collective-permute-start(f32[96,256]{1,0:T(8,128)S(1)} %add_add_fusion.1), channel_id=1, source_target_pairs={{0,16},{16,0},{32,48},{48,32},{64,80},{80,64},{96,112},{112,96},{1... | collective-permute-start | bytes 294920 | tf_op jit(solution)/shard_map/ppermute | solution.py:35
  171.5 5.9 %collective-permute-start.31 = (f32[96,256]{1,0:T(8,128)S(1)}, f32[96,256]{1,0:T(8,128)}, u32[]{:S(2)}, u32[]{:S(2)}) collective-permute-start(f32[96,256]{1,0:T(8,128)S(1)} %add_add_fusion.1), channel_id=1, source_target_pairs={{0,8},{1,9},{2,10},{3,11},{4,12},{5,13},{6,14},{7,15},{8,0},{9,1},... | collective-permute-start | bytes 294920 | tf_op jit(solution)/shard_map/ppermute | solution.py:39
  173.7 5.9 %collective-permute-start.32 = (f32[96,256]{1,0:T(8,128)S(1)}, f32[96,256]{1,0:T(8,128)}, u32[]{:S(2)}, u32[]{:S(2)}) collective-permute-start(f32[96,256]{1,0:T(8,128)S(1)} %add_add_fusion.1), channel_id=1, source_target_pairs={{0,24},{1,25},{2,26},{3,27},{4,28},{5,29},{6,30},{7,31},{8,16},{9,... | collective-permute-start | bytes 294920 | tf_op jit(solution)/shard_map/ppermute | solution.py:31
  180.6 5.9 %collective-permute-start.33 = (f32[96,256]{1,0:T(8,128)S(1)}, f32[96,256]{1,0:T(8,128)S(1)}, u32[]{:S(2)}, u32[]{:S(2)}) collective-permute-start(f32[96,256]{1,0:T(8,128)S(1)} %add_add_fusion), channel_id=1, source_target_pairs={{0,2},{1,3},{2,4},{3,5},{4,6},{5,7},{6,0},{7,1},{8,10},{9,11},{10,... | collective-permute-start | bytes 294920 | tf_op jit(solution)/shard_map/ppermute | solution.py:39
  182.1 6.3 %collective-permute-start.34 = (f32[96,256]{1,0:T(8,128)S(1)}, f32[96,256]{1,0:T(8,128)S(1)}, u32[]{:S(2)}, u32[]{:S(2)}) collective-permute-start(f32[96,256]{1,0:T(8,128)S(1)} %add_add_fusion), channel_id=1, source_target_pairs={{0,4},{1,5},{2,6},{3,7},{4,0},{5,1},{6,2},{7,3},{8,12},{9,13},{10,... | collective-permute-start | bytes 294920 | tf_op jit(solution)/shard_map/ppermute | solution.py:39
  184.8 4.6 %collective-permute-start.35 = (f32[96,256]{1,0:T(8,128)S(1)}, f32[96,256]{1,0:T(8,128)S(1)}, u32[]{:S(2)}, u32[]{:S(2)}) collective-permute-start(f32[96,256]{1,0:T(8,128)S(1)} %add_add_fusion), channel_id=1, source_target_pairs={{0,6},{1,7},{2,0},{3,1},{4,2},{5,3},{6,4},{7,5},{8,14},{9,15},{10,... | collective-permute-start | bytes 294920 | tf_op jit(solution)/shard_map/ppermute | solution.py:39
  185.3 6.5 %collective-permute-start.29 = (bf16[512,256]{1,0:T(8,128)(2,1)S(1)}, bf16[512,256]{1,0:T(8,128)(2,1)S(1)}, u32[]{:S(2)}, u32[]{:S(2)}) collective-permute-start(bf16[512,256]{1,0:T(8,128)(2,1)S(1)} %slice.167), channel_id=1, source_target_pairs={{0,8},{1,9},{2,10},{3,11},{4,12},{5,13},{6,14},{7,15},{8,0},{9,1},... | collective-permute-start | bytes 786440 | tf_op jit(solution)/shard_map/ppermute | solution.py:39
  189.5 3.4 %collective-permute-start.36 = (f32[384,256]{1,0:T(8,128)S(1)}, f32[384,256]{1,0:T(8,128)S(1)}, u32[]{:S(2)}, u32[]{:S(2)}) collective-permute-start(f32[384,256]{1,0:T(8,128)S(1)} %pad_maximum_fusion.3), channel_id=1, source_target_pairs={{0,1},{1,0},{2,3},{3,2},{4,5},{5,4},{6,7},{7,6},{8,9},{9,8},{10,11... | collective-permute-start | bytes 1179656 | tf_op jit(solution)/shard_map/ppermute | solution.py:39
  (6 other events, 9.9 us)
Sparse Core Ops, SparseCore 0:
  9.7 40.2 all-gather.1
